TPU v7x, 32 devices: a whole 2x2x4 slice. The times are simulated.
32 devices in a mesh: dp: 8 (over z, x), fsdp: 4 (over y, core).
Axes of the slice: x: 2, y: 2, z: 4, core: 2. Of those that a mesh axis runs over, the one named last changes fastest.
Arguments:
- token_states: bfloat16 [32, 1024, 768], P(('dp', 'fsdp')), may hold values from -6 to 6
- char_codes: int32 [32, 1024, 4], P(('dp', 'fsdp')), may hold values from 0 to 999
- lengths: int32 [32], P(('dp', 'fsdp')), may hold values from 256 to 1024, as said below
- token_cotangent: bfloat16 [32, 1024, 768], P(('dp', 'fsdp')), may hold values from -6 to 6
- char_cotangent: bfloat16 [32, 1024, 768], P(('dp', 'fsdp')), may hold values from -6 to 6
- char_table: bfloat16 [1000, 256], P(None, ('dp', 'fsdp')), may hold values from -6 to 6
- recur_input: bfloat16 [256, 2304], P(None, ('dp', 'fsdp')), may hold values from -0.375 to 0.375
- recur_state: bfloat16 [384, 2304], P(None, ('dp', 'fsdp')), may hold values from -0.3125 to 0.3125
- project_weight: bfloat16 [768, 2304], P(('dp', 'fsdp')), may hold values from -0.21875 to 0.21875
- output_weight: bfloat16 [768, 768], P(('dp', 'fsdp')), may hold values from -0.625 to 0.625
- merging_weight: bfloat16 [3, 1536, 768], P(None, ('dp', 'fsdp')), may hold values from -0.09375 to 0.09375
- up_weight: bfloat16 [768, 3072], P(('dp', 'fsdp')), may hold values from -0.21875 to 0.21875
- down_weight: bfloat16 [3072, 768], P(('dp', 'fsdp')), may hold values from -0.109375 to 0.109375
- char_weight: bfloat16 [768, 768], P(('dp', 'fsdp')), may hold values from -0.21875 to 0.21875
- attend_gain: bfloat16 [768], P(('dp', 'fsdp')), may hold values from 0.25 to 1.75
- attend_shift: bfloat16 [768], P(('dp', 'fsdp')), may hold values from -1.75 to 1.75
- feed_gain: bfloat16 [768], P(('dp', 'fsdp')), may hold values from 0.25 to 1.75
- feed_shift: bfloat16 [768], P(('dp', 'fsdp')), may hold values from -1.75 to 1.75
- char_gain: bfloat16 [768], P(('dp', 'fsdp')), may hold values from 0.25 to 1.75
- char_shift: bfloat16 [768], P(('dp', 'fsdp')), may hold values from -1.75 to 1.75
Outputs:
- token_stream: bfloat16 [32, 1024, 768], P(('dp', 'fsdp'))
- char_stream: bfloat16 [32, 1024, 768], P(('dp', 'fsdp'))
- input_gradient: bfloat16 [32, 1024, 768], P(('dp', 'fsdp'))
- table_gradient: float32 [1000, 256], P(None, ('dp', 'fsdp'))
- inlet_gradient: float32 [256, 2304], P(None, ('dp', 'fsdp'))
- recur_gradient: float32 [384, 2304], P(None, ('dp', 'fsdp'))
- project_gradient: float32 [768, 2304], P(('dp', 'fsdp'))
- output_gradient: float32 [768, 768], P(('dp', 'fsdp'))
- merging_gradient: float32 [3, 1536, 768], P(None, ('dp', 'fsdp'))
- up_gradient: float32 [768, 3072], P(('dp', 'fsdp'))
- down_gradient: float32 [3072, 768], P(('dp', 'fsdp'))
- branch_gradient: float32 [768, 768], P(('dp', 'fsdp'))
- attend_gain_gradient: float32 [768], P(('dp', 'fsdp'))
- attend_shift_gradient: float32 [768], P(('dp', 'fsdp'))
- feed_gain_gradient: float32 [768], P(('dp', 'fsdp'))
- feed_shift_gradient: float32 [768], P(('dp', 'fsdp'))
- char_gain_gradient: float32 [768], P(('dp', 'fsdp'))
- char_shift_gradient: float32 [768], P(('dp', 'fsdp'))
Inputs may be any that keep to these rules, and one draw needn't show every extreme that they name: `lengths`: the valid tokens of a sequence are its first ones; at least one sequence is full.
All inputs are finite; a program needn't handle non-finite values.
Results may differ from a plain program's by a relative error of at most 0.015.
Values may be sent and summed in bfloat16 or wider, within the bound.
No kernel may reach another device: no remote copies, remote signals or barrier semaphores. Data moves between devices by JAX's collectives and lax.ppermute only.
A program may use at most 384 MiB of HBM per device.

v0:
```python
import math

import jax
import jax.numpy as jnp
from jax import lax
from jax.sharding import PartitionSpec as P

HEAD_DIM = 64
CHARS = 4


EPS = 1e-05
MASKED = -1e30


def norm_apply(values, gain, shift):
    average = jnp.mean(values, axis=-1, keepdims=True)
    centred = values - average
    variance = jnp.mean(centred * centred, axis=-1, keepdims=True)
    return centred * lax.rsqrt(variance + EPS) * gain + shift


def exact_gelu(values):
    return jax.nn.gelu(values, approximate=False)


def product(left, right):
    return jnp.dot(left, right, preferred_element_type=jnp.float32)


def outer_sum(left, right):
    return jnp.einsum("sli,slo->io", left, right, preferred_element_type=jnp.float32)


def back_product(grad_rows, weight):
    return jnp.einsum("slo,io->sli", grad_rows, weight, preferred_element_type=jnp.float32)


def shift_down(values):
    return jnp.pad(values[:, :-1], ((0, 0), (1, 0), (0, 0)))


def shift_up(values):
    return jnp.pad(values[:, 1:], ((0, 0), (0, 1), (0, 0)))


def cell_forward(inputs, previous, weight, width):
    if previous is None:
        recur = jnp.zeros_like(inputs)
        before = jnp.zeros(inputs.shape[:-1] + (width,), jnp.float32)
    else:
        recur = product(previous, weight)
        before = previous.astype(jnp.float32)
    reset = jax.nn.sigmoid(inputs[..., :width] + recur[..., :width])
    update = jax.nn.sigmoid(inputs[..., width : 2 * width] + recur[..., width : 2 * width])
    fresh = jnp.tanh(inputs[..., 2 * width :] + reset * recur[..., 2 * width :])
    state = ((1.0 - update) * fresh + update * before).astype(jnp.bfloat16)
    return (state, (reset, update, fresh, recur[..., 2 * width :], before, previous))


def cell_backward(grad_state, kept, weight):
    reset, update, fresh, recur_new, before, previous = kept
    fresh_pre = grad_state * (1.0 - update) * (1.0 - fresh * fresh)
    update_pre = grad_state * (before - fresh) * update * (1.0 - update)
    reset_pre = fresh_pre * recur_new * reset * (1.0 - reset)
    grad_inputs = jnp.concatenate([reset_pre, update_pre, fresh_pre], axis=-1)
    if previous is None:
        return (grad_inputs, None, None)
    grad_recur = jnp.concatenate([reset_pre, update_pre, fresh_pre * reset], axis=-1).astype(
        jnp.bfloat16
    )
    grad_weight = outer_sum(previous, grad_recur)
    grad_previous = grad_state * update + back_product(grad_recur, weight)
    return (grad_inputs, grad_weight, grad_previous)


def on_device(
    token_states,
    char_codes,
    lengths,
    token_cotangent,
    char_cotangent,
    char_table,
    recur_input,
    recur_state,
    project_weight,
    output_weight,
    merging_weight,
    up_weight,
    down_weight,
    char_weight,
    attend_gain,
    attend_shift,
    feed_gain,
    feed_shift,
    char_gain,
    char_shift,
):
    gathered = (
        lax.all_gather(char_table, ("dp", "fsdp"), axis=1, tiled=True),
        lax.all_gather(recur_input, ("dp", "fsdp"), axis=1, tiled=True),
        lax.all_gather(recur_state, ("dp", "fsdp"), axis=1, tiled=True),
        lax.all_gather(project_weight, ("dp", "fsdp"), axis=0, tiled=True),
        lax.all_gather(output_weight, ("dp", "fsdp"), axis=0, tiled=True),
        lax.all_gather(merging_weight, ("dp", "fsdp"), axis=1, tiled=True),
        lax.all_gather(up_weight, ("dp", "fsdp"), axis=0, tiled=True),
        lax.all_gather(down_weight, ("dp", "fsdp"), axis=0, tiled=True),
        lax.all_gather(char_weight, ("dp", "fsdp"), axis=0, tiled=True),
        lax.all_gather(attend_gain, ("dp", "fsdp"), axis=0, tiled=True),
        lax.all_gather(attend_shift, ("dp", "fsdp"), axis=0, tiled=True),
        lax.all_gather(feed_gain, ("dp", "fsdp"), axis=0, tiled=True),
        lax.all_gather(feed_shift, ("dp", "fsdp"), axis=0, tiled=True),
        lax.all_gather(char_gain, ("dp", "fsdp"), axis=0, tiled=True),
        lax.all_gather(char_shift, ("dp", "fsdp"), axis=0, tiled=True),
    )
    (
        table_full,
        inlet_full,
        recur_full,
        project_full,
        output_full,
        merging_full,
        upper_full,
        lower_full,
        branch_full,
        gain_attend,
        shift_attend,
        gain_feed,
        shift_feed,
        gain_char,
        shift_char,
    ) = gathered
    count, length, width = token_states.shape
    half = width // 2
    triple = 3 * half
    heads = width // HEAD_DIM
    scale = 1.0 / math.sqrt(HEAD_DIM)
    positions = lax.broadcasted_iota(jnp.int32, (count, length), 1)
    valid = positions < lengths[:, None]
    key_valid = valid[:, None, :]
    letters = lax.broadcasted_iota(jnp.int32, (1, 1, table_full.shape[0]), 2)
    picks = []
    embeds = []
    gates = []
    for slot in range(CHARS):
        picked = (char_codes[:, :, slot][:, :, None] == letters).astype(jnp.bfloat16)
        embed = product(picked, table_full).astype(jnp.bfloat16)
        picks.append(picked)
        embeds.append(embed)
        gates.append(product(embed, inlet_full))
    forward_kept = [None] * CHARS
    state = None
    for slot in range(CHARS):
        state, forward_kept[slot] = cell_forward(
            gates[slot][..., :triple], state, recur_full[:, :triple], half
        )
    forward_last = state
    backward_kept = [None] * CHARS
    state = None
    for slot in range(CHARS - 1, -1, -1):
        state, backward_kept[slot] = cell_forward(
            gates[slot][..., triple:], state, recur_full[:, triple:], half
        )
    chars_rep = jnp.concatenate([forward_last, state], axis=-1)
    mixed = product(token_states, project_full).astype(jnp.bfloat16)

    def head_parts(head):
        start = head * HEAD_DIM
        return (
            lax.dynamic_slice_in_dim(mixed, start, HEAD_DIM, 2),
            lax.dynamic_slice_in_dim(mixed, width + start, HEAD_DIM, 2),
            lax.dynamic_slice_in_dim(mixed, 2 * width + start, HEAD_DIM, 2),
        )

    def head_scores(queries, keys_part):
        scores = (
            jnp.einsum("sqd,skd->sqk", queries, keys_part, preferred_element_type=jnp.float32)
            * scale
        )
        return jnp.where(key_valid, scores, MASKED)

    def attend_head(head):
        queries, keys_part, values_part = head_parts(head)
        scores = head_scores(queries, keys_part)
        peak = jnp.max(scores, axis=-1, keepdims=True)
        raised = jnp.exp(scores - peak)
        total = jnp.sum(raised, axis=-1, keepdims=True)
        probs = (raised / total).astype(jnp.bfloat16)
        context = jnp.einsum("sqk,skd->sqd", probs, values_part, preferred_element_type=jnp.float32)
        return (context, peak[..., 0] + jnp.log(total[..., 0]))

    contexts, log_totals = lax.map(attend_head, jnp.arange(heads))
    context_low = (
        jnp.transpose(contexts, (1, 2, 0, 3)).reshape(count, length, width).astype(jnp.bfloat16)
    )
    first_pre = token_states.astype(jnp.float32) + product(context_low, output_full)
    first, pull_first = jax.vjp(
        norm_apply, first_pre, gain_attend.astype(jnp.float32), shift_attend.astype(jnp.float32)
    )
    joined = jnp.where(
        valid[..., None],
        jnp.concatenate([first.astype(jnp.bfloat16), chars_rep], axis=-1),
        jnp.zeros((), jnp.bfloat16),
    )
    merging_pre = (
        shift_down(product(joined, merging_full[0]))
        + product(joined, merging_full[1])
        + shift_up(product(joined, merging_full[2]))
    )
    merged, pull_merged = jax.vjp(exact_gelu, merging_pre)
    summed = first + merged
    summed_low = summed.astype(jnp.bfloat16)
    hidden, pull_hidden = jax.vjp(exact_gelu, product(summed_low, upper_full))
    hidden_low = hidden.astype(jnp.bfloat16)
    token_stream, pull_token = jax.vjp(
        norm_apply,
        summed + product(hidden_low, lower_full),
        gain_feed.astype(jnp.float32),
        shift_feed.astype(jnp.float32),
    )
    merged_low = merged.astype(jnp.bfloat16)
    char_stream, pull_char = jax.vjp(
        norm_apply,
        chars_rep.astype(jnp.float32) + product(merged_low, branch_full),
        gain_char.astype(jnp.float32),
        shift_char.astype(jnp.float32),
    )
    (
        inlet_back,
        recur_back,
        project_back,
        output_back,
        merging_back,
        upper_back,
        lower_back,
        branch_back,
    ) = (
        lax.all_gather(recur_input, ("dp", "fsdp"), axis=1, tiled=True),
        lax.all_gather(recur_state, ("dp", "fsdp"), axis=1, tiled=True),
        lax.all_gather(project_weight, ("dp", "fsdp"), axis=0, tiled=True),
        lax.all_gather(output_weight, ("dp", "fsdp"), axis=0, tiled=True),
        lax.all_gather(merging_weight, ("dp", "fsdp"), axis=1, tiled=True),
        lax.all_gather(up_weight, ("dp", "fsdp"), axis=0, tiled=True),
        lax.all_gather(down_weight, ("dp", "fsdp"), axis=0, tiled=True),
        lax.all_gather(char_weight, ("dp", "fsdp"), axis=0, tiled=True),
    )
    token_pre_grad, feed_gain_grad, feed_shift_grad = pull_token(
        token_cotangent.astype(jnp.float32)
    )
    feed_grad = token_pre_grad.astype(jnp.bfloat16)
    down_grad = outer_sum(hidden_low, feed_grad)
    hidden_grad = pull_hidden(back_product(feed_grad, lower_back))[0].astype(jnp.bfloat16)
    up_grad = outer_sum(summed_low, hidden_grad)
    summed_grad = token_pre_grad + back_product(hidden_grad, upper_back)
    char_pre_grad, char_gain_grad, char_shift_grad = pull_char(char_cotangent.astype(jnp.float32))
    branch_grad = char_pre_grad.astype(jnp.bfloat16)
    branch_weight_grad = outer_sum(merged_low, branch_grad)
    merging_grad = pull_merged(summed_grad + back_product(branch_grad, branch_back))[0].astype(
        jnp.bfloat16
    )
    merging_weight_grad = jnp.stack(
        [
            outer_sum(shift_down(joined), merging_grad),
            outer_sum(joined, merging_grad),
            outer_sum(shift_up(joined), merging_grad),
        ]
    )
    joined_grad = (
        shift_up(back_product(merging_grad, merging_back[0]))
        + back_product(merging_grad, merging_back[1])
        + shift_down(back_product(merging_grad, merging_back[2]))
    )
    joined_grad = jnp.where(valid[..., None], joined_grad, 0.0)
    first_grad = summed_grad + joined_grad[..., :width]
    rep_grad = char_pre_grad + joined_grad[..., width:]
    first_pre_grad, attend_gain_grad, attend_shift_grad = pull_first(first_grad)
    attended_grad = first_pre_grad.astype(jnp.bfloat16)
    output_weight_grad = outer_sum(context_low, attended_grad)
    context_grad = back_product(attended_grad, output_back).astype(jnp.bfloat16)

    def attend_back(pair):
        head, log_total = pair
        queries, keys_part, values_part = head_parts(head)
        head_grad = lax.dynamic_slice_in_dim(context_grad, head * HEAD_DIM, HEAD_DIM, 2)
        probs = jnp.exp(head_scores(queries, keys_part) - log_total[..., None])
        prob_grad = jnp.einsum(
            "sqd,skd->sqk", head_grad, values_part, preferred_element_type=jnp.float32
        )
        delta = jnp.sum(probs * prob_grad, axis=-1, keepdims=True)
        score_grad = (probs * (prob_grad - delta)).astype(jnp.bfloat16)
        query_grad = (
            jnp.einsum("sqk,skd->sqd", score_grad, keys_part, preferred_element_type=jnp.float32)
            * scale
        )
        key_grad = (
            jnp.einsum("sqk,sqd->skd", score_grad, queries, preferred_element_type=jnp.float32)
            * scale
        )
        value_grad = jnp.einsum(
            "sqk,sqd->skd",
            probs.astype(jnp.bfloat16),
            head_grad,
            preferred_element_type=jnp.float32,
        )
        return (query_grad, key_grad, value_grad)

    head_grads = lax.map(attend_back, (jnp.arange(heads), log_totals))
    mixed_grad = jnp.concatenate(
        [jnp.transpose(part, (1, 2, 0, 3)).reshape(count, length, width) for part in head_grads],
        axis=-1,
    ).astype(jnp.bfloat16)
    project_grad = outer_sum(token_states, mixed_grad)
    input_gradient = (first_pre_grad + back_product(mixed_grad, project_back)).astype(jnp.bfloat16)
    forward_inputs = [None] * CHARS
    grad_state = rep_grad[..., :half]
    forward_weight_grad = jnp.zeros((half, triple), jnp.float32)
    for slot in range(CHARS - 1, -1, -1):
        grad_in, grad_weight, grad_state = cell_backward(
            grad_state, forward_kept[slot], recur_back[:, :triple]
        )
        forward_inputs[slot] = grad_in
        if grad_weight is not None:
            forward_weight_grad = forward_weight_grad + grad_weight
    backward_inputs = [None] * CHARS
    grad_state = rep_grad[..., half:]
    backward_weight_grad = jnp.zeros((half, triple), jnp.float32)
    for slot in range(CHARS):
        grad_in, grad_weight, grad_state = cell_backward(
            grad_state, backward_kept[slot], recur_back[:, triple:]
        )
        backward_inputs[slot] = grad_in
        if grad_weight is not None:
            backward_weight_grad = backward_weight_grad + grad_weight
    recur_weight_grad = jnp.concatenate([forward_weight_grad, backward_weight_grad], axis=1)
    inlet_grad = jnp.zeros(inlet_back.shape, jnp.float32)
    table_grad = jnp.zeros(table_full.shape, jnp.float32)
    for slot in range(CHARS):
        gate_grad = jnp.concatenate([forward_inputs[slot], backward_inputs[slot]], axis=-1).astype(
            jnp.bfloat16
        )
        inlet_grad = inlet_grad + outer_sum(embeds[slot], gate_grad)
        embed_grad = back_product(gate_grad, inlet_back).astype(jnp.bfloat16)
        table_grad = table_grad + outer_sum(picks[slot], embed_grad)
    owned = (
        lax.psum_scatter(table_grad, ("dp", "fsdp"), scatter_dimension=1, tiled=True),
        lax.psum_scatter(inlet_grad, ("dp", "fsdp"), scatter_dimension=1, tiled=True),
        lax.psum_scatter(recur_weight_grad, ("dp", "fsdp"), scatter_dimension=1, tiled=True),
        lax.psum_scatter(project_grad, ("dp", "fsdp"), scatter_dimension=0, tiled=True),
        lax.psum_scatter(output_weight_grad, ("dp", "fsdp"), scatter_dimension=0, tiled=True),
        lax.psum_scatter(merging_weight_grad, ("dp", "fsdp"), scatter_dimension=1, tiled=True),
        lax.psum_scatter(up_grad, ("dp", "fsdp"), scatter_dimension=0, tiled=True),
        lax.psum_scatter(down_grad, ("dp", "fsdp"), scatter_dimension=0, tiled=True),
        lax.psum_scatter(branch_weight_grad, ("dp", "fsdp"), scatter_dimension=0, tiled=True),
        lax.psum_scatter(attend_gain_grad, ("dp", "fsdp"), scatter_dimension=0, tiled=True),
        lax.psum_scatter(attend_shift_grad, ("dp", "fsdp"), scatter_dimension=0, tiled=True),
        lax.psum_scatter(feed_gain_grad, ("dp", "fsdp"), scatter_dimension=0, tiled=True),
        lax.psum_scatter(feed_shift_grad, ("dp", "fsdp"), scatter_dimension=0, tiled=True),
        lax.psum_scatter(char_gain_grad, ("dp", "fsdp"), scatter_dimension=0, tiled=True),
        lax.psum_scatter(char_shift_grad, ("dp", "fsdp"), scatter_dimension=0, tiled=True),
    )
    return (
        token_stream.astype(jnp.bfloat16),
        char_stream.astype(jnp.bfloat16),
        input_gradient,
        owned[0],
        owned[1],
        owned[2],
        owned[3],
        owned[4],
        owned[5],
        owned[6],
        owned[7],
        owned[8],
        owned[9],
        owned[10],
        owned[11],
        owned[12],
        owned[13],
        owned[14],
    )


def solution(mesh):
    placed = (
        P(("dp", "fsdp"), None, None),
        P(("dp", "fsdp"), None, None),
        P(("dp", "fsdp")),
        P(("dp", "fsdp"), None, None),
        P(("dp", "fsdp"), None, None),
        P(None, ("dp", "fsdp")),
        P(None, ("dp", "fsdp")),
        P(None, ("dp", "fsdp")),
        P(("dp", "fsdp"), None),
        P(("dp", "fsdp"), None),
        P(None, ("dp", "fsdp"), None),
        P(("dp", "fsdp"), None),
        P(("dp", "fsdp"), None),
        P(("dp", "fsdp"), None),
        P(("dp", "fsdp")),
        P(("dp", "fsdp")),
        P(("dp", "fsdp")),
        P(("dp", "fsdp")),
        P(("dp", "fsdp")),
        P(("dp", "fsdp")),
    )
    return jax.shard_map(
        on_device,
        mesh=mesh,
        in_specs=placed,
        out_specs=(
            P(("dp", "fsdp"), None, None),
            P(("dp", "fsdp"), None, None),
            P(("dp", "fsdp"), None, None),
            P(None, ("dp", "fsdp")),
            P(None, ("dp", "fsdp")),
            P(None, ("dp", "fsdp")),
            P(("dp", "fsdp"), None),
            P(("dp", "fsdp"), None),
            P(None, ("dp", "fsdp"), None),
            P(("dp", "fsdp"), None),
            P(("dp", "fsdp"), None),
            P(("dp", "fsdp"), None),
            P(("dp", "fsdp")),
            P(("dp", "fsdp")),
            P(("dp", "fsdp")),
            P(("dp", "fsdp")),
            P(("dp", "fsdp")),
            P(("dp", "fsdp")),
        ),
        check_vma=False,
    )
```

profile of v0, /device:TPU:0, one launch (start us, length us, event | category | flops | bytes accessed | tf_op | source)
XLA Modules:
  0.0 1836.0 jit_solution(11157678008083851323)
XLA Ops:
  13.6 45.2 %all_gather.57 = bf16[1000,256]{0,1:T(8,128)(2,1)S(1)} all-gather(bf16[1000,8]{0,1:T(8,128)(2,1)} %param.29), channel_id=1, replica_groups=mesh['dp'=8,'fsdp'=4] {'dp','fsdp'}, dimensions={1}, use_global_device_ids=true | all-gather | bytes 528000 | tf_op jit(solution)/shard_map/all_gather | solution.py:100
  64.0 37.2 %all-reduce.20 = (bf16[768]{0:T(1024)(128)(2,1)S(1)}, bf16[768]{0:T(1024)(128)(2,1)S(1)}, bf16[768]{0:T(1024)(128)(2,1)S(1)}, bf16[768]{0:T(1024)(128)(2,1)S(1)}...) all-reduce(bf16[768]{0:T(1024)(128)(2,1)S(1)} %dynamic-update-slice, ...), channel_id=1, replica_groups=mesh['dp'=8,'fsdp'=4] {'dp','fsdp'}, use_global_device_ids=true, to_apply=%add.7 | all-reduce | flops 4608 | bytes 18432
  170.3 17.1 all-gather.9.cloned.1.call-done
  195.1 130.0 %while.32 = (s32[]{:T(128)}, bf16[12,1,1024,64]{2,3,1,0:T(8,128)(2,1)S(1)}, f32[12,1,1024]{2,1,0:T(1,128)}, s32[12]{0:T(128)S(1)}, bf16[1,1024,2304]{2,1,0:T(8,1...) while((s32[]{:T(128)}, ...), condition=%wide.region_3.4_spmd.clone, body=%wide.region_0.3_spmd.clone.sunk | while | flops 281018368 | bytes 30455108 | solution.py:192
  342.7 12.0 fusion.242
  354.7 18.3 all-gather.23.cloned.1.call-done
  386.2 52.2 %all-gather.19.cloned.1.call-done = bf16[768,3072]{1,0:T(8,128)(2,1)} async-done(((bf16[24,3072]{1,0:T(8,128)(2,1)}), bf16[768,3072]{1,0:T(8,128)(2,1)}) %all-gather.19.cloned.1.call-update) | async-done | bytes 4718608 | tf_op jit(solution)/shard_map/all_gather | solution.py:106
  438.4 37.2 %multiply_convert_fusion.1 = (bf16[1024,3072]{1,0:T(8,128)(2,1)}, f32[1024,3072]{1,0:T(8,128)}, f32[1024,3072]{1,0:T(8,128)}) fusion(bf16[768,3072]{1,0:T(8,128)(2,1)} %all-gather.19.cloned.1.call-done, f32[1,1024,768]{1,2,0:T(8,128)} %fusion.95), kind=kOutput, calls=%fused_computation.67 | convolution fusion | flops 5037096960 | bytes 39321600 | tf_op jit(solution)/shard_map/dot_general | solution.py:28
  475.6 28.2 %all-gather.21.cloned.1.call-done = bf16[3072,768]{1,0:T(8,128)(2,1)} async-done(((bf16[96,768]{1,0:T(8,128)(2,1)}), bf16[3072,768]{1,0:T(8,128)(2,1)}) %all-gather.21.cloned.1.call-update) | async-done | bytes 4718608 | tf_op jit(solution)/shard_map/all_gather | solution.py:107
  503.8 9.2 fusion.362
  518.2 19.7 %add_convert_fusion = bf16[1024,3072]{1,0:T(8,128)(2,1)} fusion(f32[1024,3072]{1,0:T(8,128)} %get-tuple-element.383, f32[1024,3072]{1,0:T(8,128)} %get-tuple-element.427, bf16[3072,768]{1,0:T(8,128)(2,1)} %all-gather.21.cloned.1.call-done, f32[1024]{0:T(1024)S(1)} %negate_multiply_fusion.4, bf16[1,1024,768]{1,2,0:T(8,128)(2,1)S(1)} %copy-done.38, ...), kind=kOutput, calls=%fused_computation.66 | convolution fusion | flops 4882956288 | bytes 40913920 | tf_op jit(solution)/shard_map/slo,io->sli/dot_general | solution.py:36
  538.1 9.7 bitcast_add_fusion.3
  753.1 232.5 %while.33 = (s32[]{:T(128)}, bf16[12,1,1024,64]{2,3,1,0:T(8,128)(2,1)}, bf16[12,1,1024,64]{2,3,1,0:T(8,128)(2,1)}, bf16[12,1,1024,64]{2,3,1,0:T(8,128)(2,1)}, s3...) while((s32[]{:T(128)}, ...), condition=%wide.region_18.19_spmd.clone, body=%wide.region_16.18_spmd.clone.sunk | while | flops 686948352 | bytes 50890624 | solution.py:307
  985.5 9.6 convolution_bitcast_fusion.4
  1003.9 11.4 fusion.290
  1015.4 10.2 fusion.228
  1045.4 11.0 pad_maximum_fusion
  1057.2 40.1 %all-reduce.19 = (f32[768]{0:T(1024)S(1)}, f32[768]{0:T(1024)S(1)}, f32[768]{0:T(1024)S(1)}, f32[768]{0:T(1024)S(1)}, f32[768]{0:T(1024)S(1)}, /*index=5*/f32[768]{0:T(1024)S(1)}) all-reduce(f32[768]{0:T(1024)S(1)} %copy-done.135, f32[768]{0:T(1024)S(1)} %copy-done.136, ...), channel_id=11, replica_groups=mesh['dp'=8,'fsdp'=4] {'dp','fsdp'}, use_global_device_ids=true, to_apply=%region_29.30.clone | all-reduce | flops 4608 | bytes 36864
  1119.8 28.8 %reduce-scatter.16.cloned.1.call-done = f32[24,768]{1,0:T(8,128)} async-done(((f32[768,768]{1,0:T(8,128)}), f32[24,768]{1,0:T(8,128)}) %reduce-scatter.16.cloned.1.call-update) | async-done | bytes 73744 | tf_op jit(solution)/shard_map/reduce_scatter | solution.py:349
  1148.6 103.9 %reduce-scatter.14.cloned.1.call-done = f32[256,72]{0,1:T(8,128)} async-done(((f32[256,2304]{0,1:T(8,128)}), f32[256,72]{0,1:T(8,128)}) %reduce-scatter.14.cloned.1.call-update) | async-done | bytes 73744 | tf_op jit(solution)/shard_map/reduce_scatter | solution.py:346
  1252.5 125.4 %reduce-scatter.26.cloned.1.call-done = f32[24,2304]{1,0:T(8,128)} async-done(((f32[768,2304]{1,0:T(8,128)}), f32[24,2304]{1,0:T(8,128)}) %reduce-scatter.26.cloned.1.call-update) | async-done | bytes 221200
  1377.9 141.2 %reduce-scatter.22.cloned.1.call-done = f32[96,768]{1,0:T(8,128)} async-done(((f32[3072,768]{1,0:T(8,128)}), f32[96,768]{1,0:T(8,128)}) %reduce-scatter.22.cloned.1.call-update) | async-done | bytes 294928 | tf_op jit(solution)/shard_map/reduce_scatter | solution.py:352
  1519.0 142.0 %reduce-scatter.20.cloned.1.call-done = f32[24,3072]{1,0:T(8,128)} async-done(((f32[768,3072]{1,0:T(8,128)}), f32[24,3072]{1,0:T(8,128)}) %reduce-scatter.20.cloned.1.call-update) | async-done | bytes 294928 | tf_op jit(solution)/shard_map/reduce_scatter | solution.py:351
  1661.0 168.2 %reduce-scatter.18.cloned.1.call-done = f32[3,48,768]{2,1,0:T(8,128)} async-done(((f32[3,1536,768]{2,1,0:T(8,128)}), f32[3,48,768]{2,1,0:T(8,128)}) %reduce-scatter.18.cloned.1.call-update) | async-done | bytes 442384 | tf_op jit(solution)/shard_map/reduce_scatter | solution.py:350
  (855 shorter events, 724.0 us)
Async XLA Ops:
  7.2 104.5 %all-gather.13.cloned.1.call-start = ((), (), s32[]{:S(2)}) async-start(), calls=%async_computation.10 | async-start | bytes 1216512 | tf_op jit(solution)/shard_map/all_gather | solution.py:101
  7.9 123.9 %all-gather.15.cloned.1.call-start = ((), (), s32[]{:S(2)}) async-start(), calls=%async_computation.11 | async-start | bytes 1824768 | tf_op jit(solution)/shard_map/all_gather | solution.py:102
  8.7 178.8 %all-gather.9.cloned.1.call-start = ((), (), s32[]{:S(2)}) async-start(), calls=%async_computation.8 | async-start | bytes 3649536 | tf_op jit(solution)/shard_map/all_gather | solution.py:103
  9.4 315.7 %all-gather.11.cloned.1.call-start = ((), (), s32[]{:S(2)}) async-start(), calls=%async_computation.9 | async-start | bytes 1216512 | tf_op jit(solution)/shard_map/all_gather | solution.py:104
  10.0 323.0 %all-gather.17.cloned.1.call-start = ((), (), s32[]{:S(2)}) async-start(), calls=%async_computation.12 | async-start | bytes 7299072 | tf_op jit(solution)/shard_map/all_gather | solution.py:105
  10.6 362.4 %all-gather.23.cloned.1.call-start = ((), (), s32[]{:S(2)}) async-start(), calls=%async_computation.15 | async-start | bytes 1216512 | tf_op jit(solution)/shard_map/all_gather | solution.py:108
  11.1 427.3 %all-gather.19.cloned.1.call-start = ((), (), s32[]{:S(2)}) async-start(), calls=%async_computation.13 | async-start | bytes 4866048 | tf_op jit(solution)/shard_map/all_gather | solution.py:106
  11.9 491.9 %all-gather.21.cloned.1.call-start = ((), (), s32[]{:S(2)}) async-start(), calls=%async_computation.14 | async-start | bytes 4866048 | tf_op jit(solution)/shard_map/all_gather | solution.py:107
  12.6 1105.2 %all-reduce.23.cloned.1.call-start = ((), (), s32[]{:S(2)}) async-start(), calls=%async_computation.24 | async-start | bytes 7077888
  60.6 56.0 %copy-start.84 = (bf16[1024,256]{1,0:T(8,128)(2,1)}, bf16[1024,256]{1,0:T(8,128)(2,1)S(1)}, u32[]{:S(2)}) copy-start(bf16[1024,256]{1,0:T(8,128)(2,1)S(1)} %fusion.240) | copy-start | bytes 1572868
  61.6 60.1 %copy-start.82 = (bf16[1024,256]{1,0:T(8,128)(2,1)}, bf16[1024,256]{1,0:T(8,128)(2,1)S(1)}, u32[]{:S(2)}) copy-start(bf16[1024,256]{1,0:T(8,128)(2,1)S(1)} %fusion.239) | copy-start | bytes 1572868
  62.5 64.2 %copy-start.80 = (bf16[1024,256]{1,0:T(8,128)(2,1)}, bf16[1024,256]{1,0:T(8,128)(2,1)S(1)}, u32[]{:S(2)}) copy-start(bf16[1024,256]{1,0:T(8,128)(2,1)S(1)} %fusion.238) | copy-start | bytes 1572868
  101.2 282.5 %copy-start.110 = (f32[768]{0:T(1024)}, f32[768]{0:T(1024)S(1)}, u32[]{:S(2)}) copy-start(f32[768]{0:T(1024)S(1)} %convert_element_type.271) | copy-start | bytes 9220
  101.2 282.5 %copy-start.123 = (f32[768]{0:T(1024)}, f32[768]{0:T(1024)S(1)}, u32[]{:S(2)}) copy-start(f32[768]{0:T(1024)S(1)} %convert_element_type.272) | copy-start | bytes 9220
  104.4 238.3 %copy-start.155 = (pred[1024]{0:T(1024)(128)(4,1)}, pred[1024]{0:T(1024)(128)(4,1)S(1)}, u32[]{:S(2)}) copy-start(pred[1024]{0:T(1024)(128)(4,1)S(1)} %iota_compare_fusion.26) | copy-start | bytes 3076
  330.0 53.7 %copy-start.2 = (f32[1,1024,768]{1,2,0:T(8,128)}, f32[1,1024,768]{1,2,0:T(8,128)S(1)}, u32[]{:S(2)}) copy-start(f32[1,1024,768]{1,2,0:T(8,128)S(1)} %get-tuple-element.425) | copy-start | bytes 9437188
  668.5 451.2 %reduce-scatter.12.cloned.1.call-start = ((), (), s32[]{:S(2)}) async-start(), calls=%async_computation.16 | async-start | bytes 1081344 | tf_op jit(solution)/shard_map/reduce_scatter | solution.py:345
  717.6 402.2 %reduce-scatter.24.cloned.1.call-start = ((), (), s32[]{:S(2)}) async-start(), calls=%async_computation.22 | async-start | bytes 2433024 | tf_op jit(solution)/shard_map/reduce_scatter | solution.py:353
  723.6 425.0 %reduce-scatter.16.cloned.1.call-start = ((), (), s32[]{:S(2)}) async-start(), calls=%async_computation.18 | async-start | bytes 2433024 | tf_op jit(solution)/shard_map/reduce_scatter | solution.py:349
  731.1 521.4 %reduce-scatter.14.cloned.1.call-start = ((), (), s32[]{:S(2)}) async-start(), calls=%async_computation.17 | async-start | bytes 2433024 | tf_op jit(solution)/shard_map/reduce_scatter | solution.py:346
  743.9 634.0 %reduce-scatter.26.cloned.1.call-start = ((), (), s32[]{:S(2)}) async-start(), calls=%async_computation.23 | async-start | bytes 7299072
  1003.3 515.8 %reduce-scatter.22.cloned.1.call-start = ((), (), s32[]{:S(2)}) async-start(), calls=%async_computation.21 | async-start | bytes 9732096 | tf_op jit(solution)/shard_map/reduce_scatter | solution.py:352
  1015.4 645.6 %reduce-scatter.20.cloned.1.call-start = ((), (), s32[]{:S(2)}) async-start(), calls=%async_computation.20 | async-start | bytes 9732096 | tf_op jit(solution)/shard_map/reduce_scatter | solution.py:351
  1025.7 803.6 %reduce-scatter.18.cloned.1.call-start = ((), (), s32[]{:S(2)}) async-start(), calls=%async_computation.19 | async-start | bytes 14598144 | tf_op jit(solution)/shard_map/reduce_scatter | solution.py:350
  (221 other events, 1398.5 us)
Sparse Core Ops, SparseCore 0:
  10.9 56.7 all-gather.12
  70.6 54.8 all-gather.14
  128.4 59.0 all-gather.8
  190.2 52.9 all-gather.10
  245.9 71.5 all-gather.16
  320.3 52.6 all-gather.22
  375.9 62.5 all-gather.18
  441.3 62.3 all-gather.20
  668.7 137.8 all-reduce.22
  809.3 133.8 reduce-scatter.11
  949.1 94.9 reduce-scatter.23
  1050.6 97.9 reduce-scatter.15
  1154.5 97.9 reduce-scatter.13
  1259.5 118.2 reduce-scatter.25
  1384.2 134.8 reduce-scatter.21
  1526.4 134.5 reduce-scatter.19
  1667.4 161.7 reduce-scatter.17
where the time goes:
time: 1850 us; the launch traced here: 1840 us
  waiting for transfers between devices  830 us (45%)
  matrix products  554 us (30%)
  other arithmetic  176 us (10%)
  blocking collectives  123 us (7%)
  local copies, waits for them, and re-layouts  118 us (6%)
    reduce_scatter x1, waiting for transfers between devices, on_device(): lax.psum_scatter(merging_weight_grad, ('dp', 'fsdp'), scatter_dimension=1...  168 us
    reduce_scatter x1, waiting for transfers between devices, on_device(): lax.psum_scatter(up_grad, ('dp', 'fsdp'), scatter_dimension=0, tiled=True)  142 us
    reduce_scatter x1, waiting for transfers between devices, on_device(): lax.psum_scatter(down_grad, ('dp', 'fsdp'), scatter_dimension=0, tiled=True)  141 us
    unnamed x19, waiting for transfers between devices  131 us
    dot_general x22, matrix products, product(): return jnp.dot(left, right, preferred_element_type=jnp.float32)  113 us
    dot_general x22, matrix products, outer_sum(): jnp.einsum('sli,slo->io', left, right, preferred_element_type=jnp.float32)  110 us
    reduce_scatter x1, waiting for transfers between devices, on_device(): lax.psum_scatter(inlet_grad, ('dp', 'fsdp'), scatter_dimension=1, tiled=T...  104 us
    dot_general x14, matrix products, back_product(): jnp.einsum('slo,io->sli', grad_rows, weight, preferred_element_type=jnp.f...  84.7 us
  transfers between devices with their start and end apart: 17, of which 10 were waited for; matrix products, arithmetic and copies ran while one was open for 35% of the time, Pallas kernels for 0%

commit v1 on v0

v1 whole, which is shorter than its diff:
```python
import functools
import math

import jax
import jax.numpy as jnp
from jax import lax
from jax.experimental import pallas as pl
from jax.experimental.pallas import tpu as pltpu
from jax.sharding import PartitionSpec as P

HEAD_DIM = 64
CHARS = 4
LANES = 128
EPS = 1e-05
MASKED = -1e30
SCALE = 1.0 / math.sqrt(HEAD_DIM)
SCALE2 = math.log2(math.e) / math.sqrt(HEAD_DIM)
AXES = ("dp", "fsdp")
VMEM_LIMIT = 56 * 1024 * 1024

def norm_apply(values, gain, shift):
    average = jnp.mean(values, axis=-1, keepdims=True)
    centred = values - average
    variance = jnp.mean(centred * centred, axis=-1, keepdims=True)
    return centred * lax.rsqrt(variance + EPS) * gain + shift


def exact_gelu(values):
    return jax.nn.gelu(values, approximate=False)


def product(left, right):
    return jnp.dot(left, right, preferred_element_type=jnp.float32)


def outer_sum(left, right):
    return jnp.einsum("sli,slo->io", left, right, preferred_element_type=jnp.float32)


def back_product(grad_rows, weight):
    return jnp.einsum("slo,io->sli", grad_rows, weight, preferred_element_type=jnp.float32)


def shift_down(values):
    return jnp.pad(values[:, :-1], ((0, 0), (1, 0), (0, 0)))


def shift_up(values):
    return jnp.pad(values[:, 1:], ((0, 0), (0, 1), (0, 0)))


def cell_forward(inputs, previous, weight, width):
    if previous is None:
        recur = jnp.zeros_like(inputs)
        before = jnp.zeros(inputs.shape[:-1] + (width,), jnp.float32)
    else:
        recur = back_product(previous, weight)
        before = previous.astype(jnp.float32)
    reset = jax.nn.sigmoid(inputs[..., :width] + recur[..., :width])
    update = jax.nn.sigmoid(inputs[..., width : 2 * width] + recur[..., width : 2 * width])
    fresh = jnp.tanh(inputs[..., 2 * width :] + reset * recur[..., 2 * width :])
    state = ((1.0 - update) * fresh + update * before).astype(jnp.bfloat16)
    return (state, (reset, update, fresh, recur[..., 2 * width :], before, previous))


def cell_backward(grad_state, kept, weight):
    reset, update, fresh, recur_new, before, previous = kept
    fresh_pre = grad_state * (1.0 - update) * (1.0 - fresh * fresh)
    update_pre = grad_state * (before - fresh) * update * (1.0 - update)
    reset_pre = fresh_pre * recur_new * reset * (1.0 - reset)
    grad_inputs = jnp.concatenate([reset_pre, update_pre, fresh_pre], axis=-1)
    if previous is None:
        return (grad_inputs, None, None)
    grad_recur = jnp.concatenate([reset_pre, update_pre, fresh_pre * reset], axis=-1).astype(
        jnp.bfloat16
    )
    grad_weight = outer_sum(grad_recur, previous)
    grad_previous = grad_state * update + product(grad_recur, weight)
    return (grad_inputs, grad_weight, grad_previous)


def dotf(a,b,ca=1,cb=0):
    return lax.dot_general(a,b,(((ca,),(cb,)),((),())),preferred_element_type=jnp.float32)

def lane_half(shape):
    return lax.broadcasted_iota(jnp.int32, shape, 1) < HEAD_DIM

def attend_kernel(rows, length_ref, q_ref, k_ref, v_ref, ctx_ref, lse_ref, kx_ref, vx_ref):
    length = k_ref.shape[0]
    lane = lax.broadcasted_iota(jnp.int32, (length, LANES), 1)
    place = lax.broadcasted_iota(jnp.int32, (length, LANES), 0)
    kx_ref[:, :LANES] = k_ref[...]
    kx_ref[:, LANES:] = jnp.where((lane == 0) & (place >= length_ref[0]), MASKED, 0.0).astype(jnp.bfloat16)
    vx_ref[:, :LANES] = v_ref[...]
    vx_ref[:, LANES:] = jnp.ones((length, LANES), jnp.bfloat16)
    low = lane_half((rows, LANES))
    one = jnp.where(lax.broadcasted_iota(jnp.int32, (rows, LANES), 1) == 0, 1.0, 0.0).astype(jnp.bfloat16)
    def step(c, _):
        at = pl.ds(pl.multiple_of(c * rows, rows), rows)
        q = q_ref[at, :].astype(jnp.float32)
        outs = []
        for h in range(2):
            mine = low if h == 0 else jnp.logical_not(low)
            qx = jnp.concatenate([jnp.where(mine, q, 0.0).astype(jnp.bfloat16), one], axis=1)
            s = dotf(qx, kx_ref[...], 1, 1)
            peak = jnp.max(s, axis=1, keepdims=True) * SCALE2
            p = jnp.exp2(s * SCALE2 - peak).astype(jnp.bfloat16)
            o = dotf(p, vx_ref[...])
            total = o[:, LANES:]
            outs.append((o[:, :LANES] / total, peak + jnp.log2(total)))
        ctx_ref[at, :] = jnp.where(low, outs[0][0], outs[1][0]).astype(jnp.bfloat16)
        lse_ref[at, :] = jnp.where(low, outs[0][1], outs[1][1])
        return 0
    lax.fori_loop(0, length // rows, step, 0, unroll=True)

def attend(mixed, lengths, width, rows=256):
    length = mixed.shape[0]
    pairs = width // LANES
    spec = lambda o: pl.BlockSpec((length, LANES), lambda p, o=o: (0, p+o))
    return pl.pallas_call(
        functools.partial(attend_kernel, rows),
        grid=(pairs,),
        in_specs=[pl.BlockSpec(memory_space=pltpu.SMEM), spec(0), spec(pairs), spec(2 * pairs)],
        out_specs=[spec(0), spec(0)],
        out_shape=[jax.ShapeDtypeStruct((length, width), jnp.bfloat16), jax.ShapeDtypeStruct((length, width), jnp.float32)],
        scratch_shapes=[pltpu.VMEM((length, 2*LANES), jnp.bfloat16), pltpu.VMEM((length, 2*LANES), jnp.bfloat16)],
        compiler_params=pltpu.CompilerParams(vmem_limit_bytes=VMEM_LIMIT),
        cost_estimate=pl.CostEstimate(flops=4*12*length*length*64, bytes_accessed=10*length*width, transcendentals=12*length*length),
    )(lengths, mixed, mixed, mixed)

def back_kernel(rows, length_ref, q_ref, k_ref, v_ref, do_ref, o_ref, lse_ref, out_ref, kx_ref, vx_ref, qt_ref, dot_ref, dk_ref, dv_ref):
    length = k_ref.shape[0]
    lane = lax.broadcasted_iota(jnp.int32, (length, LANES), 1)
    place = lax.broadcasted_iota(jnp.int32, (length, LANES), 0)
    kx_ref[:, :LANES] = k_ref[...]
    kx_ref[:, LANES:] = jnp.where((lane == 0) & (place >= length_ref[0]), MASKED, 0.0).astype(jnp.bfloat16)
    qt_ref[...] = q_ref[...].T
    dot_ref[...] = do_ref[...].T
    dk_ref[...] = jnp.zeros_like(dk_ref)
    dv_ref[...] = jnp.zeros_like(dv_ref)
    low = lane_half((rows, LANES))
    one = jnp.where(lax.broadcasted_iota(jnp.int32, (rows, LANES), 1) == 0, 1.0, 0.0).astype(jnp.bfloat16)
    def step(c, _):
        at = pl.ds(pl.multiple_of(c * rows, rows), rows)
        q = q_ref[at, :].astype(jnp.float32)
        do = do_ref[at, :].astype(jnp.float32)
        doo = do * o_ref[at, :].astype(jnp.float32)
        lse = lse_ref[at, :]
        dqs = []
        for h in range(2):
            mine = low if h == 0 else jnp.logical_not(low)
            qx = jnp.concatenate([jnp.where(mine, q, 0.0).astype(jnp.bfloat16), one], axis=1)
            s = dotf(qx, kx_ref[...], 1, 1)
            p = jnp.exp2(s * SCALE2 - lse[:, h*HEAD_DIM:h*HEAD_DIM+1])
            dp = dotf(jnp.where(mine, do, 0.0).astype(jnp.bfloat16), v_ref[...], 1, 1)
            delta = jnp.sum(jnp.where(mine, doo, 0.0), axis=1, keepdims=True)
            ds = (p * (dp - delta)).astype(jnp.bfloat16)
            pb = p.astype(jnp.bfloat16)
            hs = slice(h*HEAD_DIM, (h+1)*HEAD_DIM)
            dqs.append(dotf(ds, k_ref[...]))
            dk_ref[hs, :] += dotf(qt_ref[hs, at], ds)
            dv_ref[hs, :] += dotf(dot_ref[hs, at], pb)
        out_ref[0, at, :] = (jnp.where(low, dqs[0], dqs[1]) * SCALE).astype(jnp.bfloat16)
        return 0
    lax.fori_loop(0, length // rows, step, 0, unroll=True)
    out_ref[1] = (dk_ref[...] * SCALE).T.astype(jnp.bfloat16)
    out_ref[2] = dv_ref[...].T.astype(jnp.bfloat16)

def attend_back(mixed, context_grad, context, log_totals, lengths, width, rows=256):
    length = mixed.shape[0]
    pairs = width // LANES
    spec = lambda o: pl.BlockSpec((length, LANES), lambda p, o=o: (0, p+o))
    return pl.pallas_call(
        functools.partial(back_kernel, rows),
        grid=(pairs,),
        in_specs=[pl.BlockSpec(memory_space=pltpu.SMEM), spec(0), spec(pairs), spec(2 * pairs), spec(0), spec(0), spec(0)],
        out_specs=pl.BlockSpec((3, length, LANES), lambda p: (0, 0, p)),
        out_shape=jax.ShapeDtypeStruct((3, length, width), jnp.bfloat16),
        scratch_shapes=[pltpu.VMEM((length, 2*LANES), jnp.bfloat16), pltpu.VMEM((length, 2*LANES), jnp.bfloat16),
            pltpu.VMEM((LANES, length), jnp.bfloat16), pltpu.VMEM((LANES, length), jnp.bfloat16),
            pltpu.VMEM((LANES, length), jnp.float32), pltpu.VMEM((LANES, length), jnp.float32)],
        compiler_params=pltpu.CompilerParams(vmem_limit_bytes=VMEM_LIMIT),
        cost_estimate=pl.CostEstimate(flops=10*12*length*length*64, bytes_accessed=20*length*width, transcendentals=12*length*length),
    )(lengths, mixed, mixed, mixed, context_grad, context, log_totals)


def side_by_side(rows, groups):
    r = rows.shape[-2] // groups
    return jnp.concatenate(
        [rows[..., i * r : (i + 1) * r, :] for i in range(groups)], axis=-1
    )


def one_below_other(rows, groups):
    w = rows.shape[-1] // groups
    return jnp.concatenate(
        [rows[..., i * w : (i + 1) * w] for i in range(groups)], axis=-2
    )


def whole(part):
    return part.reshape(-1, part.shape[-1])


def shares(full, devices):
    return full.reshape(devices, -1, full.shape[-1]).astype(jnp.bfloat16)


def on_device(
    token_states,
    char_codes,
    lengths,
    token_cotangent,
    char_cotangent,
    char_table,
    recur_input,
    recur_state,
    project_weight,
    output_weight,
    merging_weight,
    up_weight,
    down_weight,
    char_weight,
    attend_gain,
    attend_shift,
    feed_gain,
    feed_shift,
    char_gain,
    char_shift,
):
    count, length, width = token_states.shape
    half = width // 2
    triple = 3 * half
    letters_count, embed_width = char_table.shape
    r = project_weight.shape[0]
    devices = width // r
    ff_blocks = up_weight.shape[1] // width
    low = jnp.bfloat16

    gains = jnp.concatenate(
        [attend_gain, attend_shift, feed_gain, feed_shift, char_gain, char_shift]
    )
    own_table = char_table.T
    gain_rows = jnp.pad(gains[None, :], ((0, own_table.shape[0] - 1), (0, 0)))
    table_rows = jnp.concatenate([own_table, gain_rows], axis=1)
    table_rows = jnp.pad(table_rows, ((0, 0), (0, triple - table_rows.shape[1])))
    first_rows = jnp.concatenate(
        [
            project_weight,
            jnp.concatenate(
                [
                    side_by_side(recur_input.T, 3),
                    side_by_side(recur_state.T, 3),
                    one_below_other(table_rows, 3),
                ],
                axis=1,
            ),
        ],
        axis=0,
    )
    first_all = lax.all_gather(first_rows, AXES, axis=0)
    second_rows = jnp.concatenate(
        [
            output_weight,
            char_weight,
            merging_weight.reshape(-1, width),
            one_below_other(up_weight, ff_blocks),
            down_weight,
        ],
        axis=0,
    )
    second_all = lax.all_gather(second_rows, AXES, axis=0)

    project_full = whole(first_all[:, :r])
    chars_all = first_all[:, r:]
    inlet_full = whole(one_below_other(chars_all[:, :, :width], 3))
    recur_full = whole(one_below_other(chars_all[:, :, width : width + triple], 3))
    table_all = side_by_side(chars_all[:, :, width + triple :], 3)
    table_full = whole(table_all[:, :, :letters_count])
    gains_all = table_all[:, 0, letters_count : letters_count + 6 * r]
    gains_all = gains_all.reshape(devices, 6, r).transpose(1, 0, 2).reshape(6, width)
    gains_all = gains_all.astype(jnp.float32)

    at = 0
    parts = []
    for rows in (r, r) + (merging_weight.shape[1],) * 3 + (ff_blocks * r, down_weight.shape[0]):
        parts.append(second_all[:, at : at + rows])
        at += rows
    output_full, branch_full = whole(parts[0]), whole(parts[1])
    merging_full = [whole(part) for part in parts[2:5]]
    upper_full = whole(side_by_side(parts[5], ff_blocks))
    lower_full = whole(parts[6])

    positions = lax.broadcasted_iota(jnp.int32, (count, length), 1)
    valid = positions < lengths[:, None]
    letters = lax.broadcasted_iota(jnp.int32, (1, 1, letters_count), 2)
    picks = []
    embeds = []
    gates = []
    for slot in range(CHARS):
        picked = (char_codes[:, :, slot][:, :, None] == letters).astype(low)
        embed = back_product(picked, table_full).astype(low)
        picks.append(picked)
        embeds.append(embed)
        gates.append(back_product(embed, inlet_full))
    forward_kept = [None] * CHARS
    state = None
    for slot in range(CHARS):
        state, forward_kept[slot] = cell_forward(
            gates[slot][..., :triple], state, recur_full[:triple], half
        )
    forward_last = state
    backward_kept = [None] * CHARS
    state = None
    for slot in range(CHARS - 1, -1, -1):
        state, backward_kept[slot] = cell_forward(
            gates[slot][..., triple:], state, recur_full[triple:], half
        )
    chars_rep = jnp.concatenate([forward_last, state], axis=-1)
    mixed = product(token_states, project_full).astype(low)[0]
    context_low, log_totals = attend(mixed, lengths, width)
    context_low = context_low[None]
    first_pre = token_states.astype(jnp.float32) + product(context_low, output_full)
    first, pull_first = jax.vjp(norm_apply, first_pre, gains_all[0], gains_all[1])
    joined = jnp.where(
        valid[..., None],
        jnp.concatenate([first.astype(low), chars_rep], axis=-1),
        jnp.zeros((), low),
    )
    merging_pre = (
        shift_down(product(joined, merging_full[0]))
        + product(joined, merging_full[1])
        + shift_up(product(joined, merging_full[2]))
    )
    merged, pull_merged = jax.vjp(exact_gelu, merging_pre)
    summed = first + merged
    summed_low = summed.astype(low)
    hidden, pull_hidden = jax.vjp(exact_gelu, product(summed_low, upper_full))
    hidden_low = hidden.astype(low)
    token_stream, pull_token = jax.vjp(
        norm_apply, summed + product(hidden_low, lower_full), gains_all[2], gains_all[3]
    )
    merged_low = merged.astype(low)
    char_stream, pull_char = jax.vjp(
        norm_apply,
        chars_rep.astype(jnp.float32) + product(merged_low, branch_full),
        gains_all[4],
        gains_all[5],
    )
    token_pre_grad, feed_gain_grad, feed_shift_grad = pull_token(
        token_cotangent.astype(jnp.float32)
    )
    feed_grad = token_pre_grad.astype(low)
    down_grad = outer_sum(hidden_low, feed_grad)
    hidden_grad = pull_hidden(back_product(feed_grad, lower_full))[0].astype(low)
    up_grad = outer_sum(summed_low, hidden_grad)
    summed_grad = token_pre_grad + back_product(hidden_grad, upper_full)
    char_pre_grad, char_gain_grad, char_shift_grad = pull_char(char_cotangent.astype(jnp.float32))
    branch_grad = char_pre_grad.astype(low)
    branch_weight_grad = outer_sum(merged_low, branch_grad)
    merging_grad = pull_merged(summed_grad + back_product(branch_grad, branch_full))[0].astype(low)
    merging_weight_grads = [
        outer_sum(shift_down(joined), merging_grad),
        outer_sum(joined, merging_grad),
        outer_sum(shift_up(joined), merging_grad),
    ]
    early = jnp.concatenate(
        [shares(branch_weight_grad, devices)]
        + [shares(part, devices) for part in merging_weight_grads]
        + [one_below_other(shares(up_grad, devices), ff_blocks)]
        + [shares(down_grad, devices)],
        axis=1,
    )
    early = lax.psum_scatter(early, AXES, scatter_dimension=0, tiled=True)[0]
    joined_grad = (
        shift_up(back_product(merging_grad, merging_full[0]))
        + back_product(merging_grad, merging_full[1])
        + shift_down(back_product(merging_grad, merging_full[2]))
    )
    joined_grad = jnp.where(valid[..., None], joined_grad, 0.0)
    first_grad = summed_grad + joined_grad[..., :width]
    rep_grad = char_pre_grad + joined_grad[..., width:]
    first_pre_grad, attend_gain_grad, attend_shift_grad = pull_first(first_grad)
    attended_grad = first_pre_grad.astype(low)
    output_weight_grad = outer_sum(context_low, attended_grad)
    context_grad = back_product(attended_grad, output_full).astype(low)
    head_grads = attend_back(mixed, context_grad[0], context_low[0], log_totals, lengths, width)
    mixed_grad = jnp.concatenate([head_grads[0], head_grads[1], head_grads[2]], axis=-1)[None]
    project_grad = outer_sum(token_states, mixed_grad)
    input_gradient = (first_pre_grad + back_product(mixed_grad, project_full)).astype(low)
    forward_inputs = [None] * CHARS
    grad_state = rep_grad[..., :half]
    forward_weight_grad = jnp.zeros((triple, half), jnp.float32)
    for slot in range(CHARS - 1, -1, -1):
        grad_in, grad_weight, grad_state = cell_backward(
            grad_state, forward_kept[slot], recur_full[:triple]
        )
        forward_inputs[slot] = grad_in
        if grad_weight is not None:
            forward_weight_grad = forward_weight_grad + grad_weight
    backward_inputs = [None] * CHARS
    grad_state = rep_grad[..., half:]
    backward_weight_grad = jnp.zeros((triple, half), jnp.float32)
    for slot in range(CHARS):
        grad_in, grad_weight, grad_state = cell_backward(
            grad_state, backward_kept[slot], recur_full[triple:]
        )
        backward_inputs[slot] = grad_in
        if grad_weight is not None:
            backward_weight_grad = backward_weight_grad + grad_weight
    recur_weight_grad = jnp.concatenate([forward_weight_grad, backward_weight_grad], axis=0)
    inlet_grad = jnp.zeros(inlet_full.shape, jnp.float32)
    table_grad = jnp.zeros(table_full.shape, jnp.float32)
    for slot in range(CHARS):
        gate_grad = jnp.concatenate([forward_inputs[slot], backward_inputs[slot]], axis=-1).astype(
            low
        )
        inlet_grad = inlet_grad + outer_sum(gate_grad, embeds[slot])
        embed_grad = product(gate_grad, inlet_full).astype(low)
        table_grad = table_grad + outer_sum(embed_grad, picks[slot])
    gain_grads = jnp.stack(
        [
            attend_gain_grad,
            attend_shift_grad,
            feed_gain_grad,
            feed_shift_grad,
            char_gain_grad,
            char_shift_grad,
        ]
    )
    gain_shares = gain_grads.reshape(6, devices, r).transpose(1, 0, 2).reshape(devices, 1, 6 * r)
    table_shares = shares(table_grad, devices)
    gain_shares = jnp.pad(
        gain_shares.astype(low), ((0, 0), (0, table_shares.shape[1] - 1), (0, 0))
    )
    table_shares = jnp.concatenate([table_shares, gain_shares], axis=2)
    table_shares = jnp.pad(
        table_shares, ((0, 0), (0, 0), (0, triple - table_shares.shape[2]))
    )
    late = jnp.concatenate(
        [
            shares(project_grad, devices),
            jnp.concatenate(
                [
                    side_by_side(shares(inlet_grad, devices), 3),
                    side_by_side(shares(recur_weight_grad, devices), 3),
                    one_below_other(table_shares, 3),
                ],
                axis=2,
            ),
            side_by_side(shares(output_weight_grad, devices), 3),
        ],
        axis=1,
    )
    late = lax.psum_scatter(late, AXES, scatter_dimension=0, tiled=True)[0].astype(jnp.float32)
    early = early.astype(jnp.float32)
    own_chars = late[r : 2 * r]
    own_table_rows = side_by_side(own_chars[:, width + triple :], 3)
    own_gains = own_table_rows[0, letters_count : letters_count + 6 * r].reshape(6, r)
    spots = []
    at = 0
    for rows in (r, 3 * merging_weight.shape[1], ff_blocks * r, down_weight.shape[0]):
        spots.append(early[at : at + rows])
        at += rows
    return (
        token_stream.astype(low),
        char_stream.astype(low),
        input_gradient,
        own_table_rows[:, :letters_count].T,
        one_below_other(own_chars[:, :width], 3).T,
        one_below_other(own_chars[:, width : width + triple], 3).T,
        late[:r],
        one_below_other(late[2 * r :], 3),
        spots[1].reshape(merging_weight.shape),
        side_by_side(spots[2], ff_blocks),
        spots[3],
        spots[0],
        own_gains[0],
        own_gains[1],
        own_gains[2],
        own_gains[3],
        own_gains[4],
        own_gains[5],
    )

def solution(mesh):
    placed = (
        P(AXES, None, None),
        P(AXES, None, None),
        P(AXES),
        P(AXES, None, None),
        P(AXES, None, None),
        P(None, AXES),
        P(None, AXES),
        P(None, AXES),
        P(AXES, None),
        P(AXES, None),
        P(None, AXES, None),
        P(AXES, None),
        P(AXES, None),
        P(AXES, None),
        P(AXES),
        P(AXES),
        P(AXES),
        P(AXES),
        P(AXES),
        P(AXES),
    )
    return jax.shard_map(
        on_device,
        mesh=mesh,
        in_specs=placed,
        out_specs=(
            P(AXES, None, None),
            P(AXES, None, None),
            P(AXES, None, None),
            P(None, AXES),
            P(None, AXES),
            P(None, AXES),
            P(AXES, None),
            P(AXES, None),
            P(None, AXES, None),
            P(AXES, None),
            P(AXES, None),
            P(AXES, None),
            P(AXES),
            P(AXES),
            P(AXES),
            P(AXES),
            P(AXES),
            P(AXES),
        ),
        check_vma=False,
    )
```

time: 1850 us -> 974 us (0.53)
  waiting for transfers between devices: 830 us -> 294 us
  matrix products: 554 us -> 265 us
  blocking collectives: 123 us -> 0 us
  local copies, waits for them, and re-layouts: 118 us -> 195 us
  Pallas kernels: 0 us -> 58.2 us
  other arithmetic: 176 us -> 135 us
    reduce_scatter x7 -> x2, waiting for transfers between devices: 584 us -> 224 us  [the longest x1 200 us: on_device(): early = lax.psum_scatter(early, AXES, scatter_dimension=0, tiled=True)[0]]
    dot_general x84 -> x0, matrix products: 246 us -> none  [the longest x24 67.7 us: head_scores(): jnp.einsum('sqd,skd->sqk', queries, keys_part, preferred_element_type=jnp...]
    unnamed x19 -> x4, waiting for transfers between devices: 131 us -> 0.07 us
    unnamed x2 -> x0, blocking collectives: 77.4 us -> none
    pallas_call x0 -> x2, Pallas kernels: none -> 58.2 us  [the longest x1 36.7 us: attend_back(): pl.pallas_call(functools.partial(back_kernel, rows), grid=(pairs,), in_sp...]
    all_gather x8 -> x2, waiting for transfers between devices: 116 us -> 70 us  [the longest x1 54.2 us: on_device(): first_all = lax.all_gather(first_rows, AXES, axis=0)]
    all_gather x1 -> x0, blocking collectives: 45.2 us -> none  [on_device(): lax.all_gather(char_table, ('dp', 'fsdp'), axis=1, tiled=True)]
    slice x2 -> x31, local copies, waits for them, and re-layouts: 3.02 us -> 40.1 us  [the longest x3 15.8 us: on_device(): parts.append(second_all[:, at:at + rows])]
  transfers between devices with their start and end apart: 17 -> 4, of which waited for: 10 -> 4; matrix products, arithmetic and copies ran while one was open for 35% -> 21% of each run, Pallas kernels for 0% -> 2%
where the time goes in v1:
time: 974 us; the launch traced here: 965 us
  waiting for transfers between devices  294 us (30%)
  matrix products  265 us (27%)
  local copies, waits for them, and re-layouts  195 us (20%)
  other arithmetic  135 us (14%)
  Pallas kernels  58.2 us (6%)
  between operations  17.3 us (2%)
    reduce_scatter x1, waiting for transfers between devices, on_device(): early = lax.psum_scatter(early, AXES, scatter_dimension=0, tiled=True)[0]  200 us
    dot_general x14, matrix products, product(): return jnp.dot(left, right, preferred_element_type=jnp.float32)  107 us
    unnamed x496, local copies, waits for them, and re-layouts  88.4 us
    dot_general x22, matrix products, outer_sum(): jnp.einsum('sli,slo->io', left, right, preferred_element_type=jnp.float32)  83.8 us
    dot_general x22, matrix products, back_product(): jnp.einsum('slo,io->sli', grad_rows, weight, preferred_element_type=jnp.f...  74.2 us
    all_gather x1, waiting for transfers between devices, on_device(): first_all = lax.all_gather(first_rows, AXES, axis=0)  54.2 us
    pallas_call x1, Pallas kernels, attend_back(): pl.pallas_call(functools.partial(back_kernel, rows), grid=(pairs,), in_sp...  36.7 us
    convert_element_type x1, other arithmetic, on_device(): hidden_low = hidden.astype(low)  27.9 us
  transfers between devices with their start and end apart: 4, of which 4 were waited for; matrix products, arithmetic and copies ran while one was open for 21% of the time, Pallas kernels for 2%

profile of v1, /device:TPU:0, one launch (start us, length us, event | category | flops | bytes accessed | tf_op | source)
XLA Modules:
  0.0 964.8 jit_solution(1466509075507569244)
XLA Ops:
  40.4 54.2 %all-gather.5.cloned.1.call-done = bf16[1536,2304]{1,0:T(8,128)(2,1)} async-done(((bf16[48,2304]{1,0:T(8,128)(2,1)}), bf16[1536,2304]{1,0:T(8,128)(2,1)}) %all-gather.5.cloned.1.call-update) | async-done | bytes 7077904 | tf_op jit(solution)/shard_map/all_gather | solution.py:261
  113.4 7.3 fusion.32.q_ref.k_ref.v_ref
  120.7 21.5 %shard_map.331 = (bf16[1024,768]{1,0:T(8,128)(2,1)}, f32[1024,768]{1,0:T(8,128)}) custom-call(s32[1]{0:T(128)} %copy.388.length_ref, bf16[1024,2304]{1,0:T(8,128)(2,1)} %fusion.32.q_ref.k_ref.v_ref, bf16[1024,2304]{1,0:T(8,128)(2,1)} %fusion.32.q_ref.k_ref.v_ref, bf16[1024,2304]{1,0:T(8,128)(2,1)} %fusion.32.q_ref.k_ref.v_ref), custom_call_target="tpu_custom_call" | custom-call | flops 3221225472 | bytes 7864320 | tf_op jit(solution)/shard_map/pallas_call | solution.py:120
  204.8 15.9 %all-gather.7.cloned.1.call-done = bf16[12288,768]{1,0:T(8,128)(2,1)} async-done(((bf16[384,768]{1,0:T(8,128)(2,1)}), bf16[12288,768]{1,0:T(8,128)(2,1)}) %all-gather.7.cloned.1.call-update) | async-done | bytes 18874384 | tf_op jit(solution)/shard_map/all_gather | solution.py:272
  224.3 7.0 fusion.344
  248.6 23.3 %fusion.240 = (bf16[1,1024,768]{1,2,0:T(8,128)(2,1)}, f32[1,1024,768]{1,2,0:T(8,128)S(1)}, f32[1,1024,768]{1,2,0:T(8,128)S(1)}) fusion(f32[1,1023,768]{1,2,0:T(8,128)S(1)} %slice.822, bf16[1536,768]{1,0:T(8,128)(2,1)S(1)} %bitcast.597, bf16[1,1024,1,1,1,1,384]{1,6,5,4,3,2,0:T(8,128)(2,1)S(1)} %bitcast.577, ...), kind=kOutput, calls=%fused_computation.396 | convolution fusion | flops 2479620096 | bytes 19655680 | tf_op jit(solution)/shard_map/dot_general | solution.py:33
  275.6 35.2 %fusion = (f32[1024,3072]{1,0:T(8,128)}, f32[1024,3072]{1,0:T(8,128)}) fusion(bf16[768,3072]{1,0:T(8,128)(2,1)S(1)} %bitcast.590, bf16[1,1024,768]{1,2,0:T(8,128)(2,1)S(1)} %get-tuple-element.159), kind=kOutput, calls=%fused_computation.2 | convolution fusion | flops 5026873344 | bytes 31457280 | tf_op jit(solution)/shard_map/dot_general | solution.py:33
  310.8 13.5 %fusion.364 = (f32[1024]{0:T(1024)S(1)}, f32[1,1024,768]{1,2,0:T(8,128)}) fusion(f32[1,1024,768]{1,2,0:T(8,128)S(1)} %get-tuple-element.160, bf16[3072,768]{1,0:T(8,128)(2,1)} %bitcast.588, f32[1024,3072]{1,0:T(8,128)} %get-tuple-element.267, f32[1024,3072]{1,0:T(8,128)} %get-tuple-element.268), kind=kOutput, calls=%fused_computation.579 | convolution fusion | flops 4842847232 | bytes 36179968 | tf_op jit(solution)/shard_map/dot_general | solution.py:33
  332.1 18.7 %add_convert_fusion = bf16[1024,3072]{1,0:T(8,128)(2,1)} fusion(f32[1024,3072]{1,0:T(8,128)} %get-tuple-element.267, f32[1024,3072]{1,0:T(8,128)} %get-tuple-element.268, bf16[3072,768]{1,0:T(8,128)(2,1)} %bitcast.589, f32[1024]{0:T(1024)S(1)} %negate_multiply_fusion.4, bf16[1,1024,768]{1,2,0:T(8,128)(2,1)} %copy.251, ...), kind=kOutput, calls=%fused_computation.23 | convolution fusion | flops 4882956288 | bytes 40913920 | tf_op jit(solution)/shard_map/slo,io->sli/dot_general | solution.py:41
  350.9 10.2 %bitcast_add_fusion.3 = f32[1,1024,768]{1,2,0:T(8,128)S(1)} fusion(bf16[1024,3072]{1,0:T(8,128)(2,1)} %add_convert_fusion, bf16[768,3072]{1,0:T(8,128)(2,1)} %bitcast.591, f32[1024]{0:T(1024)S(1)} %negate_multiply_fusion.4, f32[1024]{0:T(1024)S(1)} %get-tuple-element.262, f32[1,1024,768]{1,2,0:T(8,128)} %get-tuple-element.270, ...), kind=kOutput, calls=%fused_computation.118 | convolution fusion | flops 4838916096 | bytes 18893824 | tf_op jit(solution)/shard_map/slo,io->sli/dot_general | solution.py:41
  422.3 6.3 fusion.251
  450.2 6.6 fusion.37
  463.2 36.7 %shard_map.332 = bf16[3,1024,768]{2,1,0:T(8,128)(2,1)} custom-call(s32[1]{0:T(128)} %copy.388.length_ref, bf16[1024,2304]{1,0:T(8,128)(2,1)} %fusion.32.q_ref.k_ref.v_ref, bf16[1024,2304]{1,0:T(8,128)(2,1)} %fusion.32.q_ref.k_ref.v_ref, bf16[1024,2304]{1,0:T(8,128)(2,1)} %fusion.32.q_ref.k_ref.v_ref, bf16[1024,768]{1,0:T(8,128)(2,1)} %convolution_convert_fusion.2.do_ref, ...), custom_call_target="tpu_custom_call" | custom-call | flops 8053063680 | bytes 15728640 | tf_op jit(solution)/shard_map/pallas_call | solution.py:173
  569.6 7.0 fusion.226
  576.6 6.8 fusion.225
  583.5 6.6 fusion.239
  597.1 8.5 fusion.34
  609.8 11.2 %copy.275 = bf16[32,56,2304]{2,1,0:T(8,128)(2,1)} copy(bf16[32,56,2304]{2,0,1:T(8,128)(2,1)} %maximum_maximum_fusion) | data formatting | bytes 16515072 | tf_op jit(solution)/shard_map/concatenate | solution.py:440
  631.7 27.9 %fusion.3 = bf16[3072,1024]{0,1:T(8,128)(2,1)} fusion(f32[1024,3072]{1,0:T(8,128)S(1)} %bitcast.564), kind=kLoop, calls=%fused_computation.5 | loop fusion | flops 204472320 | bytes 18874368 | tf_op jit(solution)/shard_map/convert_element_type | solution.py:339
  659.5 8.6 copy.280
  697.8 7.7 convert_dynamic-update-slice_fusion
  713.9 8.4 fusion.60
  724.9 24.6 %reduce-scatter.3.cloned.1.call-done = bf16[1,56,2304]{2,1,0:T(8,128)(2,1)} async-done(((bf16[32,56,2304]{2,1,0:T(8,128)(2,1)}), bf16[1,56,2304]{2,1,0:T(8,128)(2,1)}) %reduce-scatter.3.cloned.1.call-update) | async-done | bytes 258064 | tf_op jit(solution)/shard_map/reduce_scatter | solution.py:455
  754.4 199.6 %reduce-scatter.5.cloned.1.call-done = bf16[1,360,768]{2,1,0:T(8,128)(2,1)} async-done(((bf16[32,360,768]{2,1,0:T(8,128)(2,1)}), bf16[1,360,768]{2,1,0:T(8,128)(2,1)}) %reduce-scatter.5.cloned.1.call-update) | async-done | bytes 552976 | tf_op jit(solution)/shard_map/reduce_scatter | solution.py:374
  (703 shorter events, 374.5 us)
Async XLA Ops:
  7.2 23.5 %copy-start.69 = (bf16[1,1024,768]{2,1,0:T(8,128)(2,1)S(1)}, bf16[1,1024,768]{2,1,0:T(8,128)(2,1)}, u32[]{:S(2)}) copy-start(bf16[1,1024,768]{2,1,0:T(8,128)(2,1)} %param.23) | copy-start | bytes 4718596
  7.2 25.1 %copy-start.70 = (bf16[1,1024,768]{2,1,0:T(8,128)(2,1)S(1)}, bf16[1,1024,768]{2,1,0:T(8,128)(2,1)}, u32[]{:S(2)}) copy-start(bf16[1,1024,768]{2,1,0:T(8,128)(2,1)} %param.24) | copy-start | bytes 4718596
  7.2 87.3 %all-gather.5.cloned.1.call-start = ((), (), s32[]{:S(2)}) async-start(), calls=%async_computation.4 | async-start | bytes 7299072 | tf_op jit(solution)/shard_map/all_gather | solution.py:261
  19.0 201.7 %all-gather.7.cloned.1.call-start = ((), (), s32[]{:S(2)}) async-start(), calls=%async_computation.5 | async-start | bytes 19464192 | tf_op jit(solution)/shard_map/all_gather | solution.py:272
  30.6 718.8 %reduce-scatter.3.cloned.1.call-start = ((), (), s32[]{:S(2)}) async-start(), calls=%async_computation.2 | async-start | bytes 8515584 | tf_op jit(solution)/shard_map/reduce_scatter | solution.py:455
  40.4 112.4 %copy-start.181 = (s32[1,1024,1]{1,2,0:T(1,128)}, s32[1,1024,1]{1,2,0:T(1,128)S(1)}, u32[]{:S(2)}) copy-start(s32[1,1024,1]{1,2,0:T(1,128)S(1)} %get-tuple-element.256) | copy-start | bytes 12292
  97.8 22.9 %copy-start.73 = (bf16[32,24,2304]{2,1,0:T(8,128)(2,1)}, bf16[32,24,2304]{2,1,0:T(8,128)(2,1)S(1)}, u32[]{:S(2)}) copy-start(bf16[32,24,2304]{2,1,0:T(8,128)(2,1)S(1)} %slice.760) | copy-start | bytes 10616836
  102.8 169.1 %copy-start.154 = (f32[768]{0:T(1024)}, f32[768]{0:T(1024)S(1)}, u32[]{:S(2)}) copy-start(f32[768]{0:T(1024)S(1)} %add.310) | copy-start | bytes 9220
  105.1 166.9 %copy-start.147 = (f32[768]{0:T(1024)}, f32[768]{0:T(1024)S(1)}, u32[]{:S(2)}) copy-start(f32[768]{0:T(1024)S(1)} %mul.590) | copy-start | bytes 9220
  153.5 23.8 %copy-start.141 = (bf16[1024,256]{1,0:T(8,128)(2,1)}, bf16[1024,256]{1,0:T(8,128)(2,1)S(1)}, u32[]{:S(2)}) copy-start(bf16[1024,256]{1,0:T(8,128)(2,1)S(1)} %fusion.227) | copy-start | bytes 1572868
  163.9 30.5 %copy-start.6 = (f32[1,1024,2304]{1,2,0:T(8,128)}, f32[1,1024,2304]{1,2,0:T(8,128)S(1)}, u32[]{:S(2)}) copy-start(f32[1,1024,2304]{1,2,0:T(8,128)S(1)} %convolution_bitcast_fusion.1) | copy-start | bytes 28311556
  204.8 43.8 %copy-start.58 = (bf16[1,1024,384]{1,2,0:T(8,128)(2,1)}, bf16[1,1024,384]{1,2,0:T(8,128)(2,1)S(1)}, u32[]{:S(2)}) copy-start(bf16[1,1024,384]{1,2,0:T(8,128)(2,1)S(1)} %get-tuple-element.172) | copy-start | bytes 2359300
  224.3 24.3 %copy-start.89 = (bf16[32,48,768]{2,1,0:T(8,128)(2,1)}, bf16[32,48,768]{2,1,0:T(8,128)(2,1)S(1)}, u32[]{:S(2)}) copy-start(bf16[32,48,768]{2,1,0:T(8,128)(2,1)S(1)} %get-tuple-element.189) | copy-start | bytes 7077892
  238.1 33.9 %copy-start = (f32[1,1024,768]{1,2,0:T(8,128)}, f32[1,1024,768]{1,2,0:T(8,128)S(1)}, u32[]{:S(2)}) copy-start(f32[1,1024,768]{1,2,0:T(8,128)S(1)} %get-tuple-element.265) | copy-start | bytes 9437188
  238.1 33.9 %copy-start.145 = (f32[1024]{0:T(1024)}, f32[1024]{0:T(1024)S(1)}, u32[]{:S(2)}) copy-start(f32[1024]{0:T(1024)S(1)} %broadcast_multiply_fusion.2) | copy-start | bytes 12292
  238.5 33.4 %copy-start.149 = (f32[1024]{0:T(1024)}, f32[1024]{0:T(1024)S(1)}, u32[]{:S(2)}) copy-start(f32[1024]{0:T(1024)S(1)} %fusion.287) | copy-start | bytes 12292
  275.1 35.7 %copy-start.71 = (bf16[32,24,3072]{2,1,0:T(8,128)(2,1)}, bf16[32,24,3072]{2,1,0:T(8,128)(2,1)S(1)}, u32[]{:S(2)}) copy-start(bf16[32,24,3072]{2,1,0:T(8,128)(2,1)S(1)} %pad_maximum_fusion) | copy-start | bytes 14155780
  324.3 26.6 %copy-start.165 = (f32[1024]{0:T(1024)}, f32[1024]{0:T(1024)S(1)}, u32[]{:S(2)}) copy-start(f32[1024]{0:T(1024)S(1)} %broadcast_multiply_fusion.1) | copy-start | bytes 12292
  327.8 38.7 %copy-start.2 = (f32[1024,768]{0,1:T(8,128)}, f32[1024,768]{0,1:T(8,128)S(1)}, u32[]{:S(2)}) copy-start(f32[1024,768]{0,1:T(8,128)S(1)} %get-tuple-element.272) | copy-start | bytes 9437188
  327.8 57.0 %copy-start.151 = (f32[1024]{0:T(1024)}, f32[1024]{0:T(1024)S(1)}, u32[]{:S(2)}) copy-start(f32[1024]{0:T(1024)S(1)} %broadcast_multiply_fusion) | copy-start | bytes 12292
  460.3 44.4 %copy-start.179 = (f32[1024]{0:T(1024)}, f32[1024]{0:T(1024)S(1)}, u32[]{:S(2)}) copy-start(f32[1024]{0:T(1024)S(1)} %negate_multiply_fusion.2) | copy-start | bytes 12292
  460.5 47.4 %slice-start.26 = ((s8[4718592]{0:T(1024)(128)(4,1)}), s8[4194304]{0:T(1024)(128)(4,1)S(1)}, s32[]{:S(2)}) async-start(s8[4718592]{0:T(1024)(128)(4,1)} %bitcast.567), calls=%async_computation.32 | async-start | bytes 8388608
  463.2 44.8 %slice-start.27 = ((s8[4718592]{0:T(1024)(128)(4,1)}), s8[524288]{0:T(1024)(128)(4,1)S(1)}, s32[]{:S(2)}) async-start(s8[4718592]{0:T(1024)(128)(4,1)} %bitcast.567), calls=%async_computation.33 | async-start | bytes 1048576
  621.0 333.0 %reduce-scatter.5.cloned.1.call-start = ((), (), s32[]{:S(2)}) async-start(), calls=%async_computation.3 | async-start | bytes 18247680 | tf_op jit(solution)/shard_map/reduce_scatter | solution.py:374
  (211 other events, 991.1 us)
Sparse Core Ops, SparseCore 0:
  19.1 75.3 all-gather.4
  97.4 123.2 all-gather.6
  621.1 128.2 reduce-scatter.2
  756.9 197.0 reduce-scatter.4

commit v2 on v1

--- a/solution.py
+++ b/solution.py
@@ -25,58 +25,24 @@
     return centred * lax.rsqrt(variance + EPS) * gain + shift
 
 
-def exact_gelu(values):
-    return jax.nn.gelu(values, approximate=False)
-
-
 def product(left, right):
     return jnp.dot(left, right, preferred_element_type=jnp.float32)
 
 
 def outer_sum(left, right):
-    return jnp.einsum("sli,slo->io", left, right, preferred_element_type=jnp.float32)
+    return jnp.einsum("li,lo->io", left, right, preferred_element_type=jnp.float32)
 
 
 def back_product(grad_rows, weight):
-    return jnp.einsum("slo,io->sli", grad_rows, weight, preferred_element_type=jnp.float32)
+    return jnp.einsum("lo,io->li", grad_rows, weight, preferred_element_type=jnp.float32)
 
 
 def shift_down(values):
-    return jnp.pad(values[:, :-1], ((0, 0), (1, 0), (0, 0)))
+    return jnp.pad(values[:-1], ((1, 0), (0, 0)))
 
 
 def shift_up(values):
-    return jnp.pad(values[:, 1:], ((0, 0), (0, 1), (0, 0)))
-
-
-def cell_forward(inputs, previous, weight, width):
-    if previous is None:
-        recur = jnp.zeros_like(inputs)
-        before = jnp.zeros(inputs.shape[:-1] + (width,), jnp.float32)
-    else:
-        recur = back_product(previous, weight)
-        before = previous.astype(jnp.float32)
-    reset = jax.nn.sigmoid(inputs[..., :width] + recur[..., :width])
-    update = jax.nn.sigmoid(inputs[..., width : 2 * width] + recur[..., width : 2 * width])
-    fresh = jnp.tanh(inputs[..., 2 * width :] + reset * recur[..., 2 * width :])
-    state = ((1.0 - update) * fresh + update * before).astype(jnp.bfloat16)
-    return (state, (reset, update, fresh, recur[..., 2 * width :], before, previous))
-
-
-def cell_backward(grad_state, kept, weight):
-    reset, update, fresh, recur_new, before, previous = kept
-    fresh_pre = grad_state * (1.0 - update) * (1.0 - fresh * fresh)
-    update_pre = grad_state * (before - fresh) * update * (1.0 - update)
-    reset_pre = fresh_pre * recur_new * reset * (1.0 - reset)
-    grad_inputs = jnp.concatenate([reset_pre, update_pre, fresh_pre], axis=-1)
-    if previous is None:
-        return (grad_inputs, None, None)
-    grad_recur = jnp.concatenate([reset_pre, update_pre, fresh_pre * reset], axis=-1).astype(
-        jnp.bfloat16
-    )
-    grad_weight = outer_sum(grad_recur, previous)
-    grad_previous = grad_state * update + product(grad_recur, weight)
-    return (grad_inputs, grad_weight, grad_previous)
+    return jnp.pad(values[1:], ((0, 1), (0, 0)))
 
 
 def dotf(a,b,ca=1,cb=0):
@@ -184,6 +150,247 @@
     )(lengths, mixed, mixed, mixed, context_grad, context, log_totals)
 
 
+ROOT_HALF = math.sqrt(0.5)
+DENSITY = 1.0 / math.sqrt(2.0 * math.pi)
+
+def gelu_both(values):
+    below = 0.5 + 0.5 * lax.erf(values * ROOT_HALF)
+    return values * below, below + values * (DENSITY * jnp.exp(-0.5 * values * values))
+
+def norm_parts(values):
+    average = jnp.mean(values, axis=-1, keepdims=True)
+    centred = values - average
+    spread = lax.rsqrt(jnp.mean(centred * centred, axis=-1, keepdims=True) + EPS)
+    return centred * spread, spread
+
+def norm_back(normed, spread, scaled):
+    return spread * (scaled - jnp.mean(scaled, axis=-1, keepdims=True)
+                     - normed * jnp.mean(scaled * normed, axis=-1, keepdims=True))
+
+def column_sums(values):
+    rows, width = values.shape
+    return jnp.sum(values.reshape(rows // 8, 8, width), axis=0)
+
+def chars_kernel(half, codes_ref, table_ref, inlet_ref, recur_ref, embed_ref, rep_ref, states_ref, coef_ref):
+    rows = codes_ref.shape[0]
+    triple = 3 * half
+    width = embed_ref.shape[1] // CHARS
+    letters = lax.broadcasted_iota(jnp.int32, (rows, table_ref.shape[1]), 1)
+    embeds = []
+    for slot in range(CHARS):
+        picked = jnp.where(codes_ref[:, slot : slot + 1] == letters, 1.0, 0.0).astype(jnp.bfloat16)
+        embed = dotf(picked, table_ref[...], 1, 1).astype(jnp.bfloat16)
+        embed_ref[:, slot * width : (slot + 1) * width] = embed
+        embeds.append(embed)
+    low = jnp.bfloat16
+    for side in range(2):
+        state = None
+        base = side * triple
+        order = range(CHARS) if side == 0 else range(CHARS - 1, -1, -1)
+        for step, slot in enumerate(order):
+            gates = dotf(embeds[slot], inlet_ref[base : base + triple, :], 1, 1)
+            if state is None:
+                update = jax.nn.sigmoid(gates[:, half : 2 * half])
+                fresh = jnp.tanh(gates[:, 2 * half :])
+                new = (1.0 - update) * fresh
+                coef_ref[side, 0] = ((1.0 - update) * (1.0 - fresh * fresh)).astype(low)
+                coef_ref[side, 1] = (-fresh * update * (1.0 - update)).astype(low)
+            else:
+                recur = dotf(state, recur_ref[base : base + triple, :], 1, 1)
+                reset = jax.nn.sigmoid(gates[:, :half] + recur[:, :half])
+                update = jax.nn.sigmoid(gates[:, half : 2 * half] + recur[:, half : 2 * half])
+                recur_new = recur[:, 2 * half :]
+                fresh = jnp.tanh(gates[:, 2 * half :] + reset * recur_new)
+                before = state.astype(jnp.float32)
+                new = (1.0 - update) * fresh + update * before
+                at = 2 + 5 * (step - 1)
+                coef_ref[side, at] = ((1.0 - update) * (1.0 - fresh * fresh)).astype(low)
+                coef_ref[side, at + 1] = ((before - fresh) * update * (1.0 - update)).astype(low)
+                coef_ref[side, at + 2] = (recur_new * reset * (1.0 - reset)).astype(low)
+                coef_ref[side, at + 3] = reset.astype(low)
+                coef_ref[side, at + 4] = update.astype(low)
+            state = new.astype(low)
+            if step < CHARS - 1:
+                states_ref[side, step] = state
+        rep_ref[:, side * half : (side + 1) * half] = state
+
+COEFS = 2 + 5 * (CHARS - 1)
+
+def chars_forward(codes, table, inlet, recur, rows=256):
+    length = codes.shape[0]
+    embed, half = inlet.shape[1], recur.shape[1]
+    low = jnp.bfloat16
+    full = lambda a: pl.BlockSpec(a.shape, lambda b: (0, 0))
+    return pl.pallas_call(
+        functools.partial(chars_kernel, half),
+        grid=(length // rows,),
+        in_specs=[pl.BlockSpec((rows, CHARS), lambda b: (b, 0)), full(table), full(inlet), full(recur)],
+        out_specs=[
+            pl.BlockSpec((rows, CHARS * embed), lambda b: (b, 0)),
+            pl.BlockSpec((rows, 2 * half), lambda b: (b, 0)),
+            pl.BlockSpec((2, CHARS - 1, rows, half), lambda b: (0, 0, b, 0)),
+            pl.BlockSpec((2, COEFS, rows, half), lambda b: (0, 0, b, 0)),
+        ],
+        out_shape=[
+            jax.ShapeDtypeStruct((length, CHARS * embed), low),
+            jax.ShapeDtypeStruct((length, 2 * half), low),
+            jax.ShapeDtypeStruct((2, CHARS - 1, length, half), low),
+            jax.ShapeDtypeStruct((2, COEFS, length, half), low),
+        ],
+        compiler_params=pltpu.CompilerParams(vmem_limit_bytes=VMEM_LIMIT),
+        cost_estimate=pl.CostEstimate(flops=12 * 10**9, bytes_accessed=40 * 10**6, transcendentals=10**7),
+    )(codes, table, inlet, recur)
+
+def chars_back_kernel(half, codes_ref, inlet_ref, recur_ref, embed_ref, states_ref, coef_ref, grad_ref,
+                      table_out, inlet_out, recur_out, gates_ref, lets_ref, table_acc, inlet_acc, recur_acc):
+    rows = codes_ref.shape[0]
+    triple = 3 * half
+    width = embed_ref.shape[1] // CHARS
+    low = jnp.bfloat16
+    first, last = pl.program_id(0) == 0, pl.program_id(0) == pl.num_programs(0) - 1
+
+    @pl.when(first)
+    def _():
+        table_acc[...] = jnp.zeros_like(table_acc)
+        inlet_acc[...] = jnp.zeros_like(inlet_acc)
+        recur_acc[...] = jnp.zeros_like(recur_acc)
+
+    for side in range(2):
+        grad = grad_ref[:, side * half : (side + 1) * half]
+        base = side * triple
+        order = range(CHARS) if side == 0 else range(CHARS - 1, -1, -1)
+        for step, slot in reversed(list(enumerate(order))):
+            at = 2 + 5 * (step - 1) if step else 0
+            load = lambda k: coef_ref[side, at + k].astype(jnp.float32)
+            fresh_pre = grad * load(0)
+            update_pre = grad * load(1)
+            spot = slice(slot * rows, (slot + 1) * rows)
+            gates_ref[spot, base + half : base + 2 * half] = update_pre.astype(low)
+            gates_ref[spot, base + 2 * half : base + triple] = fresh_pre.astype(low)
+            if step == 0:
+                gates_ref[spot, base : base + half] = jnp.zeros((rows, half), low)
+                continue
+            reset_pre = fresh_pre * load(2)
+            gates_ref[spot, base : base + half] = reset_pre.astype(low)
+            recur_grad = jnp.concatenate(
+                [reset_pre.astype(low), update_pre.astype(low), (fresh_pre * load(3)).astype(low)], axis=1)
+            recur_acc[base : base + triple, :] += dotf(recur_grad, states_ref[side, step - 1], 0, 0)
+            grad = grad * load(4) + dotf(recur_grad, recur_ref[base : base + triple, :])
+    embed_all = jnp.concatenate([embed_ref[:, j * width : (j + 1) * width] for j in range(CHARS)], axis=0)
+    inlet_acc[...] += dotf(gates_ref[...], embed_all, 0, 0)
+    embed_grad = dotf(gates_ref[...], inlet_ref[...]).astype(low)
+    letters = lax.broadcasted_iota(jnp.int32, (rows, table_acc.shape[1]), 1)
+    for slot in range(CHARS):
+        lets_ref[slot * rows : (slot + 1) * rows, :] = jnp.where(
+            codes_ref[:, slot : slot + 1] == letters, 1.0, 0.0).astype(low)
+    table_acc[...] += dotf(embed_grad, lets_ref[...], 0, 0)
+
+    @pl.when(last)
+    def _():
+        table_out[...] = table_acc[...].astype(low)
+        inlet_out[...] = inlet_acc[...].astype(low)
+        recur_out[...] = recur_acc[...].astype(low)
+
+def chars_back(codes, inlet, recur, embeds, states, coefs, grad, letters, rows=256):
+    length = codes.shape[0]
+    embed, half = inlet.shape[1], recur.shape[1]
+    low = jnp.bfloat16
+    full = lambda a: pl.BlockSpec(a.shape, lambda b: (0, 0))
+    outs = [(embed, letters), inlet.shape, recur.shape]
+    return pl.pallas_call(
+        functools.partial(chars_back_kernel, half),
+        grid=(length // rows,),
+        in_specs=[
+            pl.BlockSpec((rows, CHARS), lambda b: (b, 0)), full(inlet), full(recur),
+            pl.BlockSpec((rows, CHARS * embed), lambda b: (b, 0)),
+            pl.BlockSpec((2, CHARS - 1, rows, half), lambda b: (0, 0, b, 0)),
+            pl.BlockSpec((2, COEFS, rows, half), lambda b: (0, 0, b, 0)),
+            pl.BlockSpec((rows, 2 * half), lambda b: (b, 0)),
+        ],
+        out_specs=[pl.BlockSpec(s, lambda b: (0, 0)) for s in outs],
+        out_shape=[jax.ShapeDtypeStruct(s, low) for s in outs],
+        scratch_shapes=[
+            pltpu.VMEM((CHARS * rows, 6 * half), low), pltpu.VMEM((CHARS * rows, letters), low),
+            ] + [pltpu.VMEM(s, jnp.float32) for s in outs],
+        compiler_params=pltpu.CompilerParams(vmem_limit_bytes=VMEM_LIMIT),
+        cost_estimate=pl.CostEstimate(flops=22 * 10**9, bytes_accessed=40 * 10**6, transcendentals=0),
+    )(codes, inlet, recur, embeds, states, coefs, grad)
+
+def feed_kernel(blocks, joined_ref, first_ref, rep_ref, token_cot_ref, char_cot_ref, gains_ref,
+                merging_ref, up_ref, down_ref, branch_ref,
+                token_ref, char_ref, summed_ref, merged_ref, hidden_ref, feed_grad_ref, hidden_grad_ref,
+                branch_grad_ref, merging_grad_ref, summed_grad_ref, char_grad_ref, sums_ref, slope_ref):
+    low = jnp.bfloat16
+    width = first_ref.shape[1]
+    step = up_ref.shape[1] // blocks
+
+    @pl.when(pl.program_id(0) == 0)
+    def _():
+        sums_ref[...] = jnp.zeros_like(sums_ref)
+
+    merged, merging_slope = gelu_both(dotf(joined_ref[...], merging_ref[...]))
+    merged_low = merged.astype(low)
+    merged_ref[...] = merged_low
+    summed = first_ref[...] + merged
+    summed_low = summed.astype(low)
+    summed_ref[...] = summed_low
+    total = summed
+    for c in range(blocks):
+        cols = slice(c * step, (c + 1) * step)
+        hidden, slope = gelu_both(dotf(summed_low, up_ref[:, cols]))
+        slope_ref[:, cols] = slope
+        hidden_low = hidden.astype(low)
+        hidden_ref[:, cols] = hidden_low
+        total = total + dotf(hidden_low, down_ref[cols, :])
+    normed, spread = norm_parts(total)
+    gain, shift = gains_ref[2:3, :], gains_ref[3:4, :]
+    token_ref[...] = (normed * gain + shift).astype(low)
+    cot = token_cot_ref[...].astype(jnp.float32)
+    sums_ref[0] += column_sums(cot * normed)
+    sums_ref[1] += column_sums(cot)
+    token_grad = norm_back(normed, spread, cot * gain)
+    feed_grad = token_grad.astype(low)
+    feed_grad_ref[...] = feed_grad
+    total = token_grad
+    for c in range(blocks):
+        cols = slice(c * step, (c + 1) * step)
+        hidden_grad = (slope_ref[:, cols] * dotf(feed_grad, down_ref[cols, :], 1, 1)).astype(low)
+        hidden_grad_ref[:, cols] = hidden_grad
+        total = total + dotf(hidden_grad, up_ref[:, cols], 1, 1)
+    summed_grad_ref[...] = total
+    normed, spread = norm_parts(rep_ref[...].astype(jnp.float32) + dotf(merged_low, branch_ref[...]))
+    gain, shift = gains_ref[4:5, :], gains_ref[5:6, :]
+    char_ref[...] = (normed * gain + shift).astype(low)
+    cot = char_cot_ref[...].astype(jnp.float32)
+    sums_ref[2] += column_sums(cot * normed)
+    sums_ref[3] += column_sums(cot)
+    char_grad = norm_back(normed, spread, cot * gain)
+    char_grad_ref[...] = char_grad
+    branch_grad = char_grad.astype(low)
+    branch_grad_ref[...] = branch_grad
+    merging_grad_ref[...] = (merging_slope * (total + dotf(branch_grad, branch_ref[...], 1, 1))).astype(low)
+
+def feed(joined, first, rep, token_cot, char_cot, gains, merging, up, down, branch, rows=256, blocks=2):
+    length, width = first.shape
+    ff = up.shape[1]
+    low, wide = jnp.bfloat16, jnp.float32
+    row = lambda w: pl.BlockSpec((rows, w), lambda b: (b, 0))
+    full = lambda a: pl.BlockSpec(a.shape, lambda b: (0, 0), pipeline_mode=pl.Buffered(1))
+    outs = [(width, low), (width, low), (width, low), (width, low), (ff, low), (width, low), (ff, low),
+            (width, low), (width, low), (width, wide), (width, wide)]
+    return pl.pallas_call(
+        functools.partial(feed_kernel, blocks),
+        grid=(length // rows,),
+        in_specs=[row(joined.shape[1]), row(width), row(width), row(width), row(width), full(gains),
+                  full(merging), full(up), full(down), full(branch)],
+        out_specs=[row(w) for w, _ in outs] + [pl.BlockSpec((4, 8, width), lambda b: (0, 0, 0))],
+        out_shape=[jax.ShapeDtypeStruct((length, w), t) for w, t in outs] + [jax.ShapeDtypeStruct((4, 8, width), wide)],
+        scratch_shapes=[pltpu.VMEM((rows, ff), wide)],
+        compiler_params=pltpu.CompilerParams(vmem_limit_bytes=VMEM_LIMIT),
+        cost_estimate=pl.CostEstimate(flops=30 * 10**9, bytes_accessed=70 * 10**6, transcendentals=10**7),
+    )(joined, first, rep, token_cot, char_cot, gains, merging, up, down, branch)
+
+
 def side_by_side(rows, groups):
     r = rows.shape[-2] // groups
     return jnp.concatenate(
@@ -228,10 +435,10 @@
     char_gain,
     char_shift,
 ):
-    count, length, width = token_states.shape
+    length, width = token_states.shape[1:]
     half = width // 2
     triple = 3 * half
-    letters_count, embed_width = char_table.shape
+    letters_count = char_table.shape[0]
     r = project_weight.shape[0]
     devices = width // r
     ff_blocks = up_weight.shape[1] // width
@@ -276,7 +483,7 @@
     inlet_full = whole(one_below_other(chars_all[:, :, :width], 3))
     recur_full = whole(one_below_other(chars_all[:, :, width : width + triple], 3))
     table_all = side_by_side(chars_all[:, :, width + triple :], 3)
-    table_full = whole(table_all[:, :, :letters_count])
+    table_full = whole(table_all[:, :, : pl.cdiv(letters_count, LANES) * LANES])
     gains_all = table_all[:, 0, letters_count : letters_count + 6 * r]
     gains_all = gains_all.reshape(devices, 6, r).transpose(1, 0, 2).reshape(6, width)
     gains_all = gains_all.astype(jnp.float32)
@@ -291,133 +498,76 @@
     upper_full = whole(side_by_side(parts[5], ff_blocks))
     lower_full = whole(parts[6])
 
-    positions = lax.broadcasted_iota(jnp.int32, (count, length), 1)
-    valid = positions < lengths[:, None]
-    letters = lax.broadcasted_iota(jnp.int32, (1, 1, letters_count), 2)
-    picks = []
-    embeds = []
-    gates = []
-    for slot in range(CHARS):
-        picked = (char_codes[:, :, slot][:, :, None] == letters).astype(low)
-        embed = back_product(picked, table_full).astype(low)
-        picks.append(picked)
-        embeds.append(embed)
-        gates.append(back_product(embed, inlet_full))
-    forward_kept = [None] * CHARS
-    state = None
-    for slot in range(CHARS):
-        state, forward_kept[slot] = cell_forward(
-            gates[slot][..., :triple], state, recur_full[:triple], half
-        )
-    forward_last = state
-    backward_kept = [None] * CHARS
-    state = None
-    for slot in range(CHARS - 1, -1, -1):
-        state, backward_kept[slot] = cell_forward(
-            gates[slot][..., triple:], state, recur_full[triple:], half
-        )
-    chars_rep = jnp.concatenate([forward_last, state], axis=-1)
-    mixed = product(token_states, project_full).astype(low)[0]
+    states, codes = token_states[0], char_codes[0]
+    valid = lax.broadcasted_iota(jnp.int32, (length, 1), 0) < lengths
+    embeds, chars_rep, char_states, coefs = chars_forward(
+        codes, table_full, inlet_full, recur_full
+    )
+    mixed = product(states, project_full).astype(low)
     context_low, log_totals = attend(mixed, lengths, width)
-    context_low = context_low[None]
-    first_pre = token_states.astype(jnp.float32) + product(context_low, output_full)
+    first_pre = states.astype(jnp.float32) + product(context_low, output_full)
     first, pull_first = jax.vjp(norm_apply, first_pre, gains_all[0], gains_all[1])
     joined = jnp.where(
-        valid[..., None],
-        jnp.concatenate([first.astype(low), chars_rep], axis=-1),
-        jnp.zeros((), low),
-    )
-    merging_pre = (
-        shift_down(product(joined, merging_full[0]))
-        + product(joined, merging_full[1])
-        + shift_up(product(joined, merging_full[2]))
-    )
-    merged, pull_merged = jax.vjp(exact_gelu, merging_pre)
-    summed = first + merged
-    summed_low = summed.astype(low)
-    hidden, pull_hidden = jax.vjp(exact_gelu, product(summed_low, upper_full))
-    hidden_low = hidden.astype(low)
-    token_stream, pull_token = jax.vjp(
-        norm_apply, summed + product(hidden_low, lower_full), gains_all[2], gains_all[3]
-    )
-    merged_low = merged.astype(low)
-    char_stream, pull_char = jax.vjp(
-        norm_apply,
-        chars_rep.astype(jnp.float32) + product(merged_low, branch_full),
-        gains_all[4],
-        gains_all[5],
-    )
-    token_pre_grad, feed_gain_grad, feed_shift_grad = pull_token(
-        token_cotangent.astype(jnp.float32)
-    )
-    feed_grad = token_pre_grad.astype(low)
-    down_grad = outer_sum(hidden_low, feed_grad)
-    hidden_grad = pull_hidden(back_product(feed_grad, lower_full))[0].astype(low)
-    up_grad = outer_sum(summed_low, hidden_grad)
-    summed_grad = token_pre_grad + back_product(hidden_grad, upper_full)
-    char_pre_grad, char_gain_grad, char_shift_grad = pull_char(char_cotangent.astype(jnp.float32))
-    branch_grad = char_pre_grad.astype(low)
-    branch_weight_grad = outer_sum(merged_low, branch_grad)
-    merging_grad = pull_merged(summed_grad + back_product(branch_grad, branch_full))[0].astype(low)
-    merging_weight_grads = [
-        outer_sum(shift_down(joined), merging_grad),
-        outer_sum(joined, merging_grad),
-        outer_sum(shift_up(joined), merging_grad),
-    ]
+        valid, jnp.concatenate([first.astype(low), chars_rep], axis=-1), jnp.zeros((), low)
+    )
+    joined = jnp.concatenate([shift_down(joined), joined, shift_up(joined)], axis=1)
+    (
+        token_stream,
+        char_stream,
+        summed_low,
+        merged_low,
+        hidden_low,
+        feed_grad,
+        hidden_grad,
+        branch_grad,
+        merging_grad,
+        summed_grad,
+        char_pre_grad,
+        gain_sums,
+    ) = feed(
+        joined,
+        first,
+        chars_rep,
+        token_cotangent[0],
+        char_cotangent[0],
+        gains_all,
+        jnp.concatenate(merging_full, axis=0),
+        upper_full,
+        lower_full,
+        branch_full,
+    )
+    feed_gain_grad, feed_shift_grad, char_gain_grad, char_shift_grad = jnp.sum(gain_sums, axis=1)
     early = jnp.concatenate(
-        [shares(branch_weight_grad, devices)]
-        + [shares(part, devices) for part in merging_weight_grads]
-        + [one_below_other(shares(up_grad, devices), ff_blocks)]
-        + [shares(down_grad, devices)],
+        [shares(outer_sum(merged_low, branch_grad), devices)]
+        + [
+            shares(outer_sum(joined[:, 2 * i * width : 2 * (i + 1) * width], merging_grad), devices)
+            for i in range(3)
+        ]
+        + [one_below_other(shares(outer_sum(summed_low, hidden_grad), devices), ff_blocks)]
+        + [shares(outer_sum(hidden_low, feed_grad), devices)],
         axis=1,
     )
+    early, merging_grad = lax.optimization_barrier((early, merging_grad))
     early = lax.psum_scatter(early, AXES, scatter_dimension=0, tiled=True)[0]
     joined_grad = (
         shift_up(back_product(merging_grad, merging_full[0]))
         + back_product(merging_grad, merging_full[1])
         + shift_down(back_product(merging_grad, merging_full[2]))
     )
-    joined_grad = jnp.where(valid[..., None], joined_grad, 0.0)
-    first_grad = summed_grad + joined_grad[..., :width]
-    rep_grad = char_pre_grad + joined_grad[..., width:]
+    joined_grad = jnp.where(valid, joined_grad, 0.0)
+    first_grad = summed_grad + joined_grad[:, :width]
+    rep_grad = char_pre_grad + joined_grad[:, width:]
     first_pre_grad, attend_gain_grad, attend_shift_grad = pull_first(first_grad)
+    table_grad, inlet_grad, recur_weight_grad = chars_back(
+        codes, inlet_full, recur_full, embeds, char_states, coefs, rep_grad, table_full.shape[1]
+    )
     attended_grad = first_pre_grad.astype(low)
     output_weight_grad = outer_sum(context_low, attended_grad)
     context_grad = back_product(attended_grad, output_full).astype(low)
-    head_grads = attend_back(mixed, context_grad[0], context_low[0], log_totals, lengths, width)
-    mixed_grad = jnp.concatenate([head_grads[0], head_grads[1], head_grads[2]], axis=-1)[None]
-    project_grad = outer_sum(token_states, mixed_grad)
+    head_grads = attend_back(mixed, context_grad, context_low, log_totals, lengths, width)
+    mixed_grad = jnp.concatenate([head_grads[0], head_grads[1], head_grads[2]], axis=-1)
+    project_grad = outer_sum(states, mixed_grad)
     input_gradient = (first_pre_grad + back_product(mixed_grad, project_full)).astype(low)
-    forward_inputs = [None] * CHARS
-    grad_state = rep_grad[..., :half]
-    forward_weight_grad = jnp.zeros((triple, half), jnp.float32)
-    for slot in range(CHARS - 1, -1, -1):
-        grad_in, grad_weight, grad_state = cell_backward(
-            grad_state, forward_kept[slot], recur_full[:triple]
-        )
-        forward_inputs[slot] = grad_in
-        if grad_weight is not None:
-            forward_weight_grad = forward_weight_grad + grad_weight
-    backward_inputs = [None] * CHARS
-    grad_state = rep_grad[..., half:]
-    backward_weight_grad = jnp.zeros((triple, half), jnp.float32)
-    for slot in range(CHARS):
-        grad_in, grad_weight, grad_state = cell_backward(
-            grad_state, backward_kept[slot], recur_full[triple:]
-        )
-        backward_inputs[slot] = grad_in
-        if grad_weight is not None:
-            backward_weight_grad = backward_weight_grad + grad_weight
-    recur_weight_grad = jnp.concatenate([forward_weight_grad, backward_weight_grad], axis=0)
-    inlet_grad = jnp.zeros(inlet_full.shape, jnp.float32)
-    table_grad = jnp.zeros(table_full.shape, jnp.float32)
-    for slot in range(CHARS):
-        gate_grad = jnp.concatenate([forward_inputs[slot], backward_inputs[slot]], axis=-1).astype(
-            low
-        )
-        inlet_grad = inlet_grad + outer_sum(gate_grad, embeds[slot])
-        embed_grad = product(gate_grad, inlet_full).astype(low)
-        table_grad = table_grad + outer_sum(embed_grad, picks[slot])
     gain_grads = jnp.stack(
         [
             attend_gain_grad,
@@ -429,7 +579,7 @@
         ]
     )
     gain_shares = gain_grads.reshape(6, devices, r).transpose(1, 0, 2).reshape(devices, 1, 6 * r)
-    table_shares = shares(table_grad, devices)
+    table_shares = shares(table_grad, devices)[:, :, :letters_count]
     gain_shares = jnp.pad(
         gain_shares.astype(low), ((0, 0), (0, table_shares.shape[1] - 1), (0, 0))
     )
@@ -463,9 +613,9 @@
         spots.append(early[at : at + rows])
         at += rows
     return (
-        token_stream.astype(low),
-        char_stream.astype(low),
-        input_gradient,
+        token_stream[None],
+        char_stream[None],
+        input_gradient[None],
         own_table_rows[:, :letters_count].T,
         one_below_other(own_chars[:, :width], 3).T,
         one_below_other(own_chars[:, width : width + triple], 3).T,

time: 974 us -> 818 us (0.84)
  matrix products: 265 us -> 61.5 us
  waiting for transfers between devices: 294 us -> 436 us
  Pallas kernels: 58.2 us -> 177 us
  local copies, waits for them, and re-layouts: 195 us -> 78.9 us
  other arithmetic: 135 us -> 38.3 us
    pallas_call x0 -> x3, Pallas kernels: none -> 119 us  [the longest x1 51.6 us: feed(): pl.pallas_call(functools.partial(feed_kernel, blocks), grid=(length // ro...]
    dot_general x44 -> x13, matrix products: 158 us -> 54.6 us  [the longest x8 30.7 us: outer_sum(): jnp.einsum('li,lo->io', left, right, preferred_element_type=jnp.float32)]
    dot_general x14 -> x2, matrix products: 107 us -> 6.96 us  [product(): return jnp.dot(left, right, preferred_element_type=jnp.float32)]
    reduce_scatter x1, waiting for transfers between devices: 24.6 us -> 118 us  [on_device(): lax.psum_scatter(late, AXES, scatter_dimension=0, tiled=True)[0]]
    unnamed x496 -> x117, local copies, waits for them, and re-layouts: 88.4 us -> 28.9 us
    convert_element_type x10 -> x1, other arithmetic: 54.7 us -> 0.02 us  [on_device(): gain_shares.astype(low)]
    all_gather x1, waiting for transfers between devices: 15.9 us -> 52.8 us  [on_device(): second_all = lax.all_gather(second_rows, AXES, axis=0)]
    unnamed x33 -> x2, other arithmetic: 26.3 us -> 0.01 us
  transfers between devices with their start and end apart: 4 -> 4, of which waited for: 4 -> 4; matrix products, arithmetic and copies ran while one was open for 21% -> 6% of each run, Pallas kernels for 2% -> 6%
where the time goes in v2:
time: 818 us; the launch traced here: 808 us
  waiting for transfers between devices  436 us (53%)
  Pallas kernels  177 us (22%)
  local copies, waits for them, and re-layouts  78.9 us (10%)
  matrix products  61.5 us (8%)
  other arithmetic  38.3 us (5%)
  between operations  15.4 us (2%)
    reduce_scatter x1, waiting for transfers between devices, on_device(): early = lax.psum_scatter(early, AXES, scatter_dimension=0, tiled=True)[0]  200 us
    reduce_scatter x1, waiting for transfers between devices, on_device(): lax.psum_scatter(late, AXES, scatter_dimension=0, tiled=True)[0]  118 us
    all_gather x1, waiting for transfers between devices, on_device(): first_all = lax.all_gather(first_rows, AXES, axis=0)  65.1 us
    all_gather x1, waiting for transfers between devices, on_device(): second_all = lax.all_gather(second_rows, AXES, axis=0)  52.8 us
    pallas_call x1, Pallas kernels, feed(): pl.pallas_call(functools.partial(feed_kernel, blocks), grid=(length // ro...  51.6 us
    pallas_call x1, Pallas kernels, chars_back(): pl.pallas_call(functools.partial(chars_back_kernel, half), grid=(length /...  41.4 us
    pallas_call x1, Pallas kernels, attend_back(): pl.pallas_call(functools.partial(back_kernel, rows), grid=(pairs,), in_sp...  36.5 us
    dot_general x8, matrix products, outer_sum(): jnp.einsum('li,lo->io', left, right, preferred_element_type=jnp.float32)  30.7 us
  transfers between devices with their start and end apart: 4, of which 4 were waited for; matrix products, arithmetic and copies ran while one was open for 6% of the time, Pallas kernels for 6%

profile of v2, /device:TPU:0, one launch (start us, length us, event | category | flops | bytes accessed | tf_op | source)
XLA Modules:
  0.0 807.9 jit_solution(1167392368397985757)
XLA Ops:
  7.2 4.1 concatenate.77
  29.2 65.1 %all-gather.5.cloned.1.call-done = bf16[1536,2304]{1,0:T(8,128)(2,1)} async-done(((bf16[48,2304]{1,0:T(8,128)(2,1)}), bf16[1536,2304]{1,0:T(8,128)(2,1)}) %all-gather.5.cloned.1.call-update) | async-done | bytes 7077904 | tf_op jit(solution)/shard_map/all_gather | solution.py:468
  114.9 5.4 fusion.q_ref.k_ref.v_ref
  120.3 21.5 %shard_map.331 = (bf16[1024,768]{1,0:T(8,128)(2,1)}, f32[1024,768]{1,0:T(8,128)}) custom-call(s32[1]{0:T(128)} %copy.104.length_ref, bf16[1024,2304]{1,0:T(8,128)(2,1)} %fusion.q_ref.k_ref.v_ref, bf16[1024,2304]{1,0:T(8,128)(2,1)} %fusion.q_ref.k_ref.v_ref, bf16[1024,2304]{1,0:T(8,128)(2,1)} %fusion.q_ref.k_ref.v_ref), custom_call_target="tpu_custom_call" | custom-call | flops 3221225472 | bytes 7864320 | tf_op jit(solution)/shard_map/pallas_call | solution.py:86
  141.9 26.4 %shard_map.332 = (bf16[1024,1024]{1,0:T(8,128)(2,1)}, bf16[1024,768]{1,0:T(8,128)(2,1)}, bf16[2,3,1024,384]{3,2,1,0:T(8,128)(2,1)}, bf16[2,17,1024,384]{3,2,1,0:T(8,128)(2,1)}) custom-call(s32[1024,4]{1,0:T(8,128)} %bitcast.160, bf16[256,1024]{1,0:T(8,128)(2,1)} %fusion.11.table_ref, bf16[2304,256]{1,0:T(8,128)(2,1)} %bitcast.156, bf16[2304,384]{1,0:T(8,128)(2,1)} %bitcast.143), custom_call_target="tpu_custom_call" | custom-call | flops 12000000000 | bytes 40000000 | tf_op jit(solution)/shard_map/pallas_call | solution.py:224
  168.3 52.8 %all-gather.7.cloned.1.call-done = bf16[12288,768]{1,0:T(8,128)(2,1)} async-done(((bf16[384,768]{1,0:T(8,128)(2,1)}), bf16[12288,768]{1,0:T(8,128)(2,1)}) %all-gather.7.cloned.1.call-update) | async-done | bytes 18874384 | tf_op jit(solution)/shard_map/all_gather | solution.py:479
  221.1 4.8 slice.496
  225.8 5.4 fusion.22
  231.2 5.5 fusion.23
  246.0 5.1 pad_maximum_fusion.joined_ref
  257.5 51.6 %shard_map.333 = (bf16[1024,768]{1,0:T(8,128)(2,1)}, bf16[1024,768]{1,0:T(8,128)(2,1)}, bf16[1024,768]{1,0:T(8,128)(2,1)}, bf16[1024,768]{1,0:T(8,128)(2,1)}, bf...) custom-call(bf16[1024,4608]{1,0:T(8,128)(2,1)} %pad_maximum_fusion.j, ...), custom_call_target="tpu_custom_call" | custom-call | flops 30000001024 | bytes 70000000 | tf_op jit(solution)/shard_map/pallas_call | solution.py:381
  309.2 5.1 convolution_convert_fusion.4
  323.1 5.4 convolution_convert_fusion.2
  338.1 6.0 convolution_convert_fusion.1
  346.6 4.9 fusion.3
  354.2 5.1 add_select_fusion
  359.3 4.7 multiply_reduce_fusion
  370.5 36.5 %shard_map.334 = bf16[3,1024,768]{2,1,0:T(8,128)(2,1)} custom-call(s32[1]{0:T(128)} %copy.104.length_ref, bf16[1024,2304]{1,0:T(8,128)(2,1)} %fusion.q_ref.k_ref.v_ref, bf16[1024,2304]{1,0:T(8,128)(2,1)} %fusion.q_ref.k_ref.v_ref, bf16[1024,2304]{1,0:T(8,128)(2,1)} %fusion.q_ref.k_ref.v_ref, bf16[1024,768]{1,0:T(8,128)(2,1)} %convolution_convert_fusion.7.do_ref, ...), custom_call_target="tpu_custom_call" | custom-call | flops 8053063680 | bytes 15728640 | tf_op jit(solution)/shard_map/pallas_call | solution.py:139
  409.7 41.4 %shard_map.335 = (bf16[256,1024]{1,0:T(8,128)(2,1)}, bf16[2304,256]{1,0:T(8,128)(2,1)}, bf16[2304,384]{1,0:T(8,128)(2,1)}) custom-call(s32[1024,4]{1,0:T(8,128)} %bitcast.161, bf16[2304,256]{1,0:T(8,128)(2,1)} %bitcast.157, bf16[2304,384]{1,0:T(8,128)(2,1)} %bitcast.144, bf16[1024,1024]{1,0:T(8,128)(2,1)} %get-tuple-element.55.embed_ref, ...), custom_call_target="tpu_custom_call" | custom-call | flops 22000001024 | bytes 40000000 | tf_op jit(solution)/shard_map/pallas_call | solution.py:300
  455.1 5.1 convolution_convert_fusion.3
  460.3 3.6 maximum_maximum_fusion
  465.9 8.5 %fusion.2 = bf16[1,1024,768]{2,1,0:T(8,128)(2,1)} fusion(f32[1024,768]{1,0:T(8,128)} %copy-done.13, f32[1024]{0:T(1024)S(1)} %negate_multiply_fusion, bf16[768,2304]{1,0:T(8,128)(2,1)S(1)} %bitcast.138, bf16[1024,768]{1,0:T(8,128)(2,1)} %copy-done.18, bf16[1024,768]{1,0:T(8,128)(2,1)} %copy-done.19, bf16[1024,768]{1,0:T(8,128)(2,1)} %copy-done.17), kind=kOutput, calls=%fused_computation.28 | convolution fusion | flops 3640393728 | bytes 12980224 | tf_op jit(solution)/shard_map/lo,io->li/dot_general | solution.py:37
  474.4 118.0 %reduce-scatter.3.cloned.1.call-done = bf16[1,56,2304]{2,1,0:T(8,128)(2,1)} async-done(((bf16[32,56,2304]{2,1,0:T(8,128)(2,1)}), bf16[1,56,2304]{2,1,0:T(8,128)(2,1)}) %reduce-scatter.3.cloned.1.call-update) | async-done | bytes 258064 | tf_op jit(solution)/shard_map/reduce_scatter | solution.py:605
  597.3 199.7 %reduce-scatter.5.cloned.1.call-done = bf16[1,360,768]{2,1,0:T(8,128)(2,1)} async-done(((bf16[32,360,768]{2,1,0:T(8,128)(2,1)}), bf16[1,360,768]{2,1,0:T(8,128)(2,1)}) %reduce-scatter.5.cloned.1.call-update) | async-done | bytes 552976 | tf_op jit(solution)/shard_map/reduce_scatter | solution.py:551
  (200 shorter events, 100.8 us)
Async XLA Ops:
  7.2 87.1 %all-gather.5.cloned.1.call-start = ((), (), s32[]{:S(2)}) async-start(), calls=%async_computation.4 | async-start | bytes 7299072 | tf_op jit(solution)/shard_map/all_gather | solution.py:468
  18.8 202.3 %all-gather.7.cloned.1.call-start = ((), (), s32[]{:S(2)}) async-start(), calls=%async_computation.5 | async-start | bytes 19464192 | tf_op jit(solution)/shard_map/all_gather | solution.py:479
  26.2 566.2 %reduce-scatter.3.cloned.1.call-start = ((), (), s32[]{:S(2)}) async-start(), calls=%async_computation.2 | async-start | bytes 8515584 | tf_op jit(solution)/shard_map/reduce_scatter | solution.py:605
  97.6 17.3 %copy-start.11 = (bf16[32,24,2304]{2,1,0:T(8,128)(2,1)}, bf16[32,24,2304]{2,1,0:T(8,128)(2,1)S(1)}, u32[]{:S(2)}) copy-start(bf16[32,24,2304]{2,1,0:T(8,128)(2,1)S(1)} %slice.473) | copy-start | bytes 10616836
  231.2 5.5 copy-start.23
  231.2 5.5 copy-start.32
  231.2 5.5 copy-start.34
  236.7 14.4 %copy-start = (bf16[32,48,768]{2,1,0:T(8,128)(2,1)}, bf16[32,48,768]{2,1,0:T(8,128)(2,1)S(1)}, u32[]{:S(2)}) copy-start(bf16[32,48,768]{2,1,0:T(8,128)(2,1)S(1)} %get-tuple-element.80) | copy-start | bytes 7077892
  236.7 14.4 %copy-start.5 = (bf16[32,48,768]{2,1,0:T(8,128)(2,1)}, bf16[32,48,768]{2,1,0:T(8,128)(2,1)S(1)}, u32[]{:S(2)}) copy-start(bf16[32,48,768]{2,1,0:T(8,128)(2,1)S(1)} %get-tuple-element.78) | copy-start | bytes 7077892
  246.0 5.1 copy-start.7
  251.1 4.0 copy-start.10
  309.1 5.2 copy-start.20
  314.3 8.8 %slice-start = ((s8[6291456]{0:T(1024)(128)(4,1)}), s8[4194304]{0:T(1024)(128)(4,1)S(1)}, s32[]{:S(2)}) async-start(s8[6291456]{0:T(1024)(128)(4,1)} %bitcast.179), calls=%async_computation.6 | async-start | bytes 8388608
  317.5 5.6 slice-start.1
  330.1 8.0 slice-start.2
  333.4 4.7 slice-start.3
  346.6 4.9 copy-start.6
  346.6 4.9 copy-start.21
  354.2 5.2 copy-start.14
  409.6 45.4 %copy-start.17 = (bf16[1024,768]{1,0:T(8,128)(2,1)}, bf16[1024,768]{1,0:T(8,128)(2,1)S(1)}, u32[]{:S(2)}) copy-start(bf16[1024,768]{1,0:T(8,128)(2,1)S(1)} %get-tuple-element.91) | copy-start | bytes 4718596
  409.6 45.4 %copy-start.18 = (bf16[1024,768]{1,0:T(8,128)(2,1)}, bf16[1024,768]{1,0:T(8,128)(2,1)S(1)}, u32[]{:S(2)}) copy-start(bf16[1024,768]{1,0:T(8,128)(2,1)S(1)} %get-tuple-element.92) | copy-start | bytes 4718596
  409.7 45.4 %copy-start.19 = (bf16[1024,768]{1,0:T(8,128)(2,1)}, bf16[1024,768]{1,0:T(8,128)(2,1)S(1)}, u32[]{:S(2)}) copy-start(bf16[1024,768]{1,0:T(8,128)(2,1)S(1)} %get-tuple-element.93) | copy-start | bytes 4718596
  451.1 3.7 copy-start.16
  463.9 333.1 %reduce-scatter.5.cloned.1.call-start = ((), (), s32[]{:S(2)}) async-start(), calls=%async_computation.3 | async-start | bytes 18247680 | tf_op jit(solution)/shard_map/reduce_scatter | solution.py:551
  (24 other events, 58.2 us)
Sparse Core Ops, SparseCore 0:
  18.9 75.3 all-gather.4
  97.8 123.2 all-gather.6
  464.0 128.3 reduce-scatter.2
  599.8 197.1 reduce-scatter.4

commit v3 on v2

--- a/solution.py
+++ b/solution.py
@@ -1,4 +1,5 @@
 import functools
+import itertools
 import math
 
 import jax
@@ -413,7 +414,88 @@
     return full.reshape(devices, -1, full.shape[-1]).astype(jnp.bfloat16)
 
 
+class Grid:
+    def __init__(self, sizes):
+        dp, fsdp = sizes
+        z = 4 if dp % 4 == 0 else 1
+        core = 2 if fsdp % 2 == 0 else 1
+        self.fsdp = fsdp
+        self.shape = (z, dp // z, fsdp // core, core)
+        self.devices = dp * fsdp
+
+    def own(self):
+        z, x, y, core = self.shape
+        dp, fsdp = lax.axis_index("dp"), lax.axis_index("fsdp")
+        return dp // x, dp % x, fsdp // core, fsdp % core
+
+    def send(self, values, shift):
+        pairs = []
+        for source, place in enumerate(itertools.product(*map(range, self.shape))):
+            target = 0
+            for at, by, size in zip(place, shift, self.shape):
+                target = target * size + (at + by) % size
+            pairs.append((source, target))
+        return lax.ppermute(values, AXES, pairs)
+
+    def plane(self):
+        z, x, y, core = self.shape
+        return [(i, j) for i in range(x) for j in range(y) if i or j]
+
+
+def gather_rows(grid, part):
+    nz, nx, ny, ncore = grid.shape
+    z, x, y, core = grid.own()
+    put = lax.dynamic_update_slice
+    rows, width = part.shape
+    column = jnp.zeros((nz, rows, width), part.dtype)
+    column = put(column, part[None], (z, 0, 0))
+    for s in range(1, nz):
+        came = grid.send(part, (s, 0, 0, 0))
+        column = put(column, came[None], ((z - s) % nz, 0, 0))
+    layer = jnp.zeros((nz, nx, ny, rows, width), part.dtype)
+    layer = put(layer, column[:, None, None], (0, x, y, 0, 0))
+    for i, j in grid.plane():
+        came = grid.send(column, (0, i, j, 0))
+        layer = put(layer, came[:, None, None], (0, (x - i) % nx, (y - j) % ny, 0, 0))
+    full = jnp.zeros((nz, nx, ny, ncore, rows, width), part.dtype)
+    full = put(full, layer[:, :, :, None], (0, 0, 0, core, 0, 0))
+    for s in range(1, ncore):
+        came = grid.send(layer, (0, 0, 0, s))
+        full = put(full, came[:, :, :, None], (0, 0, 0, (core - s) % ncore, 0, 0))
+    return full.reshape(-1, width)
+
+
+def scatter_sums(grid, parts):
+    nz, nx, ny, ncore = grid.shape
+    z, x, y, core = grid.own()
+    rows, width = parts.shape[1:]
+    wide, low = jnp.float32, jnp.bfloat16
+    parts = parts.reshape(nz, nx, ny, ncore, rows, width)
+
+    def of_core(at):
+        return lax.dynamic_index_in_dim(parts, at, 3, False)
+
+    total = of_core(core).astype(wide)
+    for s in range(1, ncore):
+        total = total + grid.send(of_core((core + s) % ncore), (0, 0, 0, s)).astype(wide)
+    layer = total.astype(low)
+
+    def of_column(i, j):
+        return lax.dynamic_slice(layer, (0, i, j, 0, 0), (nz, 1, 1, rows, width))[:, 0, 0]
+
+    total = of_column(x, y).astype(wide)
+    for i, j in grid.plane():
+        total = total + grid.send(of_column((x + i) % nx, (y + j) % ny), (0, i, j, 0)).astype(wide)
+    column = total.astype(low)
+    total = lax.dynamic_index_in_dim(column, z, 0, False).astype(wide)
+    for s in range(1, nz):
+        came = grid.send(lax.dynamic_index_in_dim(column, (z + s) % nz, 0, False), (s, 0, 0, 0))
+        total = total + came.astype(wide)
+    return total
+
+
 def on_device(
+    sizes,
     token_states,
     char_codes,
     lengths,
@@ -440,32 +522,11 @@
     triple = 3 * half
     letters_count = char_table.shape[0]
     r = project_weight.shape[0]
-    devices = width // r
+    grid = Grid(sizes)
+    devices = grid.devices
     ff_blocks = up_weight.shape[1] // width
     low = jnp.bfloat16
 
-    gains = jnp.concatenate(
-        [attend_gain, attend_shift, feed_gain, feed_shift, char_gain, char_shift]
-    )
-    own_table = char_table.T
-    gain_rows = jnp.pad(gains[None, :], ((0, own_table.shape[0] - 1), (0, 0)))
-    table_rows = jnp.concatenate([own_table, gain_rows], axis=1)
-    table_rows = jnp.pad(table_rows, ((0, 0), (0, triple - table_rows.shape[1])))
-    first_rows = jnp.concatenate(
-        [
-            project_weight,
-            jnp.concatenate(
-                [
-                    side_by_side(recur_input.T, 3),
-                    side_by_side(recur_state.T, 3),
-                    one_below_other(table_rows, 3),
-                ],
-                axis=1,
-            ),
-        ],
-        axis=0,
-    )
-    first_all = lax.all_gather(first_rows, AXES, axis=0)
     second_rows = jnp.concatenate(
         [
             output_weight,
@@ -477,9 +538,23 @@
         axis=0,
     )
     second_all = lax.all_gather(second_rows, AXES, axis=0)
-
-    project_full = whole(first_all[:, :r])
-    chars_all = first_all[:, r:]
+    gains = jnp.stack(
+        [attend_gain, attend_shift, feed_gain, feed_shift, char_gain, char_shift]
+    ).reshape(1, 6 * r)
+    own_table = char_table.T
+    gain_rows = jnp.pad(gains, ((0, own_table.shape[0] - 1), (0, 0)))
+    table_rows = jnp.concatenate([own_table, gain_rows], axis=1)
+    table_rows = jnp.pad(table_rows, ((0, 0), (0, triple - table_rows.shape[1])))
+    char_rows = jnp.concatenate(
+        [
+            side_by_side(recur_input.T, 3),
+            side_by_side(recur_state.T, 3),
+            one_below_other(table_rows, 3),
+        ],
+        axis=1,
+    )
+    project_full = gather_rows(grid, project_weight)
+    chars_all = gather_rows(grid, char_rows).reshape(devices, r, 3 * width)
     inlet_full = whole(one_below_other(chars_all[:, :, :width], 3))
     recur_full = whole(one_below_other(chars_all[:, :, width : width + triple], 3))
     table_all = side_by_side(chars_all[:, :, width + triple :], 3)
@@ -564,10 +639,6 @@
     attended_grad = first_pre_grad.astype(low)
     output_weight_grad = outer_sum(context_low, attended_grad)
     context_grad = back_product(attended_grad, output_full).astype(low)
-    head_grads = attend_back(mixed, context_grad, context_low, log_totals, lengths, width)
-    mixed_grad = jnp.concatenate([head_grads[0], head_grads[1], head_grads[2]], axis=-1)
-    project_grad = outer_sum(states, mixed_grad)
-    input_gradient = (first_pre_grad + back_product(mixed_grad, project_full)).astype(low)
     gain_grads = jnp.stack(
         [
             attend_gain_grad,
@@ -589,7 +660,6 @@
     )
     late = jnp.concatenate(
         [
-            shares(project_grad, devices),
             jnp.concatenate(
                 [
                     side_by_side(shares(inlet_grad, devices), 3),
@@ -602,9 +672,14 @@
         ],
         axis=1,
     )
-    late = lax.psum_scatter(late, AXES, scatter_dimension=0, tiled=True)[0].astype(jnp.float32)
+    late, context_grad = lax.optimization_barrier((late, context_grad))
+    late = scatter_sums(grid, late)
+    head_grads = attend_back(mixed, context_grad, context_low, log_totals, lengths, width)
+    mixed_grad = jnp.concatenate([head_grads[0], head_grads[1], head_grads[2]], axis=-1)
+    own_project = scatter_sums(grid, shares(outer_sum(states, mixed_grad), devices))
+    input_gradient = (first_pre_grad + back_product(mixed_grad, project_full)).astype(low)
     early = early.astype(jnp.float32)
-    own_chars = late[r : 2 * r]
+    own_chars = late[:r]
     own_table_rows = side_by_side(own_chars[:, width + triple :], 3)
     own_gains = own_table_rows[0, letters_count : letters_count + 6 * r].reshape(6, r)
     spots = []
@@ -619,8 +694,8 @@
         own_table_rows[:, :letters_count].T,
         one_below_other(own_chars[:, :width], 3).T,
         one_below_other(own_chars[:, width : width + triple], 3).T,
-        late[:r],
-        one_below_other(late[2 * r :], 3),
+        own_project,
+        one_below_other(late[r:], 3),
         spots[1].reshape(merging_weight.shape),
         side_by_side(spots[2], ff_blocks),
         spots[3],
@@ -656,8 +731,9 @@
         P(AXES),
         P(AXES),
     )
+    sizes = (mesh.shape["dp"], mesh.shape["fsdp"])
     return jax.shard_map(
-        on_device,
+        functools.partial(on_device, sizes),
         mesh=mesh,
         in_specs=placed,
         out_specs=(

time: 818 us -> 539 us (0.66)
  waiting for transfers between devices: 436 us -> 110 us
  starting transfers between devices: 0.38 us -> 41.8 us
    reduce_scatter x1, waiting for transfers between devices: 200 us -> 19.2 us  [on_device(): early = lax.psum_scatter(early, AXES, scatter_dimension=0, tiled=True)[0]]
    reduce_scatter x1 -> x0, waiting for transfers between devices: 118 us -> none  [on_device(): lax.psum_scatter(late, AXES, scatter_dimension=0, tiled=True)[0]]
    ppermute x0 -> x28, waiting for transfers between devices: none -> 90.5 us  [send(): return lax.ppermute(values, AXES, pairs)]
    all_gather x1 -> x0, waiting for transfers between devices: 65.1 us -> none  [on_device(): first_all = lax.all_gather(first_rows, AXES, axis=0)]
    all_gather x1, waiting for transfers between devices: 52.8 us -> 0.02 us  [on_device(): second_all = lax.all_gather(second_rows, AXES, axis=0)]
    ppermute x0 -> x28, starting transfers between devices: none -> 41.7 us  [send(): return lax.ppermute(values, AXES, pairs)]
    unnamed x117 -> x127, local copies, waits for them, and re-layouts: 28.9 us -> 33 us
  transfers between devices with their start and end apart: 4 -> 30, of which waited for: 4 -> 12; matrix products, arithmetic and copies ran while one was open for 6% -> 18% of each run, Pallas kernels for 6% -> 24%
where the time goes in v3:
time: 539 us; the launch traced here: 533 us
  Pallas kernels  179 us (33%)
  waiting for transfers between devices  110 us (20%)
  local copies, waits for them, and re-layouts  85.4 us (16%)
  matrix products  62.5 us (12%)
  starting transfers between devices  41.8 us (8%)
  other arithmetic  39.2 us (7%)
  between operations  16 us (3%)
    ppermute x28, waiting for transfers between devices, send(): return lax.ppermute(values, AXES, pairs)  90.5 us
    pallas_call x1, Pallas kernels, feed(): pl.pallas_call(functools.partial(feed_kernel, blocks), grid=(length // ro...  51.7 us
    ppermute x28, starting transfers between devices, send(): return lax.ppermute(values, AXES, pairs)  41.7 us
    pallas_call x1, Pallas kernels, chars_back(): pl.pallas_call(functools.partial(chars_back_kernel, half), grid=(length /...  41.2 us
    pallas_call x1, Pallas kernels, attend_back(): pl.pallas_call(functools.partial(back_kernel, rows), grid=(pairs,), in_sp...  38 us
    unnamed x127, local copies, waits for them, and re-layouts  33 us
    dot_general x8, matrix products, outer_sum(): jnp.einsum('li,lo->io', left, right, preferred_element_type=jnp.float32)  30.8 us
    pallas_call x1, Pallas kernels, chars_forward(): pl.pallas_call(functools.partial(chars_kernel, half), grid=(length // row...  26.3 us
  transfers between devices with their start and end apart: 30, of which 12 were waited for; matrix products, arithmetic and copies ran while one was open for 18% of the time, Pallas kernels for 24%

profile of v3, /device:TPU:0, one launch (start us, length us, event | category | flops | bytes accessed | tf_op | source)
XLA Modules:
  0.0 533.4 jit_solution(13551532625731783255)
XLA Ops:
  50.7 20.2 %collective-permute-done.10 = bf16[4,24,2304]{2,1,0:T(8,128)(2,1)S(1)} collective-permute-done((bf16[4,24,2304]{2,1,0:T(8,128)(2,1)S(1)}, bf16[4,24,2304]{2,1,0:T(8,128)(2,1)S(1)}, u32[]{:S(2)}, u32[]{:S(2)}) %collective-permute-start.10) | collective-permute-done | bytes 442400 | tf_op jit(solution)/shard_map/ppermute | solution.py:438
  77.3 15.3 %collective-permute-done.12 = bf16[4,24,2304]{2,1,0:T(8,128)(2,1)S(1)} collective-permute-done((bf16[4,24,2304]{2,1,0:T(8,128)(2,1)S(1)}, bf16[4,24,2304]{2,1,0:T(8,128)(2,1)S(1)}, u32[]{:S(2)}, u32[]{:S(2)}) %collective-permute-start.12) | collective-permute-done | bytes 442400 | tf_op jit(solution)/shard_map/ppermute | solution.py:438
  117.6 5.6 %fusion.q_ref.k_ref.v_ref = bf16[1024,2304]{1,0:T(8,128)(2,1)} fusion(bf16[768,2304]{1,0:T(8,128)(2,1)S(1)} %bitcast.251, bf16[1,1024,768]{2,1,0:T(8,128)(2,1)S(1)} %copy-done.36), kind=kOutput, calls=%fused_computation.7 | convolution fusion | flops 3626237952 | bytes 9830400 | tf_op jit(solution)/shard_map/dot_general | solution.py:30
  123.1 21.5 %shard_map.331 = (bf16[1024,768]{1,0:T(8,128)(2,1)}, f32[1024,768]{1,0:T(8,128)}) custom-call(s32[1]{0:T(128)} %copy.185.length_ref, bf16[1024,2304]{1,0:T(8,128)(2,1)} %fusion.q_ref.k_ref.v_ref, bf16[1024,2304]{1,0:T(8,128)(2,1)} %fusion.q_ref.k_ref.v_ref, bf16[1024,2304]{1,0:T(8,128)(2,1)} %fusion.q_ref.k_ref.v_ref), custom_call_target="tpu_custom_call" | custom-call | flops 3221225472 | bytes 7864320 | tf_op jit(solution)/shard_map/pallas_call | solution.py:87
  144.6 26.3 %shard_map.332 = (bf16[1024,1024]{1,0:T(8,128)(2,1)}, bf16[1024,768]{1,0:T(8,128)(2,1)}, bf16[2,3,1024,384]{3,2,1,0:T(8,128)(2,1)}, bf16[2,17,1024,384]{3,2,1,0:T(8,128)(2,1)}) custom-call(s32[1024,4]{1,0:T(8,128)} %bitcast.274, bf16[256,1024]{1,0:T(8,128)(2,1)} %fusion.19.table_ref, bf16[2304,256]{1,0:T(8,128)(2,1)} %bitcast.270, bf16[2304,384]{1,0:T(8,128)(2,1)} %bitcast.256), custom_call_target="tpu_custom_call" | custom-call | flops 12000000000 | bytes 40000000 | tf_op jit(solution)/shard_map/pallas_call | solution.py:225
  171.0 5.3 fusion.34
  176.3 5.3 %fusion.35 = (bf16[32,48,768]{2,1,0:T(8,128)(2,1)}, bf16[32,48,768]{2,1,0:T(8,128)(2,1)S(1)}, bf16[32,48,768]{2,1,0:T(8,128)(2,1)S(1)}) fusion(bf16[32,384,768]{2,1,0:T(8,128)(2,1)} %bitcast.231), kind=kLoop, calls=%fused_computation.172 | loop fusion | bytes 14155776 | tf_op jit(solution)/shard_map/slice | solution.py:569
  181.7 6.6 %slice.479 = bf16[32,96,768]{2,1,0:T(8,128)(2,1)} slice(bf16[32,384,768]{2,1,0:T(8,128)(2,1)} %bitcast.232), slice={[0:32], [288:384], [0:768]} | slice | bytes 9437184 | tf_op jit(solution)/shard_map/slice | solution.py:569
  197.5 5.2 pad_maximum_fusion.joined_ref
  209.2 51.7 %shard_map.333 = (bf16[1024,768]{1,0:T(8,128)(2,1)}, bf16[1024,768]{1,0:T(8,128)(2,1)}, bf16[1024,768]{1,0:T(8,128)(2,1)}, bf16[1024,768]{1,0:T(8,128)(2,1)}, bf...) custom-call(bf16[1024,4608]{1,0:T(8,128)(2,1)} %pad_maximum_fusion.j, ...), custom_call_target="tpu_custom_call" | custom-call | flops 30000001024 | bytes 70000000 | tf_op jit(solution)/shard_map/pallas_call | solution.py:382
  260.9 5.1 convolution_convert_fusion.4
  274.9 5.4 %convolution_convert_fusion.2 = bf16[768,3072]{1,0:T(8,128)(2,1)S(1)} fusion(bf16[1024,768]{1,0:T(8,128)(2,1)S(1)} %copy-done.43, bf16[1024,3072]{1,0:T(8,128)(2,1)S(1)} %bitcast.300), kind=kOutput, calls=%fused_computation.5 | convolution fusion | flops 4834197504 | bytes 12582912 | tf_op jit(solution)/shard_map/li,lo->io/dot_general | solution.py:34
  289.7 5.8 %convolution_convert_fusion.1 = bf16[3072,768]{1,0:T(8,128)(2,1)S(1)} fusion(bf16[1024,3072]{1,0:T(8,128)(2,1)S(1)} %bitcast.302, bf16[1024,768]{1,0:T(8,128)(2,1)S(1)} %copy-done.44), kind=kOutput, calls=%fused_computation.4 | convolution fusion | flops 4834197504 | bytes 12582912 | tf_op jit(solution)/shard_map/li,lo->io/dot_general | solution.py:34
  305.6 5.2 add_select_fusion
  310.9 5.1 multiply_reduce_fusion
  316.6 41.2 %shard_map.334 = (bf16[256,1024]{1,0:T(8,128)(2,1)}, bf16[2304,256]{1,0:T(8,128)(2,1)}, bf16[2304,384]{1,0:T(8,128)(2,1)}) custom-call(s32[1024,4]{1,0:T(8,128)} %bitcast.275, bf16[2304,256]{1,0:T(8,128)(2,1)} %bitcast.271, bf16[2304,384]{1,0:T(8,128)(2,1)} %bitcast.257, bf16[1024,1024]{1,0:T(8,128)(2,1)} %get-tuple-element.56.embed_ref, ...), custom_call_target="tpu_custom_call" | custom-call | flops 22000001024 | bytes 40000000 | tf_op jit(solution)/shard_map/pallas_call | solution.py:301
  370.1 38.0 %shard_map.335 = bf16[3,1024,768]{2,1,0:T(8,128)(2,1)} custom-call(s32[1]{0:T(128)} %copy.185.length_ref, bf16[1024,2304]{1,0:T(8,128)(2,1)} %fusion.q_ref.k_ref.v_ref, bf16[1024,2304]{1,0:T(8,128)(2,1)} %fusion.q_ref.k_ref.v_ref, bf16[1024,2304]{1,0:T(8,128)(2,1)} %fusion.q_ref.k_ref.v_ref, bf16[1024,768]{1,0:T(8,128)(2,1)} %convolution_convert_fusion.7.do_ref, ...), custom_call_target="tpu_custom_call" | custom-call | flops 8053063680 | bytes 15728640 | tf_op jit(solution)/shard_map/pallas_call | solution.py:140
  410.9 5.3 convolution_convert_fusion.3
  418.9 9.3 %fusion.4 = bf16[1,1024,768]{2,1,0:T(8,128)(2,1)} fusion(f32[1024,768]{1,0:T(8,128)} %copy-done.17, f32[1024]{0:T(1024)S(1)} %negate_multiply_fusion, bf16[768,2304]{1,0:T(8,128)(2,1)} %bitcast.252, bf16[1024,768]{1,0:T(8,128)(2,1)} %copy-done.22, bf16[1024,768]{1,0:T(8,128)(2,1)} %copy-done.23, bf16[1024,768]{1,0:T(8,128)(2,1)} %copy-done.21), kind=kOutput, calls=%fused_computation.39 | convolution fusion | flops 3640393728 | bytes 12980224 | tf_op jit(solution)/shard_map/lo,io->li/dot_general | solution.py:38
  439.4 9.9 %collective-permute-done.22 = bf16[4,24,2304]{2,1,0:T(8,128)(2,1)S(1)} collective-permute-done((bf16[4,24,2304]{2,1,0:T(8,128)(2,1)S(1)}, bf16[4,24,2304]{2,1,0:T(8,128)(2,1)S(1)}, u32[]{:S(2)}, u32[]{:S(2)}) %collective-permute-start.22) | collective-permute-done | bytes 442400 | tf_op jit(solution)/shard_map/ppermute | solution.py:438
  452.5 9.9 %collective-permute-done.24 = bf16[4,24,2304]{2,1,0:T(8,128)(2,1)S(1)} collective-permute-done((bf16[4,24,2304]{2,1,0:T(8,128)(2,1)S(1)}, bf16[4,24,2304]{2,1,0:T(8,128)(2,1)S(1)}, u32[]{:S(2)}, u32[]{:S(2)}) %collective-permute-start.24) | collective-permute-done | bytes 442400 | tf_op jit(solution)/shard_map/ppermute | solution.py:438
  464.7 7.9 %collective-permute-done.15 = bf16[4,32,2304]{2,1,0:T(8,128)(2,1)S(1)} collective-permute-done((bf16[4,32,2304]{2,1,0:T(8,128)(2,1)S(1)}, bf16[4,32,2304]{2,1,0:T(8,128)(2,1)S(1)}, u32[]{:S(2)}, u32[]{:S(2)}) %collective-permute-start.15) | collective-permute-done | bytes 589856 | tf_op jit(solution)/shard_map/ppermute | solution.py:438
  475.0 11.4 %collective-permute-done.17 = bf16[4,32,2304]{2,1,0:T(8,128)(2,1)S(1)} collective-permute-done((bf16[4,32,2304]{2,1,0:T(8,128)(2,1)S(1)}, bf16[4,32,2304]{2,1,0:T(8,128)(2,1)S(1)}, u32[]{:S(2)}, u32[]{:S(2)}) %collective-permute-start.17) | collective-permute-done | bytes 589856 | tf_op jit(solution)/shard_map/ppermute | solution.py:438
  503.0 19.2 %reduce-scatter.2.cloned.1.call-done = bf16[1,360,768]{2,1,0:T(8,128)(2,1)} async-done(((bf16[32,360,768]{2,1,0:T(8,128)(2,1)}), bf16[1,360,768]{2,1,0:T(8,128)(2,1)}) %reduce-scatter.2.cloned.1.call-update) | async-done | bytes 552976 | tf_op jit(solution)/shard_map/reduce_scatter | solution.py:626
  (295 shorter events, 175.7 us)
Async XLA Ops:
  7.2 163.8 %all-gather.3.cloned.1.call-start = ((), (), s32[]{:S(2)}) async-start(), calls=%async_computation.2 | async-start | bytes 19464192 | tf_op jit(solution)/shard_map/all_gather | solution.py:540
  14.6 507.6 %reduce-scatter.2.cloned.1.call-start = ((), (), s32[]{:S(2)}) async-start(), calls=%async_computation.1 | async-start | bytes 18247680 | tf_op jit(solution)/shard_map/reduce_scatter | solution.py:626
  14.6 17.9 %collective-permute-start = (bf16[24,2304]{1,0:T(8,128)(2,1)}, bf16[24,2304]{1,0:T(8,128)(2,1)S(1)}, u32[]{:S(2)}, u32[]{:S(2)}) collective-permute-start(bf16[24,2304]{1,0:T(8,128)(2,1)} %param.28), channel_id=1, source_target_pairs={{0,8},{1,9},{2,10},{3,11},{4,12},{5,13},{6,14},{7,15},{8,16},{9,17... | collective-permute-start | bytes 331784 | tf_op jit(solution)/shard_map/ppermute | solution.py:438
  17.7 17.7 %collective-permute-start.1 = (bf16[24,2304]{1,0:T(8,128)(2,1)}, bf16[24,2304]{1,0:T(8,128)(2,1)S(1)}, u32[]{:S(2)}, u32[]{:S(2)}) collective-permute-start(bf16[24,2304]{1,0:T(8,128)(2,1)} %param.28), channel_id=1, source_target_pairs={{0,16},{1,17},{2,18},{3,19},{4,20},{5,21},{6,22},{7,23},{8,24},{9,... | collective-permute-start | bytes 331784 | tf_op jit(solution)/shard_map/ppermute | solution.py:438
  20.3 15.1 %collective-permute-start.2 = (bf16[24,2304]{1,0:T(8,128)(2,1)}, bf16[24,2304]{1,0:T(8,128)(2,1)S(1)}, u32[]{:S(2)}, u32[]{:S(2)}) collective-permute-start(bf16[24,2304]{1,0:T(8,128)(2,1)} %param.28), channel_id=1, source_target_pairs={{0,24},{1,25},{2,26},{3,27},{4,28},{5,29},{6,30},{7,31},{8,0},{9,1... | collective-permute-start | bytes 331784 | tf_op jit(solution)/shard_map/ppermute | solution.py:438
  29.1 16.2 %collective-permute-start.8 = (bf16[24,2304]{1,0:T(8,128)(2,1)S(1)}, bf16[24,2304]{1,0:T(8,128)(2,1)S(1)}, u32[]{:S(2)}, u32[]{:S(2)}) collective-permute-start(bf16[24,2304]{1,0:T(8,128)(2,1)S(1)} %constant_dynamic-update-slice_fusion.8), channel_id=1, source_target_pairs={{0,16},{1,17},{2,18},{3,19},{4,20},{5,21},{6,22},{7,23},{8,24},{9,... | collective-permute-start | bytes 331784 | tf_op jit(solution)/shard_map/ppermute | solution.py:438
  32.5 12.7 %collective-permute-start.9 = (bf16[24,2304]{1,0:T(8,128)(2,1)S(1)}, bf16[24,2304]{1,0:T(8,128)(2,1)S(1)}, u32[]{:S(2)}, u32[]{:S(2)}) collective-permute-start(bf16[24,2304]{1,0:T(8,128)(2,1)S(1)} %constant_dynamic-update-slice_fusion.8), channel_id=1, source_target_pairs={{0,24},{1,25},{2,26},{3,27},{4,28},{5,29},{6,30},{7,31},{8,0},{9,1... | collective-permute-start | bytes 331784 | tf_op jit(solution)/shard_map/ppermute | solution.py:438
  35.4 57.2 %collective-permute-start.3 = (bf16[4,24,2304]{2,1,0:T(8,128)(2,1)S(1)}, bf16[4,24,2304]{2,1,0:T(8,128)(2,1)S(1)}, u32[]{:S(2)}, u32[]{:S(2)}) collective-permute-start(bf16[4,24,2304]{2,1,0:T(8,128)(2,1)S(1)} %bitcast_dynamic-update-slice_fusion.16), channel_id=1, source_target_pairs={{0,2},{1,3},{2,0},{3,1},{4,6},{5,7},{6,4},{7,5},{8,10},{9,11},{10,... | collective-permute-start | bytes 1327112 | tf_op jit(solution)/shard_map/ppermute | solution.py:438
  37.0 56.5 %collective-permute-start.4 = (bf16[4,24,2304]{2,1,0:T(8,128)(2,1)S(1)}, bf16[4,24,2304]{2,1,0:T(8,128)(2,1)S(1)}, u32[]{:S(2)}, u32[]{:S(2)}) collective-permute-start(bf16[4,24,2304]{2,1,0:T(8,128)(2,1)S(1)} %bitcast_dynamic-update-slice_fusion.16), channel_id=1, source_target_pairs={{0,4},{1,5},{2,6},{3,7},{4,0},{5,1},{6,2},{7,3},{8,12},{9,13},{10,... | collective-permute-start | bytes 1327112 | tf_op jit(solution)/shard_map/ppermute | solution.py:438
  38.5 55.8 %collective-permute-start.5 = (bf16[4,24,2304]{2,1,0:T(8,128)(2,1)S(1)}, bf16[4,24,2304]{2,1,0:T(8,128)(2,1)S(1)}, u32[]{:S(2)}, u32[]{:S(2)}) collective-permute-start(bf16[4,24,2304]{2,1,0:T(8,128)(2,1)S(1)} %bitcast_dynamic-update-slice_fusion.16), channel_id=1, source_target_pairs={{0,6},{1,7},{2,4},{3,5},{4,2},{5,3},{6,0},{7,1},{8,14},{9,15},{10,... | collective-permute-start | bytes 1327112 | tf_op jit(solution)/shard_map/ppermute | solution.py:438
  45.3 25.7 %collective-permute-start.10 = (bf16[4,24,2304]{2,1,0:T(8,128)(2,1)S(1)}, bf16[4,24,2304]{2,1,0:T(8,128)(2,1)S(1)}, u32[]{:S(2)}, u32[]{:S(2)}) collective-permute-start(bf16[4,24,2304]{2,1,0:T(8,128)(2,1)S(1)} %bitcast_dynamic-update-slice_fusion.12), channel_id=1, source_target_pairs={{0,2},{1,3},{2,0},{3,1},{4,6},{5,7},{6,4},{7,5},{8,10},{9,11},{10,... | collective-permute-start | bytes 1327112 | tf_op jit(solution)/shard_map/ppermute | solution.py:438
  46.9 30.3 %collective-permute-start.11 = (bf16[4,24,2304]{2,1,0:T(8,128)(2,1)S(1)}, bf16[4,24,2304]{2,1,0:T(8,128)(2,1)S(1)}, u32[]{:S(2)}, u32[]{:S(2)}) collective-permute-start(bf16[4,24,2304]{2,1,0:T(8,128)(2,1)S(1)} %bitcast_dynamic-update-slice_fusion.12), channel_id=1, source_target_pairs={{0,4},{1,5},{2,6},{3,7},{4,0},{5,1},{6,2},{7,3},{8,12},{9,13},{10,... | collective-permute-start | bytes 1327112 | tf_op jit(solution)/shard_map/ppermute | solution.py:438
  71.0 21.6 %collective-permute-start.12 = (bf16[4,24,2304]{2,1,0:T(8,128)(2,1)S(1)}, bf16[4,24,2304]{2,1,0:T(8,128)(2,1)S(1)}, u32[]{:S(2)}, u32[]{:S(2)}) collective-permute-start(bf16[4,24,2304]{2,1,0:T(8,128)(2,1)S(1)} %bitcast_dynamic-update-slice_fusion.12), channel_id=1, source_target_pairs={{0,6},{1,7},{2,4},{3,5},{4,2},{5,3},{6,0},{7,1},{8,14},{9,15},{10,... | collective-permute-start | bytes 1327112 | tf_op jit(solution)/shard_map/ppermute | solution.py:438
  95.1 17.7 %collective-permute-start.6 = (bf16[4,2,2,24,2304]{4,3,2,1,0:T(8,128)(2,1)}, bf16[4,2,2,24,2304]{4,3,2,1,0:T(8,128)(2,1)}, u32[]{:S(2)}, u32[]{:S(2)}) collective-permute-start(bf16[4,2,2,24,2304]{4,3,2,1,0:T(8,128)(2,1)} %bitcast_dynamic-update-slice_fusion.11), channel_id=1, source_target_pairs={{0,1},{1,0},{2,3},{3,2},{4,5},{5,4},{6,7},{7,6},{8,9},{9,8},{10,11... | collective-permute-start | bytes 5308424 | tf_op jit(solution)/shard_map/ppermute | solution.py:438
  418.4 15.5 %collective-permute-start.14 = (bf16[4,2,2,32,2304]{4,3,2,1,0:T(8,128)(2,1)}, bf16[4,2,2,32,2304]{4,3,2,1,0:T(8,128)(2,1)}, u32[]{:S(2)}, u32[]{:S(2)}) collective-permute-start(bf16[4,2,2,32,2304]{4,3,2,1,0:T(8,128)(2,1)} %dynamic-slice_bitcast_fusion), channel_id=1, source_target_pairs={{0,1},{1,0},{2,3},{3,2},{4,5},{5,4},{6,7},{7,6},{8,9},{9,8},{10,11... | collective-permute-start | bytes 7077896 | tf_op jit(solution)/shard_map/ppermute | solution.py:438
  430.3 19.0 %collective-permute-start.22 = (bf16[4,24,2304]{2,1,0:T(8,128)(2,1)S(1)}, bf16[4,24,2304]{2,1,0:T(8,128)(2,1)S(1)}, u32[]{:S(2)}, u32[]{:S(2)}) collective-permute-start(bf16[4,24,2304]{2,1,0:T(8,128)(2,1)S(1)} %get-tuple-element.105), channel_id=1, source_target_pairs={{0,2},{1,3},{2,0},{3,1},{4,6},{5,7},{6,4},{7,5},{8,10},{9,11},{10,... | collective-permute-start | bytes 1327112 | tf_op jit(solution)/shard_map/ppermute | solution.py:438
  431.9 20.5 %collective-permute-start.23 = (bf16[4,24,2304]{2,1,0:T(8,128)(2,1)S(1)}, bf16[4,24,2304]{2,1,0:T(8,128)(2,1)S(1)}, u32[]{:S(2)}, u32[]{:S(2)}) collective-permute-start(bf16[4,24,2304]{2,1,0:T(8,128)(2,1)S(1)} %get-tuple-element.107), channel_id=1, source_target_pairs={{0,4},{1,5},{2,6},{3,7},{4,0},{5,1},{6,2},{7,3},{8,12},{9,13},{10,... | collective-permute-start | bytes 1327112 | tf_op jit(solution)/shard_map/ppermute | solution.py:438
  433.5 28.9 %collective-permute-start.24 = (bf16[4,24,2304]{2,1,0:T(8,128)(2,1)S(1)}, bf16[4,24,2304]{2,1,0:T(8,128)(2,1)S(1)}, u32[]{:S(2)}, u32[]{:S(2)}) collective-permute-start(bf16[4,24,2304]{2,1,0:T(8,128)(2,1)S(1)} %get-tuple-element.106), channel_id=1, source_target_pairs={{0,6},{1,7},{2,4},{3,5},{4,2},{5,3},{6,0},{7,1},{8,14},{9,15},{10,... | collective-permute-start | bytes 1327112 | tf_op jit(solution)/shard_map/ppermute | solution.py:438
  436.3 36.3 %collective-permute-start.15 = (bf16[4,32,2304]{2,1,0:T(8,128)(2,1)S(1)}, bf16[4,32,2304]{2,1,0:T(8,128)(2,1)S(1)}, u32[]{:S(2)}, u32[]{:S(2)}) collective-permute-start(bf16[4,32,2304]{2,1,0:T(8,128)(2,1)S(1)} %get-tuple-element.102), channel_id=1, source_target_pairs={{0,2},{1,3},{2,0},{3,1},{4,6},{5,7},{6,4},{7,5},{8,10},{9,11},{10,... | collective-permute-start | bytes 1769480 | tf_op jit(solution)/shard_map/ppermute | solution.py:438
  437.9 37.1 %collective-permute-start.16 = (bf16[4,32,2304]{2,1,0:T(8,128)(2,1)S(1)}, bf16[4,32,2304]{2,1,0:T(8,128)(2,1)S(1)}, u32[]{:S(2)}, u32[]{:S(2)}) collective-permute-start(bf16[4,32,2304]{2,1,0:T(8,128)(2,1)S(1)} %get-tuple-element.104), channel_id=1, source_target_pairs={{0,4},{1,5},{2,6},{3,7},{4,0},{5,1},{6,2},{7,3},{8,12},{9,13},{10,... | collective-permute-start | bytes 1769480 | tf_op jit(solution)/shard_map/ppermute | solution.py:438
  449.3 37.1 %collective-permute-start.17 = (bf16[4,32,2304]{2,1,0:T(8,128)(2,1)S(1)}, bf16[4,32,2304]{2,1,0:T(8,128)(2,1)S(1)}, u32[]{:S(2)}, u32[]{:S(2)}) collective-permute-start(bf16[4,32,2304]{2,1,0:T(8,128)(2,1)S(1)} %get-tuple-element.103), channel_id=1, source_target_pairs={{0,6},{1,7},{2,4},{3,5},{4,2},{5,3},{6,0},{7,1},{8,14},{9,15},{10,... | collective-permute-start | bytes 1769480 | tf_op jit(solution)/shard_map/ppermute | solution.py:438
  462.6 26.3 %collective-permute-start.25 = (bf16[24,2304]{1,0:T(8,128)(2,1)S(1)}, bf16[24,2304]{1,0:T(8,128)(2,1)S(1)}, u32[]{:S(2)}, u32[]{:S(2)}) collective-permute-start(bf16[24,2304]{1,0:T(8,128)(2,1)S(1)} %get-tuple-element.121), channel_id=1, source_target_pairs={{0,8},{1,9},{2,10},{3,11},{4,12},{5,13},{6,14},{7,15},{8,16},{9,17... | collective-permute-start | bytes 331784 | tf_op jit(solution)/shard_map/ppermute | solution.py:438
  463.2 28.3 %collective-permute-start.26 = (bf16[24,2304]{1,0:T(8,128)(2,1)S(1)}, bf16[24,2304]{1,0:T(8,128)(2,1)S(1)}, u32[]{:S(2)}, u32[]{:S(2)}) collective-permute-start(bf16[24,2304]{1,0:T(8,128)(2,1)S(1)} %get-tuple-element.123), channel_id=1, source_target_pairs={{0,16},{1,17},{2,18},{3,19},{4,20},{5,21},{6,22},{7,23},{8,24},{9,... | collective-permute-start | bytes 331784 | tf_op jit(solution)/shard_map/ppermute | solution.py:438
  472.6 18.9 %collective-permute-start.27 = (bf16[24,2304]{1,0:T(8,128)(2,1)S(1)}, bf16[24,2304]{1,0:T(8,128)(2,1)S(1)}, u32[]{:S(2)}, u32[]{:S(2)}) collective-permute-start(bf16[24,2304]{1,0:T(8,128)(2,1)S(1)} %get-tuple-element.122), channel_id=1, source_target_pairs={{0,24},{1,25},{2,26},{3,27},{4,28},{5,29},{6,30},{7,31},{8,0},{9,1... | collective-permute-start | bytes 331784 | tf_op jit(solution)/shard_map/ppermute | solution.py:438
  (55 other events, 350.5 us)
Sparse Core Ops, SparseCore 0:
  14.7 150.4 all-gather.2
  298.1 224.0 reduce-scatter.1

commit v4 on v3

--- a/solution.py
+++ b/solution.py
@@ -18,13 +18,7 @@
 SCALE2 = math.log2(math.e) / math.sqrt(HEAD_DIM)
 AXES = ("dp", "fsdp")
 VMEM_LIMIT = 56 * 1024 * 1024
-
-def norm_apply(values, gain, shift):
-    average = jnp.mean(values, axis=-1, keepdims=True)
-    centred = values - average
-    variance = jnp.mean(centred * centred, axis=-1, keepdims=True)
-    return centred * lax.rsqrt(variance + EPS) * gain + shift
-
+BRIEF = pl.CostEstimate(flops=200 * 10**9, bytes_accessed=10**6, transcendentals=0)
 
 def product(left, right):
     return jnp.dot(left, right, preferred_element_type=jnp.float32)
@@ -36,14 +30,6 @@
 
 def back_product(grad_rows, weight):
     return jnp.einsum("lo,io->li", grad_rows, weight, preferred_element_type=jnp.float32)
-
-
-def shift_down(values):
-    return jnp.pad(values[:-1], ((1, 0), (0, 0)))
-
-
-def shift_up(values):
-    return jnp.pad(values[1:], ((0, 1), (0, 0)))
 
 
 def dotf(a,b,ca=1,cb=0):
@@ -92,10 +78,11 @@
         out_shape=[jax.ShapeDtypeStruct((length, width), jnp.bfloat16), jax.ShapeDtypeStruct((length, width), jnp.float32)],
         scratch_shapes=[pltpu.VMEM((length, 2*LANES), jnp.bfloat16), pltpu.VMEM((length, 2*LANES), jnp.bfloat16)],
         compiler_params=pltpu.CompilerParams(vmem_limit_bytes=VMEM_LIMIT),
-        cost_estimate=pl.CostEstimate(flops=4*12*length*length*64, bytes_accessed=10*length*width, transcendentals=12*length*length),
+        cost_estimate=BRIEF,
     )(lengths, mixed, mixed, mixed)
 
-def back_kernel(rows, length_ref, q_ref, k_ref, v_ref, do_ref, o_ref, lse_ref, out_ref, kx_ref, vx_ref, qt_ref, dot_ref, dk_ref, dv_ref):
+def back_kernel(rows, length_ref, q_ref, k_ref, v_ref, do_ref, o_ref, lse_ref, *rest):
+    dq_ref, dk_out, dv_out, kx_ref, qt_ref, dot_ref, dk_ref, dv_ref = rest[-8:]
     length = k_ref.shape[0]
     lane = lax.broadcasted_iota(jnp.int32, (length, LANES), 1)
     place = lax.broadcasted_iota(jnp.int32, (length, LANES), 0)
@@ -127,28 +114,38 @@
             dqs.append(dotf(ds, k_ref[...]))
             dk_ref[hs, :] += dotf(qt_ref[hs, at], ds)
             dv_ref[hs, :] += dotf(dot_ref[hs, at], pb)
-        out_ref[0, at, :] = (jnp.where(low, dqs[0], dqs[1]) * SCALE).astype(jnp.bfloat16)
+        dq_ref[at, :] = (jnp.where(low, dqs[0], dqs[1]) * SCALE).astype(jnp.bfloat16)
         return 0
     lax.fori_loop(0, length // rows, step, 0, unroll=True)
-    out_ref[1] = (dk_ref[...] * SCALE).T.astype(jnp.bfloat16)
-    out_ref[2] = dv_ref[...].T.astype(jnp.bfloat16)
-
-def attend_back(mixed, context_grad, context, log_totals, lengths, width, rows=256):
+    dk_out[...] = (dk_ref[...] * SCALE).T.astype(jnp.bfloat16)
+    dv_out[...] = dv_ref[...].T.astype(jnp.bfloat16)
+
+def attend_back(
+    mixed, context_grad, context, log_totals, lengths, width, start, pairs, earlier, rows=256
+):
     length = mixed.shape[0]
-    pairs = width // LANES
-    spec = lambda o: pl.BlockSpec((length, LANES), lambda p, o=o: (0, p+o))
+    every = width // LANES
+    spec = lambda o: pl.BlockSpec((length, LANES), lambda p, o=o: (0, p + o + start))
+    scratch = lambda a, b, t: pltpu.VMEM((a, b), t)
     return pl.pallas_call(
         functools.partial(back_kernel, rows),
         grid=(pairs,),
-        in_specs=[pl.BlockSpec(memory_space=pltpu.SMEM), spec(0), spec(pairs), spec(2 * pairs), spec(0), spec(0), spec(0)],
-        out_specs=pl.BlockSpec((3, length, LANES), lambda p: (0, 0, p)),
-        out_shape=jax.ShapeDtypeStruct((3, length, width), jnp.bfloat16),
-        scratch_shapes=[pltpu.VMEM((length, 2*LANES), jnp.bfloat16), pltpu.VMEM((length, 2*LANES), jnp.bfloat16),
-            pltpu.VMEM((LANES, length), jnp.bfloat16), pltpu.VMEM((LANES, length), jnp.bfloat16),
-            pltpu.VMEM((LANES, length), jnp.float32), pltpu.VMEM((LANES, length), jnp.float32)],
+        in_specs=[pl.BlockSpec(memory_space=pltpu.SMEM), spec(0), spec(every), spec(2 * every)]
+        + [spec(0)] * 3
+        + [pl.BlockSpec(memory_space=pl.ANY)] * len(earlier),
+        out_specs=[spec(0)] * 3,
+        out_shape=[jax.ShapeDtypeStruct((length, width), jnp.bfloat16)] * 3,
+        input_output_aliases={7 + i: i for i in range(len(earlier))},
+        scratch_shapes=[
+            scratch(length, 2 * LANES, jnp.bfloat16),
+            scratch(LANES, length, jnp.bfloat16),
+            scratch(LANES, length, jnp.bfloat16),
+            scratch(LANES, length, jnp.float32),
+            scratch(LANES, length, jnp.float32),
+        ],
         compiler_params=pltpu.CompilerParams(vmem_limit_bytes=VMEM_LIMIT),
-        cost_estimate=pl.CostEstimate(flops=10*12*length*length*64, bytes_accessed=20*length*width, transcendentals=12*length*length),
-    )(lengths, mixed, mixed, mixed, context_grad, context, log_totals)
+        cost_estimate=BRIEF,
+    )(lengths, mixed, mixed, mixed, context_grad, context, log_totals, *earlier)
 
 
 ROOT_HALF = math.sqrt(0.5)
@@ -239,7 +236,7 @@
             jax.ShapeDtypeStruct((2, COEFS, length, half), low),
         ],
         compiler_params=pltpu.CompilerParams(vmem_limit_bytes=VMEM_LIMIT),
-        cost_estimate=pl.CostEstimate(flops=12 * 10**9, bytes_accessed=40 * 10**6, transcendentals=10**7),
+        cost_estimate=BRIEF,
     )(codes, table, inlet, recur)
 
 def chars_back_kernel(half, codes_ref, inlet_ref, recur_ref, embed_ref, states_ref, coef_ref, grad_ref,
@@ -314,22 +311,52 @@
             pltpu.VMEM((CHARS * rows, 6 * half), low), pltpu.VMEM((CHARS * rows, letters), low),
             ] + [pltpu.VMEM(s, jnp.float32) for s in outs],
         compiler_params=pltpu.CompilerParams(vmem_limit_bytes=VMEM_LIMIT),
-        cost_estimate=pl.CostEstimate(flops=22 * 10**9, bytes_accessed=40 * 10**6, transcendentals=0),
+        cost_estimate=BRIEF,
     )(codes, inlet, recur, embeds, states, coefs, grad)
 
+def flat(ref, part=0, parts=1):
+    count = ref.shape[0] // parts
+    block = ref[part * count : (part + 1) * count]
+    return block.reshape(-1, block.shape[-1])
+
+
+PAD = 8
+
+
+def spread_rows(rows_ref, wide_ref):
+    length, width = rows_ref.shape
+    blank = jnp.zeros((PAD, width), jnp.float32)
+    wide_ref[:PAD] = blank
+    wide_ref[PAD + length :] = blank
+    for start in range(0, length, 256):
+        block = rows_ref[start : start + 256]
+        wide_ref[PAD + start : PAD + start + block.shape[0]] = block.astype(jnp.float32)
+
+
+def neighbours(wide_ref, rows):
+    base = pl.multiple_of(pl.program_id(0) * rows, rows)
+    window = wide_ref[pl.ds(base, rows + 2 * PAD)]
+    return [window[PAD + i : PAD + i + rows].astype(jnp.bfloat16) for i in (-1, 0, 1)]
+
+
 def feed_kernel(blocks, joined_ref, first_ref, rep_ref, token_cot_ref, char_cot_ref, gains_ref,
-                merging_ref, up_ref, down_ref, branch_ref,
+                up_ref, branch_ref, tap0_ref, tap1_ref, tap2_ref, down_ref,
                 token_ref, char_ref, summed_ref, merged_ref, hidden_ref, feed_grad_ref, hidden_grad_ref,
-                branch_grad_ref, merging_grad_ref, summed_grad_ref, char_grad_ref, sums_ref, slope_ref):
+                branch_grad_ref, merging_grad_ref, summed_grad_ref, char_grad_ref, sums_ref, slope_ref, wide_ref):
     low = jnp.bfloat16
     width = first_ref.shape[1]
     step = up_ref.shape[1] // blocks
+    merging_refs = (tap0_ref, tap1_ref, tap2_ref)
 
     @pl.when(pl.program_id(0) == 0)
     def _():
         sums_ref[...] = jnp.zeros_like(sums_ref)
-
-    merged, merging_slope = gelu_both(dotf(joined_ref[...], merging_ref[...]))
+        spread_rows(joined_ref, wide_ref)
+
+    merging_pre = 0.0
+    for moved, ref in zip(neighbours(wide_ref, first_ref.shape[0]), merging_refs):
+        merging_pre = merging_pre + dotf(moved, flat(ref))
+    merged, merging_slope = gelu_both(merging_pre)
     merged_low = merged.astype(low)
     merged_ref[...] = merged_low
     summed = first_ref[...] + merged
@@ -342,7 +369,7 @@
         slope_ref[:, cols] = slope
         hidden_low = hidden.astype(low)
         hidden_ref[:, cols] = hidden_low
-        total = total + dotf(hidden_low, down_ref[cols, :])
+        total = total + dotf(hidden_low, flat(down_ref, c, blocks))
     normed, spread = norm_parts(total)
     gain, shift = gains_ref[2:3, :], gains_ref[3:4, :]
     token_ref[...] = (normed * gain + shift).astype(low)
@@ -355,7 +382,7 @@
     total = token_grad
     for c in range(blocks):
         cols = slice(c * step, (c + 1) * step)
-        hidden_grad = (slope_ref[:, cols] * dotf(feed_grad, down_ref[cols, :], 1, 1)).astype(low)
+        hidden_grad = (slope_ref[:, cols] * dotf(feed_grad, flat(down_ref, c, blocks), 1, 1)).astype(low)
         hidden_grad_ref[:, cols] = hidden_grad
         total = total + dotf(hidden_grad, up_ref[:, cols], 1, 1)
     summed_grad_ref[...] = total
@@ -371,25 +398,73 @@
     branch_grad_ref[...] = branch_grad
     merging_grad_ref[...] = (merging_slope * (total + dotf(branch_grad, branch_ref[...], 1, 1))).astype(low)
 
-def feed(joined, first, rep, token_cot, char_cot, gains, merging, up, down, branch, rows=256, blocks=2):
+def feed(joined, first, rep, token_cot, char_cot, gains, up, branch, merging, down, rows=256, blocks=2):
     length, width = first.shape
     ff = up.shape[1]
     low, wide = jnp.bfloat16, jnp.float32
     row = lambda w: pl.BlockSpec((rows, w), lambda b: (b, 0))
-    full = lambda a: pl.BlockSpec(a.shape, lambda b: (0, 0), pipeline_mode=pl.Buffered(1))
+    full = lambda a: pl.BlockSpec(a.shape, lambda b: (0,) * a.ndim, pipeline_mode=pl.Buffered(1))
     outs = [(width, low), (width, low), (width, low), (width, low), (ff, low), (width, low), (ff, low),
             (width, low), (width, low), (width, wide), (width, wide)]
     return pl.pallas_call(
         functools.partial(feed_kernel, blocks),
         grid=(length // rows,),
-        in_specs=[row(joined.shape[1]), row(width), row(width), row(width), row(width), full(gains),
-                  full(merging), full(up), full(down), full(branch)],
+        in_specs=[full(joined), row(width), row(width), row(width), row(width), full(gains),
+                  full(up), full(branch)] + [spec for _, spec in merging + [down]],
         out_specs=[row(w) for w, _ in outs] + [pl.BlockSpec((4, 8, width), lambda b: (0, 0, 0))],
         out_shape=[jax.ShapeDtypeStruct((length, w), t) for w, t in outs] + [jax.ShapeDtypeStruct((4, 8, width), wide)],
-        scratch_shapes=[pltpu.VMEM((rows, ff), wide)],
+        scratch_shapes=[pltpu.VMEM((rows, ff), wide), pltpu.VMEM((length + 2 * PAD, joined.shape[1]), wide)],
         compiler_params=pltpu.CompilerParams(vmem_limit_bytes=VMEM_LIMIT),
-        cost_estimate=pl.CostEstimate(flops=30 * 10**9, bytes_accessed=70 * 10**6, transcendentals=10**7),
-    )(joined, first, rep, token_cot, char_cot, gains, merging, up, down, branch)
+        cost_estimate=BRIEF,
+    )(joined, first, rep, token_cot, char_cot, gains, up, branch, *[part for part, _ in merging + [down]])
+
+
+def merging_back_kernel(length_ref, grad_ref, summed_ref, char_ref, pre_ref, gains_ref, output_ref,
+                        tap0_ref, tap1_ref, tap2_ref,
+                        pre_grad_ref, attended_ref, context_ref, rep_ref, sums_ref, wide_ref):
+    rows, width = pre_ref.shape
+    low = jnp.bfloat16
+
+    @pl.when(pl.program_id(0) == 0)
+    def _():
+        sums_ref[...] = jnp.zeros_like(sums_ref)
+        spread_rows(grad_ref, wide_ref)
+
+    joined = 0.0
+    for moved, ref in zip(neighbours(wide_ref, rows), (tap2_ref, tap1_ref, tap0_ref)):
+        joined = joined + dotf(moved, flat(ref), 1, 1)
+    place = pl.program_id(0) * rows + lax.broadcasted_iota(jnp.int32, (rows, 1), 0)
+    joined = jnp.where(place < length_ref[0], joined, 0.0)
+    rep_ref[...] = char_ref[...] + joined[:, width:]
+    first_grad = summed_ref[...] + joined[:, :width]
+    normed, spread = norm_parts(pre_ref[...])
+    sums_ref[0] += column_sums(first_grad * normed)
+    sums_ref[1] += column_sums(first_grad)
+    pre_grad = norm_back(normed, spread, first_grad * gains_ref[0:1, :])
+    pre_grad_ref[...] = pre_grad
+    attended = pre_grad.astype(low)
+    attended_ref[...] = attended
+    context_ref[...] = dotf(attended, output_ref[...], 1, 1).astype(low)
+
+
+def merging_back(lengths, grad, summed_grad, char_grad, pre, gains, output, merging, rows=256):
+    length, width = pre.shape
+    low, wide = jnp.bfloat16, jnp.float32
+    row = pl.BlockSpec((rows, width), lambda b: (b, 0))
+    full = lambda a: pl.BlockSpec(a.shape, lambda b: (0, 0), pipeline_mode=pl.Buffered(1))
+    kinds = (wide, low, low, wide)
+    return pl.pallas_call(
+        merging_back_kernel,
+        grid=(length // rows,),
+        in_specs=[pl.BlockSpec(memory_space=pltpu.SMEM), full(grad), row, row, row, full(gains), full(output)]
+        + [spec for _, spec in merging],
+        out_specs=[row] * 4 + [pl.BlockSpec((2, 8, width), lambda b: (0, 0, 0))],
+        out_shape=[jax.ShapeDtypeStruct((length, width), t) for t in kinds]
+        + [jax.ShapeDtypeStruct((2, 8, width), wide)],
+        scratch_shapes=[pltpu.VMEM((length + 2 * PAD, width), wide)],
+        compiler_params=pltpu.CompilerParams(vmem_limit_bytes=VMEM_LIMIT),
+        cost_estimate=BRIEF,
+    )(lengths, grad, summed_grad, char_grad, pre, gains, output, *[part for part, _ in merging])
 
 
 def side_by_side(rows, groups):
@@ -442,56 +517,93 @@
         return [(i, j) for i in range(x) for j in range(y) if i or j]
 
 
-def gather_rows(grid, part):
-    nz, nx, ny, ncore = grid.shape
-    z, x, y, core = grid.own()
-    put = lax.dynamic_update_slice
-    rows, width = part.shape
-    column = jnp.zeros((nz, rows, width), part.dtype)
-    column = put(column, part[None], (z, 0, 0))
+def column_sends(grid, part):
+    return [grid.send(part, (s, 0, 0, 0)) for s in range(1, grid.shape[0])]
+
+
+def column_of(grid, part, came):
+    nz = grid.shape[0]
+    z = grid.own()[0]
+    column = jnp.zeros((nz,) + part.shape, part.dtype)
+    for s, piece in enumerate([part] + came):
+        column = lax.dynamic_update_slice(column, piece[None], ((z - s) % nz, 0, 0))
+    return column
+
+
+def plane_sends(grid, column):
+    return [grid.send(column, (0, i, j, 0)) for i, j in grid.plane()]
+
+
+def plane_of(grid, column, came):
+    nz, nx, ny, _ = grid.shape
+    _, x, y, _ = grid.own()
+    layer = jnp.zeros((nz, nx, ny) + column.shape[1:], column.dtype)
+    for (i, j), piece in zip([(0, 0)] + grid.plane(), [column] + came):
+        layer = lax.dynamic_update_slice(
+            layer, piece[:, None, None], (0, (x - i) % nx, (y - j) % ny, 0, 0)
+        )
+    return layer
+
+
+def cores_sends(grid, layer):
+    return [grid.send(layer, (0, 0, 0, s)) for s in range(1, grid.shape[3])]
+
+
+def cores_of(grid, layer, came):
+    ncore = grid.shape[3]
+    core = grid.own()[3]
+    full = jnp.zeros(grid.shape + layer.shape[3:], layer.dtype)
+    for s, piece in enumerate([layer] + came):
+        full = lax.dynamic_update_slice(
+            full, piece[:, :, :, None], (0, 0, 0, (core - s) % ncore, 0, 0)
+        )
+    return full.reshape(-1, layer.shape[-1])
+
+
+def core_terms(grid, parts):
+    ncore = grid.shape[3]
+    core = grid.own()[3]
+    parts = parts.reshape(grid.shape + parts.shape[1:])
+    terms = [lax.dynamic_index_in_dim(parts, core, 3, False)]
+    for s in range(1, ncore):
+        chunk = lax.dynamic_index_in_dim(parts, (core + s) % ncore, 3, False)
+        terms.append(grid.send(chunk, (0, 0, 0, s)))
+    return terms
+
+
+def plane_terms(grid, layer):
+    nz, nx, ny, _ = grid.shape
+    _, x, y, _ = grid.own()
+    rows, width = layer.shape[3:]
+
+    def of(i, j):
+        return lax.dynamic_slice(layer, (0, i, j, 0, 0), (nz, 1, 1, rows, width))[:, 0, 0]
+
+    return [of(x, y)] + [
+        grid.send(of((x + i) % nx, (y + j) % ny), (0, i, j, 0)) for i, j in grid.plane()
+    ]
+
+
+def column_terms(grid, column):
+    nz = grid.shape[0]
+    z = grid.own()[0]
+    terms = [lax.dynamic_index_in_dim(column, z, 0, False)]
     for s in range(1, nz):
-        came = grid.send(part, (s, 0, 0, 0))
-        column = put(column, came[None], ((z - s) % nz, 0, 0))
-    layer = jnp.zeros((nz, nx, ny, rows, width), part.dtype)
-    layer = put(layer, column[:, None, None], (0, x, y, 0, 0))
-    for i, j in grid.plane():
-        came = grid.send(column, (0, i, j, 0))
-        layer = put(layer, came[:, None, None], (0, (x - i) % nx, (y - j) % ny, 0, 0))
-    full = jnp.zeros((nz, nx, ny, ncore, rows, width), part.dtype)
-    full = put(full, layer[:, :, :, None], (0, 0, 0, core, 0, 0))
-    for s in range(1, ncore):
-        came = grid.send(layer, (0, 0, 0, s))
-        full = put(full, came[:, :, :, None], (0, 0, 0, (core - s) % ncore, 0, 0))
-    return full.reshape(-1, width)
-
-
-def scatter_sums(grid, parts):
-    nz, nx, ny, ncore = grid.shape
-    z, x, y, core = grid.own()
-    rows, width = parts.shape[1:]
-    wide, low = jnp.float32, jnp.bfloat16
-    parts = parts.reshape(nz, nx, ny, ncore, rows, width)
-
-    def of_core(at):
-        return lax.dynamic_index_in_dim(parts, at, 3, False)
-
-    total = of_core(core).astype(wide)
-    for s in range(1, ncore):
-        total = total + grid.send(of_core((core + s) % ncore), (0, 0, 0, s)).astype(wide)
-    layer = total.astype(low)
-
-    def of_column(i, j):
-        return lax.dynamic_slice(layer, (0, i, j, 0, 0), (nz, 1, 1, rows, width))[:, 0, 0]
-
-    total = of_column(x, y).astype(wide)
-    for i, j in grid.plane():
-        total = total + grid.send(of_column((x + i) % nx, (y + j) % ny), (0, i, j, 0)).astype(wide)
-    column = total.astype(low)
-    total = lax.dynamic_index_in_dim(column, z, 0, False).astype(wide)
-    for s in range(1, nz):
-        came = grid.send(lax.dynamic_index_in_dim(column, (z + s) % nz, 0, False), (s, 0, 0, 0))
-        total = total + came.astype(wide)
-    return total
+        chunk = lax.dynamic_index_in_dim(column, (z + s) % nz, 0, False)
+        terms.append(grid.send(chunk, (s, 0, 0, 0)))
+    return terms
+
+
+def added(terms):
+    return functools.reduce(lambda a, b: a + b, [t.astype(jnp.float32) for t in terms])
+
+
+def added_low(terms):
+    return added(terms).astype(jnp.bfloat16)
+
+
+def after(first, *then):
+    return lax.optimization_barrier((first,) + then)
 
 
 def on_device(
@@ -527,13 +639,14 @@
     ff_blocks = up_weight.shape[1] // width
     low = jnp.bfloat16
 
+    taps, tap_rows = merging_weight.shape[:2]
+    down_rows = down_weight.shape[0]
     second_rows = jnp.concatenate(
         [
-            output_weight,
-            char_weight,
+            down_weight,
             merging_weight.reshape(-1, width),
             one_below_other(up_weight, ff_blocks),
-            down_weight,
+            char_weight,
         ],
         axis=0,
     )
@@ -553,8 +666,26 @@
         ],
         axis=1,
     )
-    project_full = gather_rows(grid, project_weight)
-    chars_all = gather_rows(grid, char_rows).reshape(devices, r, 3 * width)
+    char_rows = jnp.concatenate([char_rows, side_by_side(output_weight, 3)], axis=0)
+    project_came = column_sends(grid, project_weight)
+    project_came, char_rows = after(project_came, char_rows)
+    char_came = column_sends(grid, char_rows)
+    project_column = column_of(grid, project_weight, project_came)
+    project_came = plane_sends(grid, project_column)
+    project_came, char_came = after(project_came, char_came)
+    char_column = column_of(grid, char_rows, char_came)
+    char_came = plane_sends(grid, char_column)
+    project_layer = plane_of(grid, project_column, project_came)
+    project_full = cores_of(grid, project_layer, cores_sends(grid, project_layer))
+    states, codes = token_states[0], char_codes[0]
+    mixed = product(states, project_full).astype(low)
+    context_low, log_totals = attend(mixed, lengths, width)
+    char_came, context_low = after(char_came, context_low)
+    char_layer = plane_of(grid, char_column, char_came)
+    first_all = cores_of(grid, char_layer, cores_sends(grid, char_layer))
+    first_all = first_all.reshape(devices, -1, 3 * width)
+    output_full = whole(one_below_other(first_all[:, r:], 3))
+    chars_all = first_all[:, :r]
     inlet_full = whole(one_below_other(chars_all[:, :, :width], 3))
     recur_full = whole(one_below_other(chars_all[:, :, width : width + triple], 3))
     table_all = side_by_side(chars_all[:, :, width + triple :], 3)
@@ -563,29 +694,32 @@
     gains_all = gains_all.reshape(devices, 6, r).transpose(1, 0, 2).reshape(6, width)
     gains_all = gains_all.astype(jnp.float32)
 
-    at = 0
-    parts = []
-    for rows in (r, r) + (merging_weight.shape[1],) * 3 + (ff_blocks * r, down_weight.shape[0]):
-        parts.append(second_all[:, at : at + rows])
-        at += rows
-    output_full, branch_full = whole(parts[0]), whole(parts[1])
-    merging_full = [whole(part) for part in parts[2:5]]
-    upper_full = whole(side_by_side(parts[5], ff_blocks))
-    lower_full = whole(parts[6])
-
-    states, codes = token_states[0], char_codes[0]
+    def second(start, rows):
+        return second_all[:, start : start + rows]
+
+    up_start = down_rows + taps * tap_rows
+    upper_full = whole(side_by_side(second(up_start, ff_blocks * r), ff_blocks))
+    branch_full = whole(second(up_start + ff_blocks * r, r))
+
+    def rows_spec(start, rows):
+        if rows % 16 == 0 and start % rows == 0:
+            place = start // rows
+            return second_all, pl.BlockSpec(
+                (devices, rows, width), lambda b: (0, place, 0), pipeline_mode=pl.Buffered(1)
+            )
+        part = second(start, rows).reshape(ff_blocks, -1, width)
+        return part, pl.BlockSpec(part.shape, lambda b: (0, 0, 0), pipeline_mode=pl.Buffered(1))
+
     valid = lax.broadcasted_iota(jnp.int32, (length, 1), 0) < lengths
     embeds, chars_rep, char_states, coefs = chars_forward(
         codes, table_full, inlet_full, recur_full
     )
-    mixed = product(states, project_full).astype(low)
-    context_low, log_totals = attend(mixed, lengths, width)
     first_pre = states.astype(jnp.float32) + product(context_low, output_full)
-    first, pull_first = jax.vjp(norm_apply, first_pre, gains_all[0], gains_all[1])
+    first = norm_parts(first_pre)[0] * gains_all[0] + gains_all[1]
     joined = jnp.where(
         valid, jnp.concatenate([first.astype(low), chars_rep], axis=-1), jnp.zeros((), low)
     )
-    joined = jnp.concatenate([shift_down(joined), joined, shift_up(joined)], axis=1)
+    merging_parts = [rows_spec(down_rows + i * tap_rows, tap_rows) for i in range(taps)]
     (
         token_stream,
         char_stream,
@@ -606,39 +740,60 @@
         token_cotangent[0],
         char_cotangent[0],
         gains_all,
-        jnp.concatenate(merging_full, axis=0),
         upper_full,
-        lower_full,
         branch_full,
+        merging_parts,
+        rows_spec(0, down_rows),
     )
     feed_gain_grad, feed_shift_grad, char_gain_grad, char_shift_grad = jnp.sum(gain_sums, axis=1)
     early = jnp.concatenate(
-        [shares(outer_sum(merged_low, branch_grad), devices)]
+        [shares(outer_sum(hidden_low, feed_grad), devices)]
         + [
-            shares(outer_sum(joined[:, 2 * i * width : 2 * (i + 1) * width], merging_grad), devices)
-            for i in range(3)
-        ]
-        + [one_below_other(shares(outer_sum(summed_low, hidden_grad), devices), ff_blocks)]
-        + [shares(outer_sum(hidden_low, feed_grad), devices)],
+            shares(outer_sum(*pair), devices)
+            for pair in (
+                (joined[:-1], merging_grad[1:]),
+                (joined, merging_grad),
+                (joined[1:], merging_grad[:-1]),
+            )
+        ],
         axis=1,
     )
-    early, merging_grad = lax.optimization_barrier((early, merging_grad))
+    early, merging_grad, summed_low, merged_low = after(
+        early, merging_grad, summed_low, merged_low
+    )
     early = lax.psum_scatter(early, AXES, scatter_dimension=0, tiled=True)[0]
-    joined_grad = (
-        shift_up(back_product(merging_grad, merging_full[0]))
-        + back_product(merging_grad, merging_full[1])
-        + shift_down(back_product(merging_grad, merging_full[2]))
-    )
-    joined_grad = jnp.where(valid, joined_grad, 0.0)
-    first_grad = summed_grad + joined_grad[:, :width]
-    rep_grad = char_pre_grad + joined_grad[:, width:]
-    first_pre_grad, attend_gain_grad, attend_shift_grad = pull_first(first_grad)
-    table_grad, inlet_grad, recur_weight_grad = chars_back(
+    up_parts = jnp.concatenate(
+        [
+            shares(outer_sum(summed_low, hidden_grad), devices),
+            shares(outer_sum(merged_low, branch_grad), devices),
+        ],
+        axis=2,
+    )
+    up_parts, merging_grad = after(up_parts, merging_grad)
+    up_terms = core_terms(grid, up_parts)
+    first_pre_grad, attended_grad, context_grad, rep_grad, attend_sums = merging_back(
+        lengths,
+        merging_grad,
+        summed_grad,
+        char_pre_grad,
+        first_pre,
+        gains_all,
+        output_full,
+        merging_parts,
+    )
+    up_terms, rep_grad, context_grad, attended_grad = after(
+        up_terms, rep_grad, context_grad, attended_grad
+    )
+    attend_gain_grad, attend_shift_grad = jnp.sum(attend_sums, axis=1)
+    up_layer, rep_grad = after(added_low(up_terms), rep_grad)
+    up_terms = plane_terms(grid, up_layer)
+    char_grads = chars_back(
         codes, inlet_full, recur_full, embeds, char_states, coefs, rep_grad, table_full.shape[1]
     )
-    attended_grad = first_pre_grad.astype(low)
+    up_terms, char_grads, context_grad = after(up_terms, char_grads, context_grad)
+    table_grad, inlet_grad, recur_weight_grad = char_grads
+    up_column = added_low(up_terms)
     output_weight_grad = outer_sum(context_low, attended_grad)
-    context_grad = back_product(attended_grad, output_full).astype(low)
     gain_grads = jnp.stack(
         [
             attend_gain_grad,
@@ -672,21 +827,39 @@
         ],
         axis=1,
     )
-    late, context_grad = lax.optimization_barrier((late, context_grad))
-    late = scatter_sums(grid, late)
-    head_grads = attend_back(mixed, context_grad, context_low, log_totals, lengths, width)
-    mixed_grad = jnp.concatenate([head_grads[0], head_grads[1], head_grads[2]], axis=-1)
-    own_project = scatter_sums(grid, shares(outer_sum(states, mixed_grad), devices))
+    def back(start, pairs, context_grad, earlier):
+        return attend_back(
+            mixed, context_grad, context_low, log_totals, lengths, width, start, pairs, earlier
+        )
+
+    every = width // LANES
+    cuts = (0, every // 6, 5 * every // 6, every)
+    up_column, late, context_grad = after(up_column, late, context_grad)
+    up_terms = column_terms(grid, up_column)
+    late_terms = core_terms(grid, late)
+    grads = back(cuts[0], cuts[1] - cuts[0], context_grad, ())
+    late_terms, grads, context_grad = after(late_terms, grads, context_grad)
+    late_layer, context_grad = after(added_low(late_terms), context_grad)
+    late_terms = plane_terms(grid, late_layer)
+    grads = back(cuts[1], cuts[2] - cuts[1], context_grad, grads)
+    late_terms, up_terms, grads, context_grad = after(late_terms, up_terms, grads, context_grad)
+    late_column, context_grad = after(added_low(late_terms), context_grad)
+    late_terms = column_terms(grid, late_column)
+    grads = back(cuts[2], cuts[3] - cuts[2], context_grad, grads)
+    mixed_grad = jnp.concatenate(grads, axis=-1)
+    project_parts = shares(outer_sum(states, mixed_grad), devices)
+    project_parts, late_terms = after(project_parts, late_terms)
+    up_own, late = added(up_terms), added(late_terms)
+    project_terms = core_terms(grid, project_parts)
+    project_terms, early = after(project_terms, early)
+    project_layer = added_low(project_terms)
+    project_column = added_low(plane_terms(grid, project_layer))
+    own_project = added(column_terms(grid, project_column))
     input_gradient = (first_pre_grad + back_product(mixed_grad, project_full)).astype(low)
     early = early.astype(jnp.float32)
     own_chars = late[:r]
     own_table_rows = side_by_side(own_chars[:, width + triple :], 3)
     own_gains = own_table_rows[0, letters_count : letters_count + 6 * r].reshape(6, r)
-    spots = []
-    at = 0
-    for rows in (r, 3 * merging_weight.shape[1], ff_blocks * r, down_weight.shape[0]):
-        spots.append(early[at : at + rows])
-        at += rows
     return (
         token_stream[None],
         char_stream[None],
@@ -696,10 +869,10 @@
         one_below_other(own_chars[:, width : width + triple], 3).T,
         own_project,
         one_below_other(late[r:], 3),
-        spots[1].reshape(merging_weight.shape),
-        side_by_side(spots[2], ff_blocks),
-        spots[3],
-        spots[0],
+        early[down_rows:].reshape(merging_weight.shape),
+        up_own[:, : ff_blocks * width],
+        early[:down_rows],
+        up_own[:, ff_blocks * width :],
         own_gains[0],
         own_gains[1],
         own_gains[2],

time: 539 us -> 498 us (0.924)
  waiting for transfers between devices: 110 us -> 67.9 us
  Pallas kernels: 179 us -> 199 us
  local copies, waits for them, and re-layouts: 85.4 us -> 73.1 us
  matrix products: 62.5 us -> 55.3 us
    ppermute x28 -> x35, waiting for transfers between devices: 90.5 us -> 48.4 us  [send(): return lax.ppermute(values, AXES, pairs)]
    dot_general x5 -> x1, matrix products: 24.7 us -> 6.49 us  [back_product(): jnp.einsum('lo,io->li', grad_rows, weight, preferred_element_type=jnp.flo...]
    pallas_call x0 -> x1, Pallas kernels: none -> 16.5 us  [merging_back(): pl.pallas_call(merging_back_kernel, grid=(length // rows,), in_specs=[pl....]
    slice x10 -> x8, local copies, waits for them, and re-layouts: 23.2 us -> 7.15 us  [the longest x1 4.1 us: second(): return second_all[:, start:start + rows]]
    dot_general x8, matrix products: 30.8 us -> 41.8 us  [outer_sum(): jnp.einsum('li,lo->io', left, right, preferred_element_type=jnp.float32)]
    squeeze x6 -> x8, local copies, waits for them, and re-layouts: 4.74 us -> 13.1 us  [the longest x2 8.11 us: core_terms(): chunk = lax.dynamic_index_in_dim(parts, (core + s) % ncore, 3, False)]
    unnamed x127 -> x102, local copies, waits for them, and re-layouts: 33 us -> 25.4 us
    dynamic_update_slice x20, local copies, waits for them, and re-layouts: 7.31 us -> 13.9 us  [the longest x8 7.86 us: plane_of(): lax.dynamic_update_slice(layer, piece[:, None, None], (0, (x - i) % nx, (...]
  transfers between devices with their start and end apart: 30 -> 37, of which waited for: 12 -> 12; matrix products, arithmetic and copies ran while one was open for 18% -> 21% of each run, Pallas kernels for 24% -> 30%
where the time goes in v4:
time: 498 us; the launch traced here: 492 us
  Pallas kernels  199 us (40%)
  local copies, waits for them, and re-layouts  73.1 us (15%)
  waiting for transfers between devices  67.9 us (14%)
  matrix products  55.3 us (11%)
  starting transfers between devices  40.5 us (8%)
  other arithmetic  40.1 us (8%)
  between operations  16.2 us (3%)
    pallas_call x1, Pallas kernels, feed(): pl.pallas_call(functools.partial(feed_kernel, blocks), grid=(length // ro...  51.9 us
    ppermute x35, waiting for transfers between devices, send(): return lax.ppermute(values, AXES, pairs)  48.4 us
    dot_general x8, matrix products, outer_sum(): jnp.einsum('li,lo->io', left, right, preferred_element_type=jnp.float32)  41.8 us
    pallas_call x1, Pallas kernels, chars_back(): pl.pallas_call(functools.partial(chars_back_kernel, half), grid=(length /...  41.1 us
    pallas_call x3, Pallas kernels, attend_back(): pl.pallas_call(functools.partial(back_kernel, rows), grid=(pairs,), in_sp...  40.9 us
    ppermute x35, starting transfers between devices, send(): return lax.ppermute(values, AXES, pairs)  40.4 us
    pallas_call x1, Pallas kernels, chars_forward(): pl.pallas_call(functools.partial(chars_kernel, half), grid=(length // row...  26.6 us
    unnamed x102, local copies, waits for them, and re-layouts  25.4 us
  transfers between devices with their start and end apart: 37, of which 12 were waited for; matrix products, arithmetic and copies ran while one was open for 21% of the time, Pallas kernels for 30%

profile of v4, /device:TPU:0, one launch (start us, length us, event | category | flops | bytes accessed | tf_op | source)
XLA Modules:
  0.0 491.6 jit_solution(761717438225858356)
XLA Ops:
  35.6 4.5 collective-permute-done.8
  43.1 12.6 %collective-permute-done.7 = bf16[32,2304]{1,0:T(8,128)(2,1)S(1)} collective-permute-done((bf16[32,2304]{1,0:T(8,128)(2,1)S(1)}, bf16[32,2304]{1,0:T(8,128)(2,1)S(1)}, u32[]{:S(2)}, u32[]{:S(2)}) %collective-permute-start.7) | collective-permute-done | bytes 147488 | tf_op jit(solution)/shard_map/ppermute | solution.py:513
  67.5 5.5 %fusion.q_ref.k_ref.v_ref = bf16[1024,2304]{1,0:T(8,128)(2,1)} fusion(bf16[768,2304]{1,0:T(8,128)(2,1)S(1)} %bitcast.231, bf16[1,1024,768]{2,1,0:T(8,128)(2,1)S(1)} %copy-done.26), kind=kOutput, calls=%fused_computation.7 | convolution fusion | flops 3626237952 | bytes 9830400 | tf_op jit(solution)/shard_map/dot_general | solution.py:24
  73.0 21.5 %shard_map.331 = (bf16[1024,768]{1,0:T(8,128)(2,1)}, f32[1024,768]{1,0:T(8,128)}) custom-call(s32[1]{0:T(128)} %copy.177.length_ref, bf16[1024,2304]{1,0:T(8,128)(2,1)} %fusion.q_ref.k_ref.v_ref, bf16[1024,2304]{1,0:T(8,128)(2,1)} %fusion.q_ref.k_ref.v_ref, bf16[1024,2304]{1,0:T(8,128)(2,1)} %fusion.q_ref.k_ref.v_ref), custom_call_target="tpu_custom_call" | custom-call | flops 199999995904 | bytes 1000000 | tf_op jit(solution)/shard_map/pallas_call | solution.py:73
  94.6 8.8 %collective-permute-done.10 = bf16[4,32,2304]{2,1,0:T(8,128)(2,1)} collective-permute-done((bf16[4,32,2304]{2,1,0:T(8,128)(2,1)}, bf16[4,32,2304]{2,1,0:T(8,128)(2,1)}, u32[]{:S(2)}, u32[]{:S(2)}) %collective-permute-start.10) | collective-permute-done | bytes 589856 | tf_op jit(solution)/shard_map/ppermute | solution.py:513
  131.0 26.6 %shard_map.332 = (bf16[1024,1024]{1,0:T(8,128)(2,1)}, bf16[1024,768]{1,0:T(8,128)(2,1)}, bf16[2,3,1024,384]{3,2,1,0:T(8,128)(2,1)}, bf16[2,17,1024,384]{3,2,1,0:T(8,128)(2,1)}) custom-call(s32[1024,4]{1,0:T(8,128)} %bitcast.264, bf16[256,1024]{1,0:T(8,128)(2,1)} %fusion.13.table_ref, bf16[2304,256]{1,0:T(8,128)(2,1)} %bitcast.259, bf16[2304,384]{1,0:T(8,128)(2,1)} %bitcast.244), custom_call_target="tpu_custom_call" | custom-call | flops 199999995904 | bytes 1000000 | tf_op jit(solution)/shard_map/pallas_call | solution.py:222
  160.9 6.0 %all-gather.3.cloned.1.call-done = bf16[11520,768]{1,0:T(8,128)(2,1)} async-done(((bf16[360,768]{1,0:T(8,128)(2,1)}), bf16[11520,768]{1,0:T(8,128)(2,1)}) %all-gather.3.cloned.1.call-update) | async-done | bytes 17694736 | tf_op jit(solution)/shard_map/all_gather | solution.py:653
  166.9 4.1 fusion.20
  173.4 51.9 %shard_map.333 = (bf16[1024,768]{1,0:T(8,128)(2,1)}, bf16[1024,768]{1,0:T(8,128)(2,1)}, bf16[1024,768]{1,0:T(8,128)(2,1)}, bf16[1024,768]{1,0:T(8,128)(2,1)}, bf...) custom-call(bf16[1024,1536]{1,0:T(8,128)(2,1)} %maximum_select_fusio, ...), custom_call_target="tpu_custom_call" | custom-call | flops 199999995904 | bytes 1000000 | tf_op jit(solution)/shard_map/pallas_call | solution.py:409
  225.3 4.5 convolution_convert_fusion.4
  229.8 13.3 %convolution_convert_fusion.5 = bf16[1536,768]{1,0:T(8,128)(2,1)S(1)} fusion(bf16[1024,1536]{1,0:T(8,128)(2,1)S(1)} %copy-done.7, bf16[1024,768]{1,0:T(8,128)(2,1)S(1)} %copy-done.35), kind=kOutput, calls=%fused_computation.13 | convolution fusion | flops 2417098752 | bytes 7077888 | tf_op jit(solution)/shard_map/li,lo->io/dot_general | solution.py:28
  246.2 5.5 %convolution_convert_fusion.2 = bf16[3072,768]{1,0:T(8,128)(2,1)S(1)} fusion(bf16[1024,3072]{1,0:T(8,128)(2,1)S(1)} %bitcast.291, bf16[1024,768]{1,0:T(8,128)(2,1)S(1)} %copy-done.36), kind=kOutput, calls=%fused_computation.5 | convolution fusion | flops 4834197504 | bytes 12582912 | tf_op jit(solution)/shard_map/li,lo->io/dot_general | solution.py:28
  251.8 5.4 %pad_maximum_fusion = bf16[32,240,768]{2,1,0:T(8,128)(2,1)} fusion(bf16[32,48,768]{2,1,0:T(8,128)(2,1)S(1)} %bitcast.233, bf16[32,48,768]{2,1,0:T(8,128)(2,1)S(1)} %bitcast.234, bf16[32,48,768]{2,1,0:T(8,128)(2,1)S(1)} %bitcast.235, bf16[32,96,768]{2,1,0:T(8,128)(2,1)S(1)} %bitcast.228), kind=kLoop, calls=%fused_computation | loop fusion | flops 47185920 | bytes 23592960 | tf_op jit(solution)/shard_map/concatenate | solution.py:749
  258.6 8.2 %convolution_convert_fusion.1 = bf16[768,3072]{1,0:T(8,128)(2,1)S(1)} fusion(bf16[1024,768]{1,0:T(8,128)(2,1)S(1)} %copy-done.34, bf16[1024,3072]{1,0:T(8,128)(2,1)} %get-tuple-element.145), kind=kOutput, calls=%fused_computation.4 | convolution fusion | flops 4834197504 | bytes 12582912 | tf_op jit(solution)/shard_map/li,lo->io/dot_general | solution.py:28
  269.7 5.7 %dynamic-slice_bitcast_fusion = (bf16[4,2,2,24,3840]{4,3,2,1,0:T(8,128)(2,1)}, bf16[4,2,2,24,3840]{4,3,2,1,0:T(8,128)(2,1)}) fusion(bf16[4,2,2,2,24,3840]{5,4,3,2,1,0:T(8,128)(2,1)} %bitcast.219, s32[]{:T(128)S(6)} %select_n.337, s32[]{:T(128)S(6)} %select_n.335), kind=kLoop, calls=%fused_computation.22 | loop fusion | bytes 11796488 | tf_op jit(solution)/shard_map/jit(dynamic_index_in_dim)/squeeze | solution.py:569
  275.6 16.5 %shard_map.334 = (f32[1024,768]{1,0:T(8,128)}, bf16[1024,768]{1,0:T(8,128)(2,1)}, bf16[1024,768]{1,0:T(8,128)(2,1)}, f32[1024,768]{1,0:T(8,128)}, f32[2,8,768]{2,1,0:T(8,128)}) custom-call(s32[1]{0:T(128)} %copy.177.length_ref, bf16[1024,768]{1,0:T(8,128)(2,1)} %get-tuple-element.149.grad_ref, f32[1024,768]{1,0:T(8,128)} %get-tuple-element.150.summed_ref, ...), custom_call_target="tpu_custom_call" | custom-call | flops 199999995904 | bytes 1000000 | tf_op jit(solution)/shard_map/pallas_call | solution.py:456
  302.8 41.1 %shard_map.335 = (bf16[256,1024]{1,0:T(8,128)(2,1)}, bf16[2304,256]{1,0:T(8,128)(2,1)}, bf16[2304,384]{1,0:T(8,128)(2,1)}) custom-call(s32[1024,4]{1,0:T(8,128)} %bitcast.265, bf16[2304,256]{1,0:T(8,128)(2,1)} %bitcast.260, bf16[2304,384]{1,0:T(8,128)(2,1)} %bitcast.245, bf16[1024,1024]{1,0:T(8,128)(2,1)} %get-tuple-element.161.embed_ref, ...), custom_call_target="tpu_custom_call" | custom-call | flops 199999995904 | bytes 1000000 | tf_op jit(solution)/shard_map/pallas_call | solution.py:298
  358.2 8.1 %shard_map.336 = (bf16[1024,768]{1,0:T(8,128)(2,1)}, bf16[1024,768]{1,0:T(8,128)(2,1)}, bf16[1024,768]{1,0:T(8,128)(2,1)}) custom-call(s32[1]{0:T(128)} %copy.177.length_ref, bf16[1024,2304]{1,0:T(8,128)(2,1)} %fusion.q_ref.k_ref.v_ref, bf16[1024,2304]{1,0:T(8,128)(2,1)} %fusion.q_ref.k_ref.v_ref, bf16[1024,2304]{1,0:T(8,128)(2,1)} %fusion.q_ref.k_ref.v_ref, ...), custom_call_target="tpu_custom_call" | custom-call | flops 199999995904 | bytes 1000000 | tf_op jit(solution)/shard_map/pallas_call | solution.py:130
  373.7 25.1 %shard_map.337 = (bf16[1024,768]{1,0:T(8,128)(2,1)}, bf16[1024,768]{1,0:T(8,128)(2,1)}, bf16[1024,768]{1,0:T(8,128)(2,1)}) custom-call(s32[1]{0:T(128)} %copy.177.length_ref, bf16[1024,2304]{1,0:T(8,128)(2,1)} %fusion.q_ref.k_ref.v_ref, bf16[1024,2304]{1,0:T(8,128)(2,1)} %fusion.q_ref.k_ref.v_ref, ...), custom_call_target="tpu_custom_call", output_to_operand_aliasing={{0}: (7, {}), {1}: (8, {}), {2}: (9, {})} | custom-call | flops 199999995904 | bytes 1000000 | tf_op jit(solution)/shard_map/pallas_call | solution.py:130
  406.0 7.8 %shard_map.338 = (bf16[1024,768]{1,0:T(8,128)(2,1)}, bf16[1024,768]{1,0:T(8,128)(2,1)}, bf16[1024,768]{1,0:T(8,128)(2,1)}) custom-call(s32[1]{0:T(128)} %copy.177.length_ref, bf16[1024,2304]{1,0:T(8,128)(2,1)} %fusion.q_ref.k_ref.v_ref, bf16[1024,2304]{1,0:T(8,128)(2,1)} %fusion.q_ref.k_ref.v_ref, ...), custom_call_target="tpu_custom_call", output_to_operand_aliasing={{0}: (7, {}), {1}: (8, {}), {2}: (9, {})} | custom-call | flops 199999995904 | bytes 1000000 | tf_op jit(solution)/shard_map/pallas_call | solution.py:130
  418.0 6.5 %fusion.7 = bf16[1,1024,768]{2,1,0:T(8,128)(2,1)} fusion(f32[1024,768]{1,0:T(8,128)} %get-tuple-element.152, bf16[1024,2304]{1,0:T(8,128)(2,1)S(1)} %constant_dynamic-update-slice_fusion.14, bf16[768,2304]{1,0:T(8,128)(2,1)S(1)} %bitcast.232), kind=kOutput, calls=%fused_computation.39 | convolution fusion | flops 3625451520 | bytes 12976128 | tf_op jit(solution)/shard_map/lo,io->li/dot_general | solution.py:32
  424.5 4.5 convolution_convert_fusion.3
  437.5 13.5 %reduce-scatter.2.cloned.1.call-done = bf16[1,240,768]{2,1,0:T(8,128)(2,1)} async-done(((bf16[32,240,768]{2,1,0:T(8,128)(2,1)}), bf16[1,240,768]{2,1,0:T(8,128)(2,1)}) %reduce-scatter.2.cloned.1.call-update) | async-done | bytes 368656 | tf_op jit(solution)/shard_map/reduce_scatter | solution.py:764
  457.3 14.0 %collective-permute-done.29 = bf16[4,24,2304]{2,1,0:T(8,128)(2,1)S(1)} collective-permute-done((bf16[4,24,2304]{2,1,0:T(8,128)(2,1)S(1)}, bf16[4,24,2304]{2,1,0:T(8,128)(2,1)S(1)}, u32[]{:S(2)}, u32[]{:S(2)}) %collective-permute-start.29) | collective-permute-done | bytes 442400 | tf_op jit(solution)/shard_map/ppermute | solution.py:513
  (279 shorter events, 154.4 us)
Async XLA Ops:
  7.2 159.7 %all-gather.3.cloned.1.call-start = ((), (), s32[]{:S(2)}) async-start(), calls=%async_computation.2 | async-start | bytes 18247680 | tf_op jit(solution)/shard_map/all_gather | solution.py:653
  7.2 23.0 %collective-permute-start.1 = (bf16[24,2304]{1,0:T(8,128)(2,1)}, bf16[24,2304]{1,0:T(8,128)(2,1)S(1)}, u32[]{:S(2)}, u32[]{:S(2)}) collective-permute-start(bf16[24,2304]{1,0:T(8,128)(2,1)} %param.28), channel_id=1, source_target_pairs={{0,16},{1,17},{2,18},{3,19},{4,20},{5,21},{6,22},{7,23},{8,24},{9,... | collective-permute-start | bytes 331784 | tf_op jit(solution)/shard_map/ppermute | solution.py:513
  11.3 18.9 %collective-permute-start = (bf16[24,2304]{1,0:T(8,128)(2,1)}, bf16[24,2304]{1,0:T(8,128)(2,1)S(1)}, u32[]{:S(2)}, u32[]{:S(2)}) collective-permute-start(bf16[24,2304]{1,0:T(8,128)(2,1)} %param.28), channel_id=1, source_target_pairs={{0,8},{1,9},{2,10},{3,11},{4,12},{5,13},{6,14},{7,15},{8,16},{9,17... | collective-permute-start | bytes 331784 | tf_op jit(solution)/shard_map/ppermute | solution.py:513
  21.7 429.3 %reduce-scatter.2.cloned.1.call-start = ((), (), s32[]{:S(2)}) async-start(), calls=%async_computation.1 | async-start | bytes 12165120 | tf_op jit(solution)/shard_map/reduce_scatter | solution.py:764
  30.3 25.4 %collective-permute-start.7 = (bf16[32,2304]{1,0:T(8,128)(2,1)S(1)}, bf16[32,2304]{1,0:T(8,128)(2,1)S(1)}, u32[]{:S(2)}, u32[]{:S(2)}) collective-permute-start(bf16[32,2304]{1,0:T(8,128)(2,1)S(1)} %maximum_maximum_fusion.1), channel_id=1, source_target_pairs={{0,16},{1,17},{2,18},{3,19},{4,20},{5,21},{6,22},{7,23},{8,24},{9,... | collective-permute-start | bytes 442376 | tf_op jit(solution)/shard_map/ppermute | solution.py:513
  31.5 24.2 %collective-permute-start.6 = (bf16[32,2304]{1,0:T(8,128)(2,1)S(1)}, bf16[32,2304]{1,0:T(8,128)(2,1)S(1)}, u32[]{:S(2)}, u32[]{:S(2)}) collective-permute-start(bf16[32,2304]{1,0:T(8,128)(2,1)S(1)} %maximum_maximum_fusion.1), channel_id=1, source_target_pairs={{0,8},{1,9},{2,10},{3,11},{4,12},{5,13},{6,14},{7,15},{8,16},{9,17... | collective-permute-start | bytes 442376 | tf_op jit(solution)/shard_map/ppermute | solution.py:513
  32.4 23.4 %collective-permute-start.5 = (bf16[4,24,2304]{2,1,0:T(8,128)(2,1)S(1)}, bf16[4,24,2304]{2,1,0:T(8,128)(2,1)S(1)}, u32[]{:S(2)}, u32[]{:S(2)}) collective-permute-start(bf16[4,24,2304]{2,1,0:T(8,128)(2,1)S(1)} %bitcast_dynamic-update-slice_fusion.16), channel_id=1, source_target_pairs={{0,6},{1,7},{2,4},{3,5},{4,2},{5,3},{6,0},{7,1},{8,14},{9,15},{10,... | collective-permute-start | bytes 1327112 | tf_op jit(solution)/shard_map/ppermute | solution.py:513
  34.9 20.8 %collective-permute-start.4 = (bf16[4,24,2304]{2,1,0:T(8,128)(2,1)S(1)}, bf16[4,24,2304]{2,1,0:T(8,128)(2,1)S(1)}, u32[]{:S(2)}, u32[]{:S(2)}) collective-permute-start(bf16[4,24,2304]{2,1,0:T(8,128)(2,1)S(1)} %bitcast_dynamic-update-slice_fusion.16), channel_id=1, source_target_pairs={{0,4},{1,5},{2,6},{3,7},{4,0},{5,1},{6,2},{7,3},{8,12},{9,13},{10,... | collective-permute-start | bytes 1327112 | tf_op jit(solution)/shard_map/ppermute | solution.py:513
  58.0 36.6 %collective-permute-start.11 = (bf16[4,32,2304]{2,1,0:T(8,128)(2,1)}, bf16[4,32,2304]{2,1,0:T(8,128)(2,1)}, u32[]{:S(2)}, u32[]{:S(2)}) collective-permute-start(bf16[4,32,2304]{2,1,0:T(8,128)(2,1)} %bitcast_dynamic-update-slice_fusion.12), channel_id=1, source_target_pairs={{0,6},{1,7},{2,4},{3,5},{4,2},{5,3},{6,0},{7,1},{8,14},{9,15},{10,... | collective-permute-start | bytes 1769480 | tf_op jit(solution)/shard_map/ppermute | solution.py:513
  60.4 43.0 %collective-permute-start.10 = (bf16[4,32,2304]{2,1,0:T(8,128)(2,1)}, bf16[4,32,2304]{2,1,0:T(8,128)(2,1)}, u32[]{:S(2)}, u32[]{:S(2)}) collective-permute-start(bf16[4,32,2304]{2,1,0:T(8,128)(2,1)} %bitcast_dynamic-update-slice_fusion.12), channel_id=1, source_target_pairs={{0,4},{1,5},{2,6},{3,7},{4,0},{5,1},{6,2},{7,3},{8,12},{9,13},{10,... | collective-permute-start | bytes 1769480 | tf_op jit(solution)/shard_map/ppermute | solution.py:513
  60.9 42.5 %collective-permute-start.9 = (bf16[4,32,2304]{2,1,0:T(8,128)(2,1)}, bf16[4,32,2304]{2,1,0:T(8,128)(2,1)}, u32[]{:S(2)}, u32[]{:S(2)}) collective-permute-start(bf16[4,32,2304]{2,1,0:T(8,128)(2,1)} %bitcast_dynamic-update-slice_fusion.12), channel_id=1, source_target_pairs={{0,2},{1,3},{2,0},{3,1},{4,6},{5,7},{6,4},{7,5},{8,10},{9,11},{10,... | collective-permute-start | bytes 1769480 | tf_op jit(solution)/shard_map/ppermute | solution.py:513
  299.3 46.2 %collective-permute-start.17 = (bf16[4,24,3840]{2,1,0:T(8,128)(2,1)}, bf16[4,24,3840]{2,1,0:T(8,128)(2,1)}, u32[]{:S(2)}, u32[]{:S(2)}) collective-permute-start(bf16[4,24,3840]{2,1,0:T(8,128)(2,1)} %get-tuple-element.249), channel_id=1, source_target_pairs={{0,6},{1,7},{2,4},{3,5},{4,2},{5,3},{6,0},{7,1},{8,14},{9,15},{10,... | collective-permute-start | bytes 2211848 | tf_op jit(solution)/shard_map/ppermute | solution.py:513
  301.0 44.6 %collective-permute-start.16 = (bf16[4,24,3840]{2,1,0:T(8,128)(2,1)}, bf16[4,24,3840]{2,1,0:T(8,128)(2,1)}, u32[]{:S(2)}, u32[]{:S(2)}) collective-permute-start(bf16[4,24,3840]{2,1,0:T(8,128)(2,1)} %get-tuple-element.250), channel_id=1, source_target_pairs={{0,4},{1,5},{2,6},{3,7},{4,0},{5,1},{6,2},{7,3},{8,12},{9,13},{10,... | collective-permute-start | bytes 2211848 | tf_op jit(solution)/shard_map/ppermute | solution.py:513
  302.4 43.1 %collective-permute-start.15 = (bf16[4,24,3840]{2,1,0:T(8,128)(2,1)}, bf16[4,24,3840]{2,1,0:T(8,128)(2,1)}, u32[]{:S(2)}, u32[]{:S(2)}) collective-permute-start(bf16[4,24,3840]{2,1,0:T(8,128)(2,1)} %get-tuple-element.251), channel_id=1, source_target_pairs={{0,2},{1,3},{2,0},{3,1},{4,6},{5,7},{6,4},{7,5},{8,10},{9,11},{10,... | collective-permute-start | bytes 2211848 | tf_op jit(solution)/shard_map/ppermute | solution.py:513
  354.4 18.8 %collective-permute-start.24 = (bf16[24,3840]{1,0:T(8,128)(2,1)}, bf16[24,3840]{1,0:T(8,128)(2,1)}, u32[]{:S(2)}, u32[]{:S(2)}) collective-permute-start(bf16[24,3840]{1,0:T(8,128)(2,1)} %get-tuple-element.263), channel_id=1, source_target_pairs={{0,24},{1,25},{2,26},{3,27},{4,28},{5,29},{6,30},{7,31},{8,0},{9,1... | collective-permute-start | bytes 552968 | tf_op jit(solution)/shard_map/ppermute | solution.py:513
  355.7 43.0 %collective-permute-start.23 = (bf16[24,3840]{1,0:T(8,128)(2,1)}, bf16[24,3840]{1,0:T(8,128)(2,1)}, u32[]{:S(2)}, u32[]{:S(2)}) collective-permute-start(bf16[24,3840]{1,0:T(8,128)(2,1)} %get-tuple-element.264), channel_id=1, source_target_pairs={{0,16},{1,17},{2,18},{3,19},{4,20},{5,21},{6,22},{7,23},{8,24},{9,... | collective-permute-start | bytes 552968 | tf_op jit(solution)/shard_map/ppermute | solution.py:513
  356.0 42.7 %collective-permute-start.22 = (bf16[24,3840]{1,0:T(8,128)(2,1)}, bf16[24,3840]{1,0:T(8,128)(2,1)}, u32[]{:S(2)}, u32[]{:S(2)}) collective-permute-start(bf16[24,3840]{1,0:T(8,128)(2,1)} %get-tuple-element.265), channel_id=1, source_target_pairs={{0,8},{1,9},{2,10},{3,11},{4,12},{5,13},{6,14},{7,15},{8,16},{9,17... | collective-permute-start | bytes 552968 | tf_op jit(solution)/shard_map/ppermute | solution.py:513
  370.2 28.6 %collective-permute-start.21 = (bf16[4,32,2304]{2,1,0:T(8,128)(2,1)}, bf16[4,32,2304]{2,1,0:T(8,128)(2,1)}, u32[]{:S(2)}, u32[]{:S(2)}) collective-permute-start(bf16[4,32,2304]{2,1,0:T(8,128)(2,1)} %get-tuple-element.253), channel_id=1, source_target_pairs={{0,6},{1,7},{2,4},{3,5},{4,2},{5,3},{6,0},{7,1},{8,14},{9,15},{10,... | collective-permute-start | bytes 1769480 | tf_op jit(solution)/shard_map/ppermute | solution.py:513
  371.5 28.1 %collective-permute-start.20 = (bf16[4,32,2304]{2,1,0:T(8,128)(2,1)}, bf16[4,32,2304]{2,1,0:T(8,128)(2,1)}, u32[]{:S(2)}, u32[]{:S(2)}) collective-permute-start(bf16[4,32,2304]{2,1,0:T(8,128)(2,1)} %get-tuple-element.254), channel_id=1, source_target_pairs={{0,4},{1,5},{2,6},{3,7},{4,0},{5,1},{6,2},{7,3},{8,12},{9,13},{10,... | collective-permute-start | bytes 1769480 | tf_op jit(solution)/shard_map/ppermute | solution.py:513
  373.1 26.5 %collective-permute-start.19 = (bf16[4,32,2304]{2,1,0:T(8,128)(2,1)}, bf16[4,32,2304]{2,1,0:T(8,128)(2,1)}, u32[]{:S(2)}, u32[]{:S(2)}) collective-permute-start(bf16[4,32,2304]{2,1,0:T(8,128)(2,1)} %get-tuple-element.255), channel_id=1, source_target_pairs={{0,2},{1,3},{2,0},{3,1},{4,6},{5,7},{6,4},{7,5},{8,10},{9,11},{10,... | collective-permute-start | bytes 1769480 | tf_op jit(solution)/shard_map/ppermute | solution.py:513
  402.3 26.7 %collective-permute-start.27 = (bf16[32,2304]{1,0:T(8,128)(2,1)}, bf16[32,2304]{1,0:T(8,128)(2,1)}, u32[]{:S(2)}, u32[]{:S(2)}) collective-permute-start(bf16[32,2304]{1,0:T(8,128)(2,1)} %get-tuple-element.267), channel_id=1, source_target_pairs={{0,24},{1,25},{2,26},{3,27},{4,28},{5,29},{6,30},{7,31},{8,0},{9,1... | collective-permute-start | bytes 442376 | tf_op jit(solution)/shard_map/ppermute | solution.py:513
  404.3 26.1 %collective-permute-start.26 = (bf16[32,2304]{1,0:T(8,128)(2,1)}, bf16[32,2304]{1,0:T(8,128)(2,1)}, u32[]{:S(2)}, u32[]{:S(2)}) collective-permute-start(bf16[32,2304]{1,0:T(8,128)(2,1)} %get-tuple-element.268), channel_id=1, source_target_pairs={{0,16},{1,17},{2,18},{3,19},{4,20},{5,21},{6,22},{7,23},{8,24},{9,... | collective-permute-start | bytes 442376 | tf_op jit(solution)/shard_map/ppermute | solution.py:513
  405.4 25.0 %collective-permute-start.25 = (bf16[32,2304]{1,0:T(8,128)(2,1)}, bf16[32,2304]{1,0:T(8,128)(2,1)}, u32[]{:S(2)}, u32[]{:S(2)}) collective-permute-start(bf16[32,2304]{1,0:T(8,128)(2,1)} %get-tuple-element.269), channel_id=1, source_target_pairs={{0,8},{1,9},{2,10},{3,11},{4,12},{5,13},{6,14},{7,15},{8,16},{9,17... | collective-permute-start | bytes 442376 | tf_op jit(solution)/shard_map/ppermute | solution.py:513
  451.6 19.8 %collective-permute-start.29 = (bf16[4,24,2304]{2,1,0:T(8,128)(2,1)S(1)}, bf16[4,24,2304]{2,1,0:T(8,128)(2,1)S(1)}, u32[]{:S(2)}, u32[]{:S(2)}) collective-permute-start(bf16[4,24,2304]{2,1,0:T(8,128)(2,1)S(1)} %get-tuple-element.257), channel_id=1, source_target_pairs={{0,2},{1,3},{2,0},{3,1},{4,6},{5,7},{6,4},{7,5},{8,10},{9,11},{10,... | collective-permute-start | bytes 1327112 | tf_op jit(solution)/shard_map/ppermute | solution.py:513
  (52 other events, 529.7 us)
Sparse Core Ops, SparseCore 0:
  21.9 145.0 all-gather.2
  269.8 181.2 reduce-scatter.1
